TPU v7x, 128 devices: a whole 4x4x4 slice. The times are simulated.
128 devices in a mesh: shard: 4 (over x), context: 4 (over z), tensor: 8 (over y, core).
Axes of the slice: x: 4, y: 4, z: 4, core: 2. Of those that a mesh axis runs over, the one named last changes fastest.
Arguments:
- hidden: bfloat16 [32768, 768], P(('shard', 'context')), may hold values from -6 to 6
- cotangent: bfloat16 [32768, 768], P(('shard', 'context')), may hold values from -6 to 6
- lengths: int32 [4, 4], P('shard'), may hold values from 1 to 8189, as said below
- norm_gain: float32 [768], replicated, may hold values from 0.5 to 1.5
- gate_proj: bfloat16 [768, 1536], P(('shard', 'context'), 'tensor'), may hold values from -0.21875 to 0.21875
- value_proj: bfloat16 [768, 1536], P(('shard', 'context'), 'tensor'), may hold values from -0.21875 to 0.21875
- state_proj: bfloat16 [768, 256], P(('shard', 'context'), 'tensor'), may hold values from -0.21875 to 0.21875
- step_proj: bfloat16 [768, 24], P(('shard', 'context'), 'tensor'), may hold values from -0.21875 to 0.21875
- conv_value: float32 [4, 1536], P(None, 'tensor'), may hold values from -0.5 to 0.5
- conv_state: float32 [4, 256], P(None, 'tensor'), may hold values from -0.5 to 0.5
- value_bias: float32 [1536], P('tensor'), may hold values from -0.5 to 0.5
- state_bias: float32 [256], P('tensor'), may hold values from -0.5 to 0.5
- step_bias: float32 [24], P('tensor'), may hold values from -3 to -1
- decay_log: float32 [24], P('tensor'), may hold values from -10 to -1
- skip_gain: float32 [24], P('tensor'), may hold values from 0.5 to 3
- mixer_gain: float32 [1536], P('tensor'), may hold values from 0.5 to 1.5
- out_proj: bfloat16 [1536, 768], P('tensor', ('shard', 'context')), may hold values from -0.15625 to 0.15625
Outputs:
- output: bfloat16 [32768, 768], P(('shard', 'context'))
- grad_hidden: bfloat16 [32768, 768], P(('shard', 'context'))
- grad_norm_gain: float32 [768], replicated
- grad_gate_proj: float32 [768, 1536], P(('shard', 'context'), 'tensor')
- grad_value_proj: float32 [768, 1536], P(('shard', 'context'), 'tensor')
- grad_state_proj: float32 [768, 256], P(('shard', 'context'), 'tensor')
- grad_step_proj: float32 [768, 24], P(('shard', 'context'), 'tensor')
- grad_conv_value: float32 [4, 1536], P(None, 'tensor')
- grad_conv_state: float32 [4, 256], P(None, 'tensor')
- grad_value_bias: float32 [1536], P('tensor')
- grad_state_bias: float32 [256], P('tensor')
- grad_step_bias: float32 [24], P('tensor')
- grad_decay_log: float32 [24], P('tensor')
- grad_skip_gain: float32 [24], P('tensor')
- grad_mixer_gain: float32 [1536], P('tensor')
- grad_out_proj: float32 [1536, 768], P('tensor', ('shard', 'context'))
Inputs may be any that keep to these rules, and one draw needn't show every extreme that they name: Row g lists the lengths of the 4 sequences of group g in order; each row sums to 8192, and one sequence of each row starts among its first 2048 tokens and ends among its last 2048.
All inputs are finite; a program needn't handle non-finite values.
Results may differ from a plain program's by a relative error of at most 0.017.
Values may be sent and summed in bfloat16 or wider, within the bound.
No kernel may reach another device: no remote copies, remote signals or barrier semaphores. Data moves between devices by JAX's collectives and lax.ppermute only.
A program may use at most 128 MiB of HBM per device.

v0:
```python
import jax
import jax.numpy as jnp
from jax import lax
from jax.sharding import PartitionSpec as P

INNER = 1536
HEADDIM = 64
STATE = 128
CONV = 4
BLOCK = 256


HIGH = lax.Precision.HIGHEST
EPSILON = 1e-05


def passed_along(shard, axis, by):
    count = lax.axis_size(axis)
    pairs = [(i, i + by) for i in range(count) if 0 <= i + by < count]
    return lax.ppermute(shard, axis, pairs)


def carried_in(part, axis, combine, identity, reverse):
    count = lax.axis_size(axis)
    place = lax.axis_index(axis)
    ahead = count - 1 - place if reverse else place
    gathered = jax.tree.map(lambda a: lax.all_gather(a, axis), part)
    state = jax.tree.map(lambda a, e: jnp.zeros_like(a) + jnp.asarray(e, a.dtype), part, identity)

    def one(turn, state):
        source = count - 1 - turn if reverse else turn
        return combine(
            state, jax.tree.map(lambda a: lax.dynamic_index_in_dim(a, source, 0, False), gathered)
        )

    return lax.fori_loop(0, ahead, one, state)


def silu_slope(values):
    sigmoid_v = jax.nn.sigmoid(values)
    return sigmoid_v * (1.0 + values * (1.0 - sigmoid_v))


def segment_marks(lengths_row, first_pos, count):
    finishes = jnp.cumsum(lengths_row)
    starts = finishes - lengths_row
    places = first_pos + jnp.arange(count, dtype=jnp.int32)
    segment = jnp.sum((places[:, None] >= finishes[None, :]).astype(jnp.int32), axis=1)
    opening = jnp.sum((places[:, None] == starts[None, :]).astype(jnp.int32), axis=1)
    return (segment, opening)


def chain_join(earlier, following):
    return (earlier[0] * following[0], following[0][:, None, None] * earlier[1] + following[1])


def block_forward(values, timestep, log_decay, b_matrix, c_matrix, segment, opening):
    cumulative = jnp.cumsum(log_decay, axis=1)
    positions = jnp.arange(segment.shape[0], dtype=jnp.int32)
    allowed = (segment[:, None] == segment[None, :]) & (positions[None, :] <= positions[:, None])
    spread = cumulative[:, :, None] - cumulative[:, None, :]
    decays = jnp.where(allowed[None], jnp.exp(jnp.where(allowed[None], spread, 0.0)), 0.0)
    scores = jnp.einsum("in,jn->ij", c_matrix, b_matrix, preferred_element_type=jnp.float32)
    mixing = (scores[None] * decays * timestep[:, None, :]).astype(jnp.bfloat16)
    intra_out = jnp.einsum("hij,jhp->ihp", mixing, values, preferred_element_type=jnp.float32)
    carried = (jnp.cumsum(opening) == 0).astype(jnp.float32)
    lead_decay = jnp.exp(cumulative) * carried[None, :]
    last_same = (segment == segment[-1]).astype(jnp.float32)
    tail_base = jnp.exp(cumulative[:, -1:] - cumulative) * last_same[None, :]
    tail_decay = tail_base * timestep
    packed = (values.astype(jnp.float32) * tail_decay.T[:, :, None]).astype(jnp.bfloat16)
    fresh_state = jnp.einsum("jhp,jn->hpn", packed, b_matrix, preferred_element_type=jnp.float32)
    return (
        (decays, scores, mixing, lead_decay, tail_base, tail_decay, packed),
        intra_out,
        fresh_state,
    )


def block_backward(kept, d_out, state_in, state_grad, reach, b_matrix, c_matrix, values, timestep):
    decays, scores, mixing, lead_decay, tail_base, tail_decay, packed = kept
    b_float = b_matrix.astype(jnp.float32)
    c_float = c_matrix.astype(jnp.float32)
    v_float = values.astype(jnp.float32)
    held_state = state_in.astype(jnp.bfloat16).astype(jnp.float32)
    last_lead = lead_decay[:, -1]
    lead_last_grad = jnp.sum(state_grad * state_in, axis=(1, 2))
    packed_grad = jnp.einsum("jn,hpn->jhp", b_float, state_grad, precision=HIGH)
    value_grad = packed_grad * tail_decay.T[:, :, None]
    tail_grad = jnp.sum(packed_grad * v_float, axis=2).T
    b_grad = jnp.einsum("jhp,hpn->jn", packed.astype(jnp.float32), state_grad, precision=HIGH)
    cross_term = jnp.einsum("in,hpn->ihp", c_float, held_state, precision=HIGH)
    lead_grad = jnp.sum(d_out * cross_term, axis=2).T
    c_grad = jnp.einsum("ihp,hpn->in", d_out * lead_decay.T[:, :, None], held_state, precision=HIGH)
    mix_grad = jnp.einsum("ihp,jhp->hij", d_out, v_float, precision=HIGH)
    value_grad = value_grad + jnp.einsum(
        "hij,ihp->jhp", mixing.astype(jnp.float32), d_out, precision=HIGH
    )
    score_grad = jnp.sum(mix_grad * decays * timestep[:, None, :], axis=0)
    time_grad = jnp.sum(mix_grad * scores[None] * decays, axis=1) + tail_grad * tail_base
    decay_term = mix_grad * scores[None] * timestep[:, None, :] * decays
    c_grad = c_grad + jnp.dot(score_grad, b_float, precision=HIGH)
    b_grad = b_grad + jnp.einsum("ij,in->jn", score_grad, c_float, precision=HIGH)
    tail_term = tail_grad * tail_decay
    cumul_grad = (
        jnp.sum(decay_term, axis=2)
        - jnp.sum(decay_term, axis=1)
        + lead_grad * lead_decay
        - tail_term
    )
    last_column = jnp.sum(tail_term, axis=1) + lead_last_grad * last_lead
    cumul_grad = cumul_grad.at[:, -1].add(last_column)
    log_grad = lax.cumsum(cumul_grad, axis=1, reverse=True)
    entry_grad = last_lead[:, None, None] * state_grad + reach
    return (value_grad, b_grad, c_grad, time_grad, log_grad, entry_grad)


def body(
    hidden,
    cotangent,
    lengths,
    norm_gain,
    gate_proj,
    value_proj,
    state_proj,
    step_proj,
    conv_value,
    conv_state,
    value_bias,
    state_bias,
    step_bias,
    decay_log,
    skip_gain,
    mixer_gain,
    out_proj,
):
    tok_rows = hidden.shape[0]
    head_count = step_bias.shape[0]
    inner_local = gate_proj.shape[1]
    ctx_index = lax.axis_index("context")
    first_pos = ctx_index * tok_rows
    segment, opening = segment_marks(lengths[0], first_pos, tok_rows)
    edge_segment, unused_marks = segment_marks(lengths[0], first_pos - (CONV - 1), CONV - 1)
    full_gate, full_value, full_state, full_step, full_out = (
        lax.all_gather(gate_proj, ("shard", "context"), axis=0, tiled=True),
        lax.all_gather(value_proj, ("shard", "context"), axis=0, tiled=True),
        lax.all_gather(state_proj, ("shard", "context"), axis=0, tiled=True),
        lax.all_gather(step_proj, ("shard", "context"), axis=0, tiled=True),
        lax.all_gather(out_proj, ("shard", "context"), axis=1, tiled=True),
    )
    residual = hidden.astype(jnp.float32)
    scaling = lax.rsqrt(jnp.mean(residual * residual, axis=1, keepdims=True) + EPSILON)
    unit_rows = residual * scaling
    normed = (unit_rows * norm_gain[None, :]).astype(jnp.bfloat16)
    gate_pre = jnp.dot(normed, full_gate, preferred_element_type=jnp.float32)
    value_pre = jnp.dot(normed, full_value, preferred_element_type=jnp.float32)
    state_pre = jnp.dot(normed, full_state, preferred_element_type=jnp.float32)
    step_pre = jnp.dot(normed, full_step, preferred_element_type=jnp.float32)
    conv_input = jnp.concatenate([value_pre, state_pre], axis=1).astype(jnp.bfloat16)
    edge_rows = passed_along(conv_input[tok_rows - (CONV - 1) :], "context", 1)
    extended = jnp.concatenate([edge_rows, conv_input], axis=0).astype(jnp.float32)
    ext_segment = jnp.concatenate([edge_segment, segment])
    conv_taps = jnp.concatenate([conv_value, conv_state], axis=1)
    channel_width = conv_taps.shape[1]
    conv_out = jnp.broadcast_to(
        jnp.concatenate([value_bias, state_bias])[None, :], (tok_rows, channel_width)
    )
    seq_masks = []
    for kernel_pos in range(CONV):
        same_seq = (ext_segment[kernel_pos : kernel_pos + tok_rows] == segment).astype(jnp.float32)[
            :, None
        ]
        seq_masks.append(same_seq)
        conv_out = (
            conv_out
            + conv_taps[kernel_pos][None, :]
            * extended[kernel_pos : kernel_pos + tok_rows]
            * same_seq
        )
    activated = jax.nn.silu(conv_out)
    x_values = activated[:, :inner_local].astype(jnp.bfloat16)
    state_local = activated[:, inner_local:].astype(jnp.bfloat16)
    state_full = lax.all_gather(state_local, "tensor", axis=1, tiled=True)
    b_matrix = state_full[:, :STATE]
    c_matrix = state_full[:, STATE:]
    timestep = jax.nn.softplus(step_pre + step_bias[None, :])
    rates = -jnp.exp(decay_log)
    log_decay = timestep * rates[None, :]
    head_values = x_values.reshape(tok_rows, head_count, HEADDIM)
    blocks = tok_rows // BLOCK
    kept_parts = []
    intra_parts = []
    fresh_parts = []
    dev_decay = jnp.ones((head_count,), jnp.float32)
    dev_state = jnp.zeros((head_count, HEADDIM, STATE), jnp.float32)
    for block_index in range(blocks):
        lower = block_index * BLOCK
        upper = lower + BLOCK
        kept, intra_out, fresh_state = block_forward(
            head_values[lower:upper],
            timestep[lower:upper].T,
            log_decay[lower:upper].T,
            b_matrix[lower:upper],
            c_matrix[lower:upper],
            segment[lower:upper],
            opening[lower:upper],
        )
        kept_parts.append(kept)
        intra_parts.append(intra_out)
        fresh_parts.append(fresh_state)
        last_lead = kept[3][:, -1]
        dev_state = last_lead[:, None, None] * dev_state + fresh_state
        dev_decay = dev_decay * last_lead
    identity = (
        jnp.ones((head_count,), jnp.float32),
        jnp.zeros((head_count, HEADDIM, STATE), jnp.float32),
    )
    prefix = carried_in((dev_decay, dev_state), "context", chain_join, identity, False)
    state_now = prefix[1]
    block_outs = []
    entry_states = []
    for block_index in range(blocks):
        lower = block_index * BLOCK
        upper = lower + BLOCK
        entry_states.append(state_now)
        lead_decay = kept_parts[block_index][3]
        held_state = state_now.astype(jnp.bfloat16)
        cross_term = jnp.einsum(
            "in,hpn->ihp", c_matrix[lower:upper], held_state, preferred_element_type=jnp.float32
        )
        block_outs.append(intra_parts[block_index] + lead_decay.T[:, :, None] * cross_term)
        state_now = lead_decay[:, -1][:, None, None] * state_now + fresh_parts[block_index]
    head_float = head_values.astype(jnp.float32)
    ssd_out = jnp.concatenate(block_outs, axis=0) + skip_gain[None, :, None] * head_float
    y_rows = ssd_out.reshape(tok_rows, inner_local)
    gate_act = jax.nn.silu(gate_pre)
    gated = y_rows * gate_act
    squares = jnp.sum(gated * gated, axis=1)
    mixed = (gated * mixer_gain[None, :]).astype(jnp.bfloat16)
    partial_value = jnp.dot(mixed, full_out, preferred_element_type=jnp.float32)
    projected, square_total = (
        lax.psum(partial_value.astype(jnp.bfloat16), "tensor").astype(jnp.float32),
        lax.psum(squares.astype(jnp.bfloat16), "tensor").astype(jnp.float32),
    )
    root_fwd = lax.rsqrt(square_total / INNER + EPSILON)
    output = (residual + root_fwd[:, None] * projected).astype(jnp.bfloat16)
    cot_rows = cotangent.astype(jnp.float32)
    back_rows = jnp.einsum("td,kd->tk", cotangent, full_out, preferred_element_type=jnp.float32)
    mixed_float = mixed.astype(jnp.float32)
    dot_part = jnp.sum(back_rows * mixed_float, axis=1)
    square_sum, dot_total = lax.psum((squares, dot_part), "tensor")
    root = lax.rsqrt(square_sum / INNER + EPSILON)
    mixed_grad = root[:, None] * back_rows
    grad_out = jnp.einsum("tk,td->kd", mixed_float, root[:, None] * cot_rows, precision=HIGH)
    grad_mixer = jnp.sum(gated * mixed_grad, axis=0)
    gated_grad = mixer_gain[None, :] * mixed_grad - (dot_total * root**3 / INNER)[:, None] * gated
    y_grad = gated_grad * gate_act
    gate_grad = gated_grad * y_rows * silu_slope(gate_pre)
    head_grads = y_grad.reshape(tok_rows, head_count, HEADDIM)
    grad_skip = jnp.sum(head_grads * head_float, axis=(0, 2))
    reach_parts = []
    for block_index in range(blocks):
        lower = block_index * BLOCK
        upper = lower + BLOCK
        lead_decay = kept_parts[block_index][3]
        lead_dout = head_grads[lower:upper] * lead_decay.T[:, :, None]
        reach_parts.append(
            jnp.einsum(
                "ihp,in->hpn", lead_dout, c_matrix[lower:upper].astype(jnp.float32), precision=HIGH
            )
        )
    back_state = jnp.zeros((head_count, HEADDIM, STATE), jnp.float32)
    for block_index in range(blocks - 1, -1, -1):
        back_state = (
            kept_parts[block_index][3][:, -1][:, None, None] * back_state + reach_parts[block_index]
        )
    suffix = carried_in((dev_decay, back_state), "context", chain_join, identity, True)
    state_grad = suffix[1]
    value_list = [None] * blocks
    b_list = [None] * blocks
    c_list = [None] * blocks
    time_list = [None] * blocks
    log_list = [None] * blocks
    for block_index in range(blocks - 1, -1, -1):
        lower = block_index * BLOCK
        upper = lower + BLOCK
        value_grad, b_grad, c_grad, time_grad, log_grad, state_grad = block_backward(
            kept_parts[block_index],
            head_grads[lower:upper],
            entry_states[block_index],
            state_grad,
            reach_parts[block_index],
            b_matrix[lower:upper],
            c_matrix[lower:upper],
            head_values[lower:upper],
            timestep[lower:upper].T,
        )
        value_list[block_index] = value_grad
        b_list[block_index] = b_grad
        c_list[block_index] = c_grad
        time_list[block_index] = time_grad
        log_list[block_index] = log_grad
    value_grads = jnp.concatenate(value_list, axis=0) + skip_gain[None, :, None] * head_grads
    time_grads = jnp.concatenate(time_list, axis=1)
    log_grads = jnp.concatenate(log_list, axis=1)
    time_total = (time_grads + log_grads * rates[:, None]).T
    grad_decay = jnp.sum(log_grads * timestep.T, axis=1) * rates
    step_grad = time_total * jax.nn.sigmoid(step_pre + step_bias[None, :])
    grad_step_bias = jnp.sum(step_grad, axis=0)
    bc_grads = jnp.concatenate(
        [jnp.concatenate(b_list, axis=0), jnp.concatenate(c_list, axis=0)], axis=1
    )
    bc_local_grad = lax.psum_scatter(bc_grads, "tensor", scatter_dimension=1, tiled=True)
    act_grad = jnp.concatenate(
        [value_grads.reshape(tok_rows, inner_local), bc_local_grad], axis=1
    ) * silu_slope(conv_out)
    tap_grads = []
    ext_grad = jnp.zeros((tok_rows + CONV - 1, channel_width), jnp.float32)
    for kernel_pos in range(CONV):
        masked_grad = act_grad * seq_masks[kernel_pos]
        tap_grads.append(
            jnp.sum(masked_grad * extended[kernel_pos : kernel_pos + tok_rows], axis=0)
        )
        ext_grad = ext_grad.at[kernel_pos : kernel_pos + tok_rows].add(
            conv_taps[kernel_pos][None, :] * masked_grad
        )
    grad_taps = jnp.stack(tap_grads)
    grad_biases = jnp.sum(act_grad, axis=0)
    spill = passed_along(ext_grad[: CONV - 1], "context", -1)
    input_grad = ext_grad[CONV - 1 :] + jnp.concatenate(
        [jnp.zeros((tok_rows - (CONV - 1), channel_width), jnp.float32), spill], axis=0
    )
    gate_low = gate_grad.astype(jnp.bfloat16)
    value_low = input_grad[:, :inner_local].astype(jnp.bfloat16)
    state_low = input_grad[:, inner_local:].astype(jnp.bfloat16)
    step_low = step_grad.astype(jnp.bfloat16)
    grad_gate = jnp.einsum("td,tk->dk", normed, gate_low, preferred_element_type=jnp.float32)
    grad_value = jnp.einsum("td,tk->dk", normed, value_low, preferred_element_type=jnp.float32)
    grad_state = jnp.einsum("td,tk->dk", normed, state_low, preferred_element_type=jnp.float32)
    grad_step = jnp.einsum("td,tk->dk", normed, step_low, preferred_element_type=jnp.float32)
    normed_part = jnp.einsum("tk,dk->td", gate_low, full_gate, preferred_element_type=jnp.float32)
    normed_part = normed_part + jnp.einsum(
        "tk,dk->td", value_low, full_value, preferred_element_type=jnp.float32
    )
    normed_part = normed_part + jnp.einsum(
        "tk,dk->td", state_low, full_state, preferred_element_type=jnp.float32
    )
    normed_part = normed_part + jnp.einsum(
        "tk,dk->td", step_low, full_step, preferred_element_type=jnp.float32
    )
    normed_grad = lax.psum(normed_part, "tensor")
    scaled_grad = normed_grad * norm_gain[None, :]
    grad_norm = jnp.sum(normed_grad * unit_rows, axis=0)
    hidden_grad = cot_rows + scaling * (
        scaled_grad - unit_rows * jnp.mean(scaled_grad * unit_rows, axis=1, keepdims=True)
    )
    owned_gate, owned_value, owned_state, owned_step, owned_out = (
        lax.psum_scatter(grad_gate, ("shard", "context"), scatter_dimension=0, tiled=True),
        lax.psum_scatter(grad_value, ("shard", "context"), scatter_dimension=0, tiled=True),
        lax.psum_scatter(grad_state, ("shard", "context"), scatter_dimension=0, tiled=True),
        lax.psum_scatter(grad_step, ("shard", "context"), scatter_dimension=0, tiled=True),
        lax.psum_scatter(grad_out, ("shard", "context"), scatter_dimension=1, tiled=True),
    )
    summed_small = lax.psum(
        (
            grad_norm,
            grad_taps[:, :inner_local],
            grad_taps[:, inner_local:],
            grad_biases[:inner_local],
            grad_biases[inner_local:],
            grad_step_bias,
            grad_decay,
            grad_skip,
            grad_mixer,
        ),
        ("shard", "context"),
    )
    return (
        output,
        hidden_grad.astype(jnp.bfloat16),
        summed_small[0],
        owned_gate,
        owned_value,
        owned_state,
        owned_step,
        summed_small[1],
        summed_small[2],
        summed_small[3],
        summed_small[4],
        summed_small[5],
        summed_small[6],
        summed_small[7],
        summed_small[8],
        owned_out,
    )


def solution(mesh):
    placed = (
        P(("shard", "context"), None),
        P(("shard", "context"), None),
        P("shard", None),
        P(),
        P(("shard", "context"), "tensor"),
        P(("shard", "context"), "tensor"),
        P(("shard", "context"), "tensor"),
        P(("shard", "context"), "tensor"),
        P(None, "tensor"),
        P(None, "tensor"),
        P("tensor"),
        P("tensor"),
        P("tensor"),
        P("tensor"),
        P("tensor"),
        P("tensor"),
        P("tensor", ("shard", "context")),
    )
    return jax.shard_map(
        body,
        mesh=mesh,
        in_specs=placed,
        out_specs=(
            P(("shard", "context"), None),
            P(("shard", "context"), None),
            P(),
            P(("shard", "context"), "tensor"),
            P(("shard", "context"), "tensor"),
            P(("shard", "context"), "tensor"),
            P(("shard", "context"), "tensor"),
            P(None, "tensor"),
            P(None, "tensor"),
            P("tensor"),
            P("tensor"),
            P("tensor"),
            P("tensor"),
            P("tensor"),
            P("tensor"),
            P("tensor", ("shard", "context")),
        ),
        check_vma=False,
    )
```

profile of v0, /device:TPU:0, one launch (start us, length us, event | category | flops | bytes accessed | tf_op | source)
XLA Modules:
  0.0 1067.4 jit_solution(3625054394692992079)
XLA Ops:
  7.3 2.6 fusion.11
  9.9 25.1 %all-gather.3 = bf16[16,48,32]{1,2,0:T(8,128)(2,1)S(1)} all-gather(bf16[1,48,32]{1,2,0:T(8,128)(2,1)S(1)} %bitcast.1034), channel_id=1, replica_groups=mesh['shard'=4,'context'=4,'tensor'=8] {'shard','context'}, dimensions={0}, use_global_device_ids=true | all-gather | bytes 52224 | tf_op jit(solution)/shard_map/all_gather | solution.py:147
  35.2 23.2 %all_gather.36 = bf16[768,192]{1,0:T(8,128)(2,1)S(1)} all-gather(bf16[48,192]{1,0:T(8,128)(2,1)S(1)} %copy-done.219), channel_id=1, replica_groups=mesh['shard'=4,'context'=4,'tensor'=8] {'shard','context'}, dimensions={0}, use_global_device_ids=true | all-gather | bytes 313344 | tf_op jit(solution)/shard_map/all_gather | solution.py:146
  58.4 2.8 fusion.6
  76.4 22.6 %all-gather.4 = bf16[16,48,3]{1,2,0:T(4,128)(2,1)S(1)} all-gather(bf16[1,48,3]{1,2,0:T(4,128)(2,1)S(1)} %bitcast.1072), channel_id=1, replica_groups=mesh['shard'=4,'context'=4,'tensor'=8] {'shard','context'}, dimensions={0}, use_global_device_ids=true | all-gather | bytes 4896 | tf_op jit(solution)/shard_map/all_gather | solution.py:148
  119.0 5.2 compare_convert_fusion
  131.5 23.6 %all_gather.43 = bf16[768,192]{1,0:T(8,128)(2,1)} all-gather(bf16[48,192]{1,0:T(8,128)(2,1)S(1)} %copy-done.220), channel_id=1, replica_groups=mesh['shard'=4,'context'=4,'tensor'=8] {'shard','context'}, dimensions={0}, use_global_device_ids=true | all-gather | bytes 313344 | tf_op jit(solution)/shard_map/all_gather | solution.py:145
  158.9 2.8 multiply_convert_fusion
  163.6 25.1 %all_gather.44 = bf16[192,768]{0,1:T(8,128)(2,1)} all-gather(bf16[192,48]{0,1:T(8,128)(2,1)S(1)} %copy-done.221), channel_id=1, replica_groups=mesh['shard'=4,'context'=4,'tensor'=8] {'shard','context'}, dimensions={1}, use_global_device_ids=true | all-gather | bytes 313344 | tf_op jit(solution)/shard_map/all_gather | solution.py:149
  188.7 8.8 all-reduce.2
  203.9 2.0 fusion.421
  214.8 13.3 %all-gather.1 = f32[12,64,128]{2,1,0:T(8,128)} all-gather(f32[3,64,128]{2,1,0:T(8,128)S(1)} %convolution_add_fusion.18), channel_id=3, replica_groups=mesh['shard'=4,'context'=4,'tensor'=8] {'context'}, dimensions={0}, use_global_device_ids=true | all-gather | bytes 491520 | tf_op jit(solution)/shard_map/all_gather | solution.py:27
  239.0 3.1 multiply_reduce_fusion.6
  242.6 12.6 %psum.100 = f32[2048]{0:T(1024)S(1)} all-reduce(f32[2048]{0:T(1024)S(1)} %get-tuple-element.393), channel_id=1, replica_groups=mesh['shard'=4,'context'=4,'tensor'=8] {'tensor'}, use_global_device_ids=true, to_apply=%region_42.43 | all-reduce | flops 2048 | bytes 16384 | tf_op jit(solution)/shard_map/psum | solution.py:251
  255.3 5.7 multiply_reduce_fusion.4
  261.0 13.1 %psum.101 = f32[2048]{0:T(1024)S(1)} all-reduce(f32[2048]{0:T(1024)S(1)} %get-tuple-element.298), channel_id=1, replica_groups=mesh['shard'=4,'context'=4,'tensor'=8] {'tensor'}, use_global_device_ids=true, to_apply=%region_44.45 | all-reduce | flops 2048 | bytes 16384 | tf_op jit(solution)/shard_map/psum | solution.py:251
  274.1 6.0 fusion.17
  304.8 16.3 %all-gather.2 = f32[12,64,128]{2,1,0:T(8,128)} all-gather(f32[3,64,128]{2,1,0:T(8,128)S(1)} %convolution_add_fusion.17), channel_id=4, replica_groups=mesh['shard'=4,'context'=4,'tensor'=8] {'context'}, dimensions={0}, use_global_device_ids=true | all-gather | bytes 491520 | tf_op jit(solution)/shard_map/all_gather | solution.py:27
  321.1 5.1 while.39
  354.2 1.9 convolution_bitcast_fusion.31
  357.4 2.3 fusion.26
  360.8 2.0 fusion.351
  367.5 4.5 reduce-window.231
  379.1 2.4 fusion.25
  382.6 2.0 fusion.352
  389.9 5.0 reduce-window.235
  402.7 2.4 fusion.24
  406.3 2.0 fusion.353
  410.9 2.3 fusion.23
  419.0 3.8 reduce-window.239
  423.6 3.8 reduce-window.241
  429.5 2.4 fusion.22
  433.0 2.0 fusion.355
  440.4 5.0 reduce-window.294
  451.9 2.3 fusion.21
  455.3 2.0 fusion.356
  459.9 2.3 fusion.20
  463.3 2.0 fusion.357
  471.5 4.5 reduce-window.296
  479.2 4.5 reduce-window.298
  489.3 2.2 fusion.19
  495.4 3.8 reduce-window.300
  520.9 3.7 fusion.424
  526.1 16.1 %reduce-scatter.7.cloned.1.call-done = f32[2048,32]{0,1:T(8,128)} async-done(((f32[2048,256]{0,1:T(8,128)}), f32[2048,32]{0,1:T(8,128)}) %reduce-scatter.7.cloned.1.call-update) | async-done | bytes 262160 | tf_op jit(solution)/shard_map/reduce_scatter | solution.py:313
  542.2 6.5 multiply_reduce_fusion.3
  553.3 10.1 scatter-add.39
  563.4 3.9 slice_add_fusion.1
  567.2 10.1 scatter-add.40
  579.7 3.7 fusion.314
  587.8 4.8 fusion.62
  592.7 10.2 add_add_fusion
  603.9 3.9 convolution_convert_fusion
  608.4 8.4 fusion.5
  618.4 12.5 %psum.98 = bf16[2048]{0:T(1024)(128)(2,1)S(1)} all-reduce(bf16[2048]{0:T(1024)(128)(2,1)S(1)} %convert_element_type.400), channel_id=1, replica_groups=mesh['shard'=4,'context'=4,'tensor'=8] {'tensor'}, use_global_device_ids=true, to_apply=%region_40.41 | all-reduce | flops 2048 | bytes 8192 | tf_op jit(solution)/shard_map/psum | solution.py:243
  631.0 3.1 fusion.425
  635.6 1.9 fusion.60
  637.6 36.4 %all-reduce.14.cloned.1.call-done = f32[768,32]{0,1:T(8,128)} async-done(((f32[768,32]{0,1:T(8,128)}), f32[768,32]{0,1:T(8,128)}) %all-reduce.14.cloned.1.call-update) | async-done | bytes 98320
  675.4 83.8 %all-reduce.12.cloned.1.call-done = f32[2048,768]{1,0:T(8,128)} async-done(((f32[2048,768]{1,0:T(8,128)}), f32[2048,768]{1,0:T(8,128)}) %all-reduce.12.cloned.1.call-update) | async-done | bytes 6291472 | tf_op jit(solution)/shard_map/psum | solution.py:351
  759.2 5.2 fusion.10
  764.5 74.5 %all-reduce.5 = (f32[768]{0:T(1024)}, f32[768,3]{0,1:T(4,128)S(1)}, f32[4,192]{1,0:T(4,128)}, f32[4,32]{1,0:T(4,128)}, f32[192]{0:T(256)}, /*index=5*/f32[32]{0:...) all-reduce(f32[768]{0:T(1024)S(1)} %get-tuple-element.290, ...), channel_id=1, replica_groups=mesh['shard'=4,'context'=4,'tensor'=8] {'shard','context'}, use_global_device_ids=true, to_apply=%region_131.132 | all-reduce | flops 4393 | bytes 35144 | tf_op jit(solution)/shard_map/psum | solution.py:364
  839.6 7.6 fusion.4
  847.2 60.8 %reduce-scatter.13.cloned.1.call-done = f32[192,48]{0,1:T(8,128)} async-done(((f32[192,768]{0,1:T(8,128)}), f32[192,48]{0,1:T(8,128)}) %reduce-scatter.13.cloned.1.call-update) | async-done | bytes 36880 | tf_op jit(solution)/shard_map/reduce_scatter | solution.py:362
  908.0 76.2 %reduce-scatter.9.cloned.1.call-done = f32[48,192]{1,0:T(8,128)} async-done(((f32[768,192]{1,0:T(8,128)}), f32[48,192]{1,0:T(8,128)}) %reduce-scatter.9.cloned.1.call-update) | async-done | bytes 36880 | tf_op jit(solution)/shard_map/reduce_scatter | solution.py:358
  984.2 76.2 %reduce-scatter.11.cloned.1.call-done = f32[48,192]{1,0:T(8,128)} async-done(((f32[768,192]{1,0:T(8,128)}), f32[48,192]{1,0:T(8,128)}) %reduce-scatter.11.cloned.1.call-update) | async-done | bytes 36880 | tf_op jit(solution)/shard_map/reduce_scatter | solution.py:359
  (1161 shorter events, 246.7 us)
Async XLA Ops:
  7.2 28.0 %copy-start.219 = (bf16[48,192]{1,0:T(8,128)(2,1)S(1)}, bf16[48,192]{1,0:T(8,128)(2,1)}, u32[]{:S(2)}) copy-start(bf16[48,192]{1,0:T(8,128)(2,1)} %param.50) | copy-start | bytes 55300
  7.2 51.2 %copy-start.205 = (f32[768]{0:T(1024)S(1)}, f32[768]{0:T(1024)}, u32[]{:S(2)}) copy-start(f32[768]{0:T(1024)} %param.48) | copy-start | bytes 9220
  7.2 198.7 %all-gather.7.cloned.1.call-start = ((), (), s32[]{:S(2)}) async-start(), calls=%async_computation.4 | async-start | bytes 1179648 | tf_op jit(solution)/shard_map/all_gather | solution.py:183
  9.8 48.6 %copy-start.143 = (f32[2048]{0:T(1024)}, f32[2048]{0:T(1024)S(1)}, u32[]{:S(2)}) copy-start(f32[2048]{0:T(1024)S(1)} %add_rsqrt_fusion.2) | copy-start | bytes 24580
  35.2 26.0 %copy-start.120 = (bf16[768,32]{0,1:T(8,128)(2,1)}, bf16[768,32]{0,1:T(8,128)(2,1)S(1)}, u32[]{:S(2)}) copy-start(bf16[768,32]{0,1:T(8,128)(2,1)S(1)} %reshape.1526) | copy-start | bytes 147460
  62.3 37.5 %copy-start.357 = (f32[3]{0:T(128)S(1)}, f32[3]{0:T(128)}, u32[]{:S(2)}) copy-start(f32[3]{0:T(128)} %param.57) | copy-start | bytes 40
  64.5 92.7 %collective-permute-start = (bf16[3,224]{0,1:T(8,128)(2,1)S(1)}, bf16[3,224]{0,1:T(8,128)(2,1)S(1)}, u32[]{:S(2)}, u32[]{:S(2)}) collective-permute-start(bf16[3,224]{0,1:T(8,128)(2,1)S(1)} %pad_maximum_fusion.1), channel_id=1, source_target_pairs={{0,8},{8,16},{16,24},{1,9},{9,17},{17,25},{2,10},{10,18},{18,26},{... | collective-permute-start | bytes 4040 | tf_op jit(solution)/shard_map/ppermute | solution.py:20
  68.0 33.4 %copy-start.308 = (f32[3]{0:T(128)}, f32[3]{0:T(128)S(1)}, u32[]{:S(2)}) copy-start(f32[3]{0:T(128)S(1)} %exponential_negate_fusion) | copy-start | bytes 40
  70.7 47.5 %copy-start.264 = (f32[256]{0:T(256)}, f32[256]{0:T(256)S(1)}, u32[]{:S(2)}) copy-start(f32[256]{0:T(256)S(1)} %fusion.359) | copy-start | bytes 3076
  75.4 42.9 %copy-start.263 = (f32[256]{0:T(256)}, f32[256]{0:T(256)S(1)}, u32[]{:S(2)}) copy-start(f32[256]{0:T(256)S(1)} %fusion.366) | copy-start | bytes 3076
  76.3 82.5 %copy-start.145 = (f32[2048]{0:T(1024)}, f32[2048]{0:T(1024)S(1)}, u32[]{:S(2)}) copy-start(f32[2048]{0:T(1024)S(1)} %get-tuple-element.450) | copy-start | bytes 24580
  76.3 82.5 %copy-start.147 = (f32[2048]{0:T(1024)}, f32[2048]{0:T(1024)S(1)}, u32[]{:S(2)}) copy-start(f32[2048]{0:T(1024)S(1)} %get-tuple-element.451) | copy-start | bytes 24580
  76.3 82.5 %copy-start.149 = (f32[2048]{0:T(1024)}, f32[2048]{0:T(1024)S(1)}, u32[]{:S(2)}) copy-start(f32[2048]{0:T(1024)S(1)} %get-tuple-element.449) | copy-start | bytes 24580
  99.8 31.6 %copy-start.220 = (bf16[48,192]{1,0:T(8,128)(2,1)S(1)}, bf16[48,192]{1,0:T(8,128)(2,1)}, u32[]{:S(2)}) copy-start(bf16[48,192]{1,0:T(8,128)(2,1)} %param.49) | copy-start | bytes 55300
  102.7 56.0 %copy-start.202 = (f32[1,3,2,128]{3,2,1,0:T(2,128)}, f32[1,3,2,128]{3,2,1,0:T(2,128)S(1)}, u32[]{:S(2)}) copy-start(f32[1,3,2,128]{3,2,1,0:T(2,128)S(1)} %add_bitcast_fusion.14) | copy-start | bytes 9220
  105.4 53.4 %copy-start.196 = (f32[1,3,2,128]{3,2,1,0:T(2,128)}, f32[1,3,2,128]{3,2,1,0:T(2,128)S(1)}, u32[]{:S(2)}) copy-start(f32[1,3,2,128]{3,2,1,0:T(2,128)S(1)} %add_bitcast_fusion.9) | copy-start | bytes 9220
  106.7 52.0 %copy-start.197 = (f32[1,3,2,128]{3,2,1,0:T(2,128)}, f32[1,3,2,128]{3,2,1,0:T(2,128)S(1)}, u32[]{:S(2)}) copy-start(f32[1,3,2,128]{3,2,1,0:T(2,128)S(1)} %add_bitcast_fusion.10) | copy-start | bytes 9220
  108.0 50.7 %copy-start.199 = (f32[1,3,2,128]{3,2,1,0:T(2,128)}, f32[1,3,2,128]{3,2,1,0:T(2,128)S(1)}, u32[]{:S(2)}) copy-start(f32[1,3,2,128]{3,2,1,0:T(2,128)S(1)} %add_bitcast_fusion.11) | copy-start | bytes 9220
  109.4 49.4 %copy-start.200 = (f32[1,3,2,128]{3,2,1,0:T(2,128)}, f32[1,3,2,128]{3,2,1,0:T(2,128)S(1)}, u32[]{:S(2)}) copy-start(f32[1,3,2,128]{3,2,1,0:T(2,128)S(1)} %add_bitcast_fusion.12) | copy-start | bytes 9220
  110.7 48.1 %copy-start.203 = (f32[1,3,2,128]{3,2,1,0:T(2,128)}, f32[1,3,2,128]{3,2,1,0:T(2,128)S(1)}, u32[]{:S(2)}) copy-start(f32[1,3,2,128]{3,2,1,0:T(2,128)S(1)} %add_bitcast_fusion.13) | copy-start | bytes 9220
  118.3 40.5 %copy-start.231 = (f32[3,256]{1,0:T(4,128)}, f32[3,256]{1,0:T(4,128)S(1)}, u32[]{:S(2)}) copy-start(f32[3,256]{1,0:T(4,128)S(1)} %get-tuple-element.526) | copy-start | bytes 9220
  118.3 40.4 %copy-start.224 = (f32[3,256]{1,0:T(4,128)}, f32[3,256]{1,0:T(4,128)S(1)}, u32[]{:S(2)}) copy-start(f32[3,256]{1,0:T(4,128)S(1)} %get-tuple-element.513) | copy-start | bytes 9220
  125.6 36.1 %copy-start.228 = (f32[3,256]{1,0:T(4,128)}, f32[3,256]{1,0:T(4,128)S(1)}, u32[]{:S(2)}) copy-start(f32[3,256]{1,0:T(4,128)S(1)} %get-tuple-element.530) | copy-start | bytes 9220
  125.6 36.1 %copy-start.229 = (f32[3,256]{1,0:T(4,128)}, f32[3,256]{1,0:T(4,128)S(1)}, u32[]{:S(2)}) copy-start(f32[3,256]{1,0:T(4,128)S(1)} %get-tuple-element.532) | copy-start | bytes 9220
  125.6 36.1 %copy-start.230 = (f32[3,256]{1,0:T(4,128)}, f32[3,256]{1,0:T(4,128)S(1)}, u32[]{:S(2)}) copy-start(f32[3,256]{1,0:T(4,128)S(1)} %get-tuple-element.528) | copy-start | bytes 9220
  127.1 34.7 %copy-start.225 = (f32[3,256]{1,0:T(4,128)}, f32[3,256]{1,0:T(4,128)S(1)}, u32[]{:S(2)}) copy-start(f32[3,256]{1,0:T(4,128)S(1)} %get-tuple-element.536) | copy-start | bytes 9220
  127.1 34.7 %copy-start.226 = (f32[3,256]{1,0:T(4,128)}, f32[3,256]{1,0:T(4,128)S(1)}, u32[]{:S(2)}) copy-start(f32[3,256]{1,0:T(4,128)S(1)} %get-tuple-element.538) | copy-start | bytes 9220
  127.1 34.7 %copy-start.227 = (f32[3,256]{1,0:T(4,128)}, f32[3,256]{1,0:T(4,128)S(1)}, u32[]{:S(2)}) copy-start(f32[3,256]{1,0:T(4,128)S(1)} %get-tuple-element.534) | copy-start | bytes 9220
  128.1 30.7 %copy-start.307 = (f32[3]{0:T(128)}, f32[3]{0:T(128)S(1)}, u32[]{:S(2)}) copy-start(f32[3]{0:T(128)S(1)} %get-tuple-element.335) | copy-start | bytes 40
  131.5 30.3 %copy-start.240 = (f32[1,224]{1,0:T(1,128)}, f32[1,224]{1,0:T(1,128)S(1)}, u32[]{:S(2)}) copy-start(f32[1,224]{1,0:T(1,128)S(1)} %get-tuple-element.510) | copy-start | bytes 2692
  131.5 30.3 %copy-start.242 = (f32[1,224]{1,0:T(1,128)}, f32[1,224]{1,0:T(1,128)S(1)}, u32[]{:S(2)}) copy-start(f32[1,224]{1,0:T(1,128)S(1)} %get-tuple-element.511) | copy-start | bytes 2692
  131.5 30.3 %copy-start.244 = (f32[1,224]{1,0:T(1,128)}, f32[1,224]{1,0:T(1,128)S(1)}, u32[]{:S(2)}) copy-start(f32[1,224]{1,0:T(1,128)S(1)} %get-tuple-element.509) | copy-start | bytes 2692
  131.5 30.3 %copy-start.289 = (f32[1,224]{1,0:T(1,128)}, f32[1,224]{1,0:T(1,128)S(1)}, u32[]{:S(2)}) copy-start(f32[1,224]{1,0:T(1,128)S(1)} %get-tuple-element.508) | copy-start | bytes 2692
  158.8 38.6 %copy-start.360 = (f32[3]{0:T(128)S(1)}, f32[3]{0:T(128)}, u32[]{:S(2)}) copy-start(f32[3]{0:T(128)} %param.59) | copy-start | bytes 40
  158.9 40.0 %copy-start.262 = (s32[256]{0:T(256)S(1)}, s32[256]{0:T(256)}, u32[]{:S(2)}) copy-start(s32[256]{0:T(256)} %get-tuple-element.469) | copy-start | bytes 3076
  158.9 40.7 %copy-start.261 = (s32[256]{0:T(256)S(1)}, s32[256]{0:T(256)}, u32[]{:S(2)}) copy-start(s32[256]{0:T(256)} %get-tuple-element.470) | copy-start | bytes 3076
  158.9 41.4 %copy-start.260 = (s32[256]{0:T(256)S(1)}, s32[256]{0:T(256)}, u32[]{:S(2)}) copy-start(s32[256]{0:T(256)} %get-tuple-element.471) | copy-start | bytes 3076
  158.9 42.1 %copy-start.259 = (s32[256]{0:T(256)S(1)}, s32[256]{0:T(256)}, u32[]{:S(2)}) copy-start(s32[256]{0:T(256)} %get-tuple-element.472) | copy-start | bytes 3076
  158.9 42.8 %copy-start.258 = (s32[256]{0:T(256)S(1)}, s32[256]{0:T(256)}, u32[]{:S(2)}) copy-start(s32[256]{0:T(256)} %get-tuple-element.473) | copy-start | bytes 3076
  158.9 43.5 %copy-start.257 = (s32[256]{0:T(256)S(1)}, s32[256]{0:T(256)}, u32[]{:S(2)}) copy-start(s32[256]{0:T(256)} %get-tuple-element.474) | copy-start | bytes 3076
  158.9 44.2 %copy-start.256 = (s32[256]{0:T(256)S(1)}, s32[256]{0:T(256)}, u32[]{:S(2)}) copy-start(s32[256]{0:T(256)} %get-tuple-element.475) | copy-start | bytes 3076
  163.5 378.7 %reduce-scatter.7.cloned.1.call-start = ((), (), s32[]{:S(2)}) async-start(), calls=%async_computation.6 | async-start | bytes 2359296 | tf_op jit(solution)/shard_map/reduce_scatter | solution.py:313
  205.9 31.2 %copy-start.54 = (bf16[256,192]{0,1:T(8,128)(2,1)}, bf16[256,192]{0,1:T(8,128)(2,1)S(1)}, u32[]{:S(2)}) copy-start(bf16[256,192]{0,1:T(8,128)(2,1)S(1)} %get-tuple-element.416) | copy-start | bytes 294916
  205.9 32.2 %copy-start.50 = (bf16[256,192]{0,1:T(8,128)(2,1)}, bf16[256,192]{0,1:T(8,128)(2,1)S(1)}, u32[]{:S(2)}) copy-start(bf16[256,192]{0,1:T(8,128)(2,1)S(1)} %get-tuple-element.415) | copy-start | bytes 294916
  229.6 67.2 %copy-start.33 = (f32[3,64,128]{2,1,0:T(8,128)}, f32[3,64,128]{2,1,0:T(8,128)S(1)}, u32[]{:S(2)}) copy-start(f32[3,64,128]{2,1,0:T(8,128)S(1)} %get-tuple-element.397) | copy-start | bytes 294916
  280.3 23.8 %copy-start.19 = (f32[256,192]{0,1:T(8,128)}, f32[256,192]{0,1:T(8,128)S(1)}, u32[]{:S(2)}) copy-start(f32[256,192]{0,1:T(8,128)S(1)} %get-tuple-element.414) | copy-start | bytes 589828
  280.3 24.1 %copy-start.31 = (f32[256,192]{0,1:T(8,128)}, f32[256,192]{0,1:T(8,128)S(1)}, u32[]{:S(2)}) copy-start(f32[256,192]{0,1:T(8,128)S(1)} %get-tuple-element.408) | copy-start | bytes 589828
  360.7 40.8 %copy-start.71 = (bf16[256,192]{0,1:T(8,128)(2,1)S(1)}, bf16[256,192]{0,1:T(8,128)(2,1)}, u32[]{:S(2)}) copy-start(bf16[256,192]{0,1:T(8,128)(2,1)} %get-tuple-element.420) | copy-start | bytes 294916
  381.5 29.4 %copy-start.172 = (f32[3,256]{1,0:T(4,128)S(1)}, f32[3,256]{1,0:T(4,128)}, u32[]{:S(2)}) copy-start(f32[3,256]{1,0:T(4,128)} %get-tuple-element.436) | copy-start | bytes 9220
  413.2 38.6 %copy-start.169 = (f32[3,256]{1,0:T(4,128)S(1)}, f32[3,256]{1,0:T(4,128)}, u32[]{:S(2)}) copy-start(f32[3,256]{1,0:T(4,128)} %get-tuple-element.433) | copy-start | bytes 9220
  429.5 24.7 %copy-start.34 = (f32[3,64,128]{2,1,0:T(8,128)S(1)}, f32[3,64,128]{2,1,0:T(8,128)}, u32[]{:S(2)}) copy-start(f32[3,64,128]{2,1,0:T(8,128)} %copy-done.33) | copy-start | bytes 294916
  455.2 32.9 %copy-start.53 = (bf16[256,192]{0,1:T(8,128)(2,1)S(1)}, bf16[256,192]{0,1:T(8,128)(2,1)}, u32[]{:S(2)}) copy-start(bf16[256,192]{0,1:T(8,128)(2,1)} %copy-done.50) | copy-start | bytes 294916
  513.4 160.5 %all-reduce.14.cloned.1.call-start = ((), (), s32[]{:S(2)}) async-start(), calls=%async_computation.11 | async-start | bytes 196608
  578.2 6.7 collective-permute-start.1
  592.6 166.6 %all-reduce.12.cloned.1.call-start = ((), (), s32[]{:S(2)}) async-start(), calls=%async_computation.7 | async-start | bytes 12582912 | tf_op jit(solution)/shard_map/psum | solution.py:351
  602.9 236.7 %all-reduce.10.cloned.1.call-start = ((), (), s32[]{:S(2)}) async-start(), calls=%async_computation.5 | async-start | bytes 6291456 | tf_op jit(solution)/shard_map/psum | solution.py:242
  607.8 300.2 %reduce-scatter.13.cloned.1.call-start = ((), (), s32[]{:S(2)}) async-start(), calls=%async_computation.10 | async-start | bytes 835584 | tf_op jit(solution)/shard_map/reduce_scatter | solution.py:362
  616.8 367.3 %reduce-scatter.9.cloned.1.call-start = ((), (), s32[]{:S(2)}) async-start(), calls=%async_computation.8 | async-start | bytes 835584 | tf_op jit(solution)/shard_map/reduce_scatter | solution.py:358
  634.2 426.2 %reduce-scatter.11.cloned.1.call-start = ((), (), s32[]{:S(2)}) async-start(), calls=%async_computation.9 | async-start | bytes 835584 | tf_op jit(solution)/shard_map/reduce_scatter | solution.py:359
  635.6 123.6 %copy-start.144 = (f32[2048]{0:T(1024)S(1)}, f32[2048]{0:T(1024)}, u32[]{:S(2)}) copy-start(f32[2048]{0:T(1024)} %copy-done.143) | copy-start | bytes 24580
  635.6 123.6 %copy-start.206 = (f32[768]{0:T(1024)S(1)}, f32[768]{0:T(1024)}, u32[]{:S(2)}) copy-start(f32[768]{0:T(1024)} %param.48) | copy-start | bytes 9220
  675.4 89.1 %copy-start.317 = (f32[192]{0:T(256)S(1)}, f32[192]{0:T(256)}, u32[]{:S(2)}) copy-start(f32[192]{0:T(256)} %get-tuple-element.297) | copy-start | bytes 2308
  675.4 89.1 %copy-start.356 = (f32[3]{0:T(128)S(1)}, f32[3]{0:T(128)}, u32[]{:S(2)}) copy-start(f32[3]{0:T(128)} %get-tuple-element.376) | copy-start | bytes 40
  759.2 80.4 %copy-start.1 = (bf16[2048,768]{1,0:T(8,128)(2,1)S(1)}, bf16[2048,768]{1,0:T(8,128)(2,1)}, u32[]{:S(2)}) copy-start(bf16[2048,768]{1,0:T(8,128)(2,1)} %param.45) | copy-start | bytes 9437188
  (311 other events, 1802.6 us)
Sparse Core Ops, SparseCore 0:
  163.6 22.8 all-gather.6
  513.5 28.6 reduce-scatter.6
  592.8 81.1 all-reduce.13
  676.3 82.8 all-reduce.11
  762.1 69.5 all-reduce.9
  835.7 72.2 reduce-scatter.12
  912.1 72.0 reduce-scatter.8
  988.3 72.0 reduce-scatter.10
where the time goes:
time: 1080 us; the launch traced here: 1070 us
  waiting for transfers between devices  351 us (32%)
  blocking collectives  271 us (25%)
  other arithmetic  160 us (15%)
  matrix products  150 us (14%)
  local copies, waits for them, and re-layouts  111 us (10%)
  between operations  20.4 us (2%)
    psum x1, waiting for transfers between devices, body(): normed_grad = lax.psum(normed_part, 'tensor')  83.8 us
    reduce_scatter x1, waiting for transfers between devices, body(): lax.psum_scatter(grad_gate, ('shard', 'context'), scatter_dimension=0, ti...  76.2 us
    reduce_scatter x1, waiting for transfers between devices, body(): lax.psum_scatter(grad_value, ('shard', 'context'), scatter_dimension=0, t...  76.2 us
    psum x1, blocking collectives, body(): lax.psum((grad_norm, grad_taps[:, :inner_local], grad_taps[:, inner_local...  74.5 us
    reduce_scatter x1, waiting for transfers between devices, body(): lax.psum_scatter(grad_out, ('shard', 'context'), scatter_dimension=1, til...  60.8 us
    another operation x51, other arithmetic  54.7 us
    unnamed x9, waiting for transfers between devices  36.5 us
    all_gather x2, blocking collectives, carried_in(): gathered = jax.tree.map(lambda a: lax.all_gather(a, axis), part)  29.5 us
  transfers between devices with their start and end apart: 10, of which 7 were waited for; matrix products, arithmetic and copies ran while one was open for 10% of the time, Pallas kernels for 0%

commit v1 on v0

v1 whole, which is shorter than its diff:
```python
import jax
import jax.numpy as jnp
from jax import lax
from jax.experimental import pallas as pl
from jax.experimental.pallas import tpu as pltpu
from jax.sharding import PartitionSpec as P

MODEL = 768
INNER = 1536
HEADDIM = 64
STATE = 128
CONV = 4
BLOCK = 256
HEADS_DEV = 3
INNER_DEV = 192
WIDE = 256
CHAN = 512
EPSILON = 1e-05
F32 = jnp.float32
BF16 = jnp.bfloat16
CELLS = ("shard", "context")
VMEM_LIMIT = 60 * 1024 * 1024


def nn(a, b):
    return lax.dot_general(a, b, (((1,), (0,)), ((), ())), preferred_element_type=F32)


def nt(a, b):
    return lax.dot_general(a, b, (((1,), (1,)), ((), ())), preferred_element_type=F32)


def tn(a, b):
    return lax.dot_general(a, b, (((0,), (0,)), ((), ())), preferred_element_type=F32)


def iota(shape, dim):
    return lax.broadcasted_iota(jnp.int32, shape, dim)


def start_of(marks, pos):
    start = jnp.zeros_like(pos)
    for k in range(3):
        start = jnp.where(pos >= marks[k], marks[k], start)
    return start


def end_of(marks, pos):
    end = jnp.full_like(pos, marks[3])
    for k in (2, 1, 0):
        end = jnp.where(pos < marks[k], marks[k], end)
    return end


def running_sum(rows, ones):
    top = rows.astype(BF16)
    rest = rows - top.astype(F32)
    mid = rest.astype(BF16)
    low = (rest - mid.astype(F32)).astype(BF16)
    pieces = [top.astype(F32), mid.astype(F32), low.astype(F32), jnp.zeros((8, BLOCK), F32)]
    sums = nn(jnp.concatenate(pieces, axis=0).astype(BF16), ones)
    return sums[0:8] + sums[8:16] + sums[16:24]


def by_head(cols, width=WIDE):
    lane = iota((1, width), 1)
    return jnp.where(
        lane < HEADDIM,
        cols[0],
        jnp.where(lane < 2 * HEADDIM, cols[1], jnp.where(lane < 3 * HEADDIM, cols[2], 0.0)),
    )


def head_masks():
    row = iota((8, WIDE), 0)
    lane = iota((8, WIDE), 1)
    low = row * HEADDIM
    return jnp.where((lane >= low) & (lane < low + HEADDIM) & (row < HEADS_DEV), 1.0, 0.0)


def of_head(values, h):
    lane = iota((1, WIDE), 1)
    return jnp.where((lane >= h * HEADDIM) & (lane < (h + 1) * HEADDIM), values, 0.0)


def to_columns(rows):
    have = 8 * len(rows)
    stacked = jnp.concatenate(list(rows) + [jnp.zeros((128 - have, BLOCK), F32)], axis=0)
    return stacked.T


def column(cols, part, h):
    at = 8 * part + h
    return cols[:, at : at + 1]


def silu_parts(values):
    sig = 1.0 / (1.0 + jnp.exp(-values))
    return values * sig, sig * (1.0 + values * (1.0 - sig))


class Block:
    def __init__(self, marks, b):
        self.marks = marks
        self.start = marks[4] + b * BLOCK
        self.pos_row = self.start + iota((1, BLOCK), 1)
        self.pos_col = self.start + iota((BLOCK, 1), 0)

    def lead(self, cum):
        carried = start_of(self.marks, self.pos_row) < self.start
        return jnp.where(carried, jnp.exp(cum), 0.0)

    def tail_base(self, cum):
        last = cum[:, BLOCK - 1 : BLOCK]
        kept = end_of(self.marks, self.pos_row) > self.start + BLOCK - 1
        return jnp.where(kept, jnp.exp(last - cum), 0.0)

    def allowed(self):
        first = start_of(self.marks, self.pos_col)
        return (self.pos_row >= first) & (self.pos_row <= self.pos_col)

    def since_start(self):
        return self.pos_col - start_of(self.marks, self.pos_col)

    def until_end(self):
        return end_of(self.marks, self.pos_col) - self.pos_col


def decay_of(allowed, cum_col, cum_row):
    return jnp.exp(jnp.where(allowed, cum_col - cum_row, -1e30))


def last_by_lane(rows):
    return by_head([rows[h : h + 1, BLOCK - 1 : BLOCK] for h in range(HEADS_DEV)])


def call(kernel, grid, in_specs, out_specs, out_shape, scratch, flops, moved, *args):
    return pl.pallas_call(
        kernel,
        grid=(grid,),
        in_specs=in_specs,
        out_specs=out_specs,
        out_shape=out_shape,
        scratch_shapes=scratch,
        compiler_params=pltpu.CompilerParams(
            dimension_semantics=("arbitrary",), vmem_limit_bytes=VMEM_LIMIT
        ),
        cost_estimate=pl.CostEstimate(flops=flops, bytes_accessed=moved, transcendentals=0),
    )(*args)


def shape(dims, dtype=F32):
    return jax.ShapeDtypeStruct(dims, dtype)


SMEM = pl.BlockSpec(memory_space=pltpu.SMEM)


def whole(dims):
    return pl.BlockSpec(dims, lambda s: (0,) * len(dims))


def project_kernel(
    marks, hidden, halo, gain, wv, ws, taps, cbias, hcols, upto,
    normed_o, xbc_o, slope_o, cin_o, cin_halo_o, rows_o, state_o, device_o,
    ext, state, decay,
):
    b = pl.program_id(0)
    blk = Block(marks, b)

    def norm(rows):
        rows = rows.astype(F32)
        scale = lax.rsqrt(jnp.mean(rows * rows, axis=1, keepdims=True) + EPSILON)
        return (rows * scale * gain[...]).astype(BF16)

    @pl.when(b == 0)
    def _():
        ahead = norm(halo[...])
        into = jnp.concatenate([nn(ahead, wv[...]), nn(ahead, ws[...])], axis=1)
        into = into.astype(BF16).astype(F32)
        ext[0:8] = into[8:16]
        cin_halo_o[...] = into[8:16]
        state[...] = jnp.zeros_like(state)
        decay[...] = jnp.ones_like(decay)

    normed = norm(hidden[...])
    normed_o[...] = normed
    value_pre = nn(normed, wv[...])
    state_pre = nn(normed, ws[...])
    cin = jnp.concatenate([value_pre, state_pre], axis=1).astype(BF16)
    cin_o[...] = cin
    ext[8 : 8 + BLOCK] = cin.astype(F32)
    pre = cbias[...] + taps[3:4] * ext[8 : 8 + BLOCK]
    since = blk.since_start()
    for lag in range(1, CONV):
        pre = pre + taps[3 - lag : 4 - lag] * (
            jnp.where(since >= lag, ext[8 - lag : 8 - lag + BLOCK], 0.0)
        )
    ext[0:8] = ext[BLOCK : BLOCK + 8]
    act, slope = silu_parts(pre)
    act = act.astype(BF16)
    xbc_o[...] = act
    slope_o[...] = slope.astype(BF16)

    raw = value_pre[:, 128:256].T[64:72] + hcols[0]
    dt = jnp.maximum(raw, 0.0) + jnp.log1p(jnp.exp(-jnp.abs(raw)))
    sig = 1.0 / (1.0 + jnp.exp(-raw))
    cum = running_sum(dt * hcols[1], upto[...])
    rows_o[0:8] = dt
    rows_o[8:16] = sig
    rows_o[16:24] = cum
    lead = blk.lead(cum)
    tail = blk.tail_base(cum) * dt
    cols = to_columns([tail])
    tail_lanes = by_head([column(cols, 0, h) for h in range(HEADS_DEV)])
    packed = (act[:, :WIDE].astype(F32) * tail_lanes).astype(BF16)
    fresh = tn(act[:, WIDE : WIDE + STATE], packed)
    last = last_by_lane(lead)
    state_o[0, 0:STATE] = state[...]
    state_o[0, STATE : STATE + 8] = decay[...]
    state[...] = last * state[...] + fresh
    decay[...] = last * decay[...]

    @pl.when(b == pl.num_programs(0) - 1)
    def _():
        device_o[0:STATE] = state[...]
        device_o[STATE : STATE + 8] = decay[...]


def intra_kernel(marks, normed, cot, wg, wo_t, xbc, rows, skip, z_o, e_o, yi_o):
    b = pl.program_id(0)
    blk = Block(marks, b)
    z_o[...] = nn(normed[...], wg[...])
    e_o[...] = nn(cot[...], wo_t[...])
    dt = rows[0:8]
    cum = rows[16:24]
    x = xbc[:, :WIDE].astype(F32)
    scores = nt(xbc[:, WIDE + STATE :], xbc[:, WIDE : WIDE + STATE])
    allowed = blk.allowed()
    cols = to_columns([cum])
    out = skip[...] * x
    for h in range(HEADS_DEV):
        decays = decay_of(allowed, column(cols, 0, h), cum[h : h + 1])
        mix = (scores * decays * dt[h : h + 1]).astype(BF16)
        out = out + nn(mix, of_head(x, h).astype(BF16))
    yi_o[...] = out


def gated_kernel(
    marks, yi, z, e, xbc, rows, states, prefix, mgain, wo_t, y_o, mixed_o, part_o, sums_o
):
    b = pl.program_id(0)
    blk = Block(marks, b)
    lead = blk.lead(rows[16:24])
    cols = to_columns([lead])
    lead_lanes = by_head([column(cols, 0, h) for h in range(HEADS_DEV)])
    entering = states[0, 0:STATE] + states[0, STATE : STATE + 1] * prefix[...]
    y = yi[...] + lead_lanes * nn(xbc[:, WIDE + STATE :], entering.astype(BF16))
    y_o[...] = y
    gate, _ = silu_parts(z[...])
    v = y * gate
    mixed = (v * mgain[...]).astype(BF16)
    mixed_o[...] = mixed
    part_o[...] = nt(mixed, wo_t[...]).astype(BF16)
    row = iota((8, 2 * WIDE), 0)
    lane = iota((8, 2 * WIDE), 1)
    pick = jnp.where(((row == 0) & (lane < WIDE)) | ((row == 1) & (lane >= WIDE)), 1.0, 0.0)
    both = jnp.concatenate([v * v, e[...] * mixed.astype(F32)], axis=1)
    sums_o[...] = nt(pick.astype(BF16), both.astype(BF16))


def gate_back_kernel(
    marks, y, z, e, xbc, rows, sums, mgain,
    dy_o, dz_o, reach_o, device_o, gains_o,
    carry, decay,
):
    s = pl.program_id(0)
    b = pl.num_programs(0) - 1 - s
    blk = Block(marks, b)

    @pl.when(s == 0)
    def _():
        carry[...] = jnp.zeros_like(carry)
        decay[...] = jnp.ones_like(decay)
        gains_o[...] = jnp.zeros_like(gains_o)

    lead = blk.lead(rows[16:24])
    root = lax.rsqrt(sums[0:1] / INNER + EPSILON)
    coef = sums[1:2] * root * root * root / INNER
    cols = to_columns([lead, jnp.broadcast_to(root, (8, BLOCK)), jnp.broadcast_to(coef, (8, BLOCK))])
    lead_lanes = by_head([column(cols, 0, h) for h in range(HEADS_DEV)])
    gate, slope = silu_parts(z[...])
    y_v = y[...]
    v = y_v * gate
    dm = column(cols, 1, 0) * e[...]
    dv = mgain[...] * dm - column(cols, 2, 0) * v
    dy = dv * gate
    dy_o[...] = dy
    dz_o[...] = (dv * y_v * slope).astype(BF16)
    x = xbc[:, :WIDE].astype(F32)
    gains_o[0:1] += jnp.sum(v * dm, axis=0, keepdims=True)
    gains_o[1:2] += jnp.sum(dy * x, axis=0, keepdims=True)
    reach = tn(xbc[:, WIDE + STATE :], (dy * lead_lanes).astype(BF16))
    last = last_by_lane(lead)
    reach_o[0, 0:STATE] = carry[...]
    reach_o[0, STATE : STATE + 8] = decay[...]
    carry[...] = last * carry[...] + reach
    decay[...] = last * decay[...]

    @pl.when(b == 0)
    def _():
        device_o[0:STATE] = carry[...]
        device_o[STATE : STATE + 8] = decay[...]


def intra_back_kernel(
    marks, dy_r, xbc, rows, states, prefix, sums, mixed, cot, skip,
    dxi_o, dbc_o, stats_o, grad_out_o,
):
    b = pl.program_id(0)
    blk = Block(marks, b)

    @pl.when(b == 0)
    def _():
        grad_out_o[...] = jnp.zeros_like(grad_out_o)

    dt = rows[0:8]
    cum = rows[16:24]
    lead = blk.lead(cum)
    root = lax.rsqrt(sums[0:1] / INNER + EPSILON)
    cols = to_columns([cum, lead, jnp.broadcast_to(root, (8, BLOCK))])
    lead_lanes = by_head([column(cols, 1, h) for h in range(HEADS_DEV)])
    rooted = (mixed[...].astype(F32) * column(cols, 2, 0)).astype(BF16)
    grad_out_o[...] += tn(cot[...], rooted)

    dy = dy_r[...]
    x_low = xbc[:, :WIDE]
    b_low = xbc[:, WIDE : WIDE + STATE]
    c_low = xbc[:, WIDE + STATE :]
    entering = states[0, 0:STATE] + states[0, STATE : STATE + 1] * prefix[...]
    held = entering.astype(BF16)
    masks = head_masks().astype(BF16)
    cross = nn(c_low, held)
    lead_grad = nt(masks, (dy * cross).astype(BF16))
    dc = nt((dy * lead_lanes).astype(BF16), held)
    scores = nt(c_low, b_low)
    allowed = blk.allowed()
    ds = jnp.zeros((BLOCK, BLOCK), F32)
    dx = skip[...] * dy
    lane = iota((1, 128), 1)
    row8 = iota((8, 1), 0)
    row_sums = jnp.zeros((BLOCK, 128), F32)
    time_grad = jnp.zeros((8, BLOCK), F32)
    for h in range(HEADS_DEV):
        dt_h = dt[h : h + 1]
        dy_h = of_head(dy, h).astype(BF16)
        decays = decay_of(allowed, column(cols, 0, h), cum[h : h + 1])
        weighted = nt(dy_h, x_low) * decays
        ds = ds + weighted * dt_h
        scored = weighted * scores
        time_grad = time_grad + jnp.where(
            row8 == h, jnp.sum(scored, axis=0, keepdims=True), 0.0
        )
        row_sums = row_sums + jnp.where(
            lane == h, jnp.sum(scored * dt_h, axis=1, keepdims=True), 0.0
        )
        mix = (scores * decays * dt_h).astype(BF16)
        dx = dx + tn(mix, dy_h)
    ds_low = ds.astype(BF16)
    dxi_o[...] = dx
    dbc_o[:, 0:STATE] = tn(ds_low, c_low)
    dbc_o[:, STATE : 2 * STATE] = dc + nn(ds_low, b_low)
    stats_o[0:8] = time_grad
    stats_o[8:16] = row_sums.T[0:8] - time_grad * dt + lead_grad * lead


def input_back_kernel(
    marks, hidden, normed, halo, dz, dxi, dbc, xbc, slope, cin, cin_before, cin_halo,
    rows, stats, states, prefix, reaches, suffix, gain, wg, wv, ws, taps, hcols, since,
    dn_o, wgrad_o, chan_o, step_o, norm_o, spill_o,
    ext, ahead,
):
    s = pl.program_id(0)
    b = pl.num_programs(0) - 1 - s
    blk = Block(marks, b)

    @pl.when(s == 0)
    def _():
        wgrad_o[...] = jnp.zeros_like(wgrad_o)
        chan_o[...] = jnp.zeros_like(chan_o)
        step_o[...] = jnp.zeros_like(step_o)
        norm_o[...] = jnp.zeros_like(norm_o)
        ahead[BLOCK : BLOCK + 8] = jnp.zeros((8, CHAN), F32)

    dt = rows[0:8]
    sig = rows[8:16]
    cum = rows[16:24]
    rate = hcols[1]
    lead = blk.lead(cum)
    tail_base = blk.tail_base(cum)
    tail = tail_base * dt
    cols = to_columns([tail])
    tail_lanes = by_head([column(cols, 0, h) for h in range(HEADS_DEV)])
    entering = states[0, 0:STATE] + states[0, STATE : STATE + 1] * prefix[...]
    leaving = reaches[0, 0:STATE] + reaches[0, STATE : STATE + 1] * suffix[...]
    leaving_low = leaving.astype(BF16)
    x = xbc[:, :WIDE].astype(F32)
    dpacked = nn(xbc[:, WIDE : WIDE + STATE], leaving_low)
    packed = (x * tail_lanes).astype(BF16)
    masks = head_masks()
    tail_grad = nt(masks.astype(BF16), (dpacked * x).astype(BF16))
    dx = dxi[...] + dpacked * tail_lanes
    db = dbc[:, 0:STATE] + nt(packed, leaving_low)
    dc = dbc[:, STATE : 2 * STATE]

    tail_term = tail_grad * tail
    state_term = jnp.sum(leaving * entering, axis=0, keepdims=True)
    last_term = jnp.sum(tail_term, axis=1, keepdims=True) + (
        jnp.sum(masks * state_term, axis=1, keepdims=True) * lead[:, BLOCK - 1 : BLOCK]
    )
    dcum = stats[8:16] - tail_term + jnp.where(iota((8, BLOCK), 1) == BLOCK - 1, last_term, 0.0)
    dla = running_sum(dcum, since[...])
    ddt = stats[0:8] + tail_grad * tail_base + dla * rate
    dstep = jnp.where(iota((8, 1), 0) < HEADS_DEV, ddt * sig, 0.0)
    step_o[0:8] += dstep
    step_o[8:16] += dla * dt * rate
    placed = jnp.concatenate(
        [jnp.zeros((64, BLOCK), F32), dstep, jnp.zeros((56, BLOCK), F32)], axis=0
    ).T

    dpre = jnp.concatenate([dx, db, dc], axis=1) * slope[...].astype(F32)
    ext[0:8] = jnp.where(b == 0, cin_halo[...], cin_before[8:16].astype(F32))
    ext[8 : 8 + BLOCK] = cin[...].astype(F32)
    ahead[0:BLOCK] = dpre
    chan_o[4:5] += jnp.sum(dpre, axis=0, keepdims=True)
    chan_o[3:4] += jnp.sum(dpre * ext[8 : 8 + BLOCK], axis=0, keepdims=True)
    din = taps[3:4] * dpre
    reach_back = blk.since_start()
    reach_ahead = blk.until_end()
    for lag in range(1, CONV):
        at = 3 - lag
        chan_o[at : at + 1] += jnp.sum(
            jnp.where(reach_back >= lag, dpre * ext[8 - lag : 8 - lag + BLOCK], 0.0),
            axis=0,
            keepdims=True,
        )
        din = din + taps[at : at + 1] * (
            jnp.where(reach_ahead > lag, ahead[lag : lag + BLOCK], 0.0)
        )
    ahead[BLOCK : BLOCK + 8] = dpre[0:8]

    dz_low = dz[...]
    dv_low = jnp.concatenate([din[:, 0:128], din[:, 128:256] + placed], axis=1).astype(BF16)
    ds_low = din[:, WIDE:].astype(BF16)
    dn = nt(dz_low, wg[...]) + nt(dv_low, wv[...]) + nt(ds_low, ws[...])
    dn_o[...] = dn.astype(BF16)
    wgrad_o[...] += tn(normed[...], jnp.concatenate([dz_low, dv_low, ds_low], axis=1))

    def unit_of(rows_in):
        rows_in = rows_in.astype(F32)
        return rows_in * lax.rsqrt(jnp.mean(rows_in * rows_in, axis=1, keepdims=True) + EPSILON)

    norm_o[0:1] += jnp.sum(dn * unit_of(hidden[...]), axis=0, keepdims=True)

    @pl.when(b == 0)
    def _():
        ahead[0:8] = jnp.zeros((8, CHAN), F32)
        ahead[8:16] = dpre[0:8]
        ahead[16:24] = jnp.zeros((8, CHAN), F32)
        pos = blk.start - 8 + iota((8, 1), 0)
        left = end_of(marks, pos) - pos
        back = jnp.zeros((8, CHAN), F32)
        for lag in range(1, CONV):
            same = (left > lag) & (pos >= 0)
            back = back + taps[3 - lag : 4 - lag] * (
                ahead[lag : lag + 8] * jnp.where(same, 1.0, 0.0)
            )
        low = jnp.concatenate([jnp.zeros((8, CHAN), F32), back], axis=0).astype(BF16)
        given = nt(low[:, :WIDE], wv[...]) + nt(low[:, WIDE:], ws[...])
        spill_o[...] = given[8:16]
        unit_halo = unit_of(halo[...])
        norm_o[0:1] += jnp.sum(given[8:16] * unit_halo[8:16], axis=0, keepdims=True)
        wgrad_o[:, WIDE:] += tn((unit_halo * gain[...]).astype(BF16), low)


def passed_along(values, axis, by):
    count = lax.axis_size(axis)
    pairs = [(i, i + by) for i in range(count) if 0 <= i + by < count]
    return lax.ppermute(values, axis, pairs)


def handed_to_all(values, axis):
    count = lax.axis_size(axis)
    return lax.all_to_all(
        jnp.broadcast_to(values[None], (count,) + values.shape), axis, 0, 0, tiled=False
    )


def carried(device, sign):
    one, two, three = (passed_along(device, "context", sign * k) for k in (1, 2, 3))

    def join(near, far):
        return near[:STATE] + near[STATE : STATE + 1] * far

    return join(one, join(two, three[:STATE]))


def padded(values, width):
    extra = width - values.shape[-1]
    return jnp.pad(values, [(0, 0)] * (values.ndim - 1) + [(0, extra)])


def body(
    hidden, cotangent, lengths, norm_gain, gate_proj, value_proj, state_proj, step_proj,
    conv_value, conv_state, value_bias, state_bias, step_bias, decay_log, skip_gain,
    mixer_gain, out_proj,
):
    tok = hidden.shape[0]
    blocks = tok // BLOCK
    ctx = lax.axis_index("context")
    rank = lax.axis_index("tensor")
    finishes = jnp.cumsum(lengths[0])
    marks = jnp.concatenate([finishes, (ctx * tok)[None], jnp.zeros((3,), jnp.int32)])
    marks = marks.astype(jnp.int32)

    own_rows = state_proj.shape[0]
    low = state_proj.astype(BF16)
    conv_own = jnp.concatenate([conv_state, state_bias[None]], axis=0)
    top = lax.reduce_precision(conv_own, 8, 7)
    mid = lax.reduce_precision(conv_own - top, 8, 7)
    bot = conv_own - top - mid
    spread = jnp.concatenate([top, mid, bot, jnp.zeros((1, low.shape[1]), F32)], axis=0)
    first = jnp.concatenate([low, spread.astype(BF16)], axis=0)
    first = handed_to_all(first, "tensor").transpose(1, 0, 2).reshape(own_rows + 16, 2 * STATE)
    parts = first[own_rows : own_rows + 15].astype(F32).reshape(3, 5, 2 * STATE)
    conv_shared = parts[0] + parts[1] + parts[2]
    weights = jnp.concatenate(
        [
            value_proj, step_proj, jnp.zeros((own_rows, 61), BF16), first[:own_rows],
            padded(gate_proj, WIDE), padded(out_proj.T, WIDE),
        ],
        axis=1,
    )
    weights = handed_to_all(weights, CELLS).reshape(MODEL, 4 * WIDE)
    wv, ws, wg, wo_t = (weights[:, k * WIDE : (k + 1) * WIDE] for k in range(4))
    place = jnp.arange(BLOCK, dtype=jnp.int32)
    upto = (place[:, None] <= place[None, :]).astype(BF16)

    taps = jnp.concatenate([padded(conv_value, WIDE), conv_shared[:4]], axis=1)
    cbias = jnp.concatenate([padded(value_bias[None], WIDE), conv_shared[4:5]], axis=1)
    rates = -jnp.exp(decay_log)
    hcols = jnp.stack([padded(step_bias, 8), padded(rates, 8)])[:, :, None]
    skip = padded(jnp.repeat(skip_gain, HEADDIM)[None], WIDE)
    mgain = padded(mixer_gain[None], WIDE)
    gain = norm_gain[None]
    halo = passed_along(hidden[tok - 16 :], "context", 1)

    def up(dims):
        return pl.BlockSpec(dims, lambda s: (s,) + (0,) * (len(dims) - 1))

    def up_rows(count):
        return pl.BlockSpec((count, BLOCK), lambda s: (0, s))

    def down(dims):
        return pl.BlockSpec(dims, lambda s: (blocks - 1 - s,) + (0,) * (len(dims) - 1))

    def down_rows(count):
        return pl.BlockSpec((count, BLOCK), lambda s: (0, blocks - 1 - s))

    state_dims = (STATE + 8, WIDE)
    one_state = (1,) + state_dims
    all_states = (blocks,) + state_dims
    normed, xbc, slope, cin, cin_halo, rows, states, device = call(
        project_kernel,
        blocks,
        [
            SMEM, up((BLOCK, MODEL)), whole((16, MODEL)), whole((1, MODEL)),
            whole((MODEL, WIDE)), whole((MODEL, WIDE)), whole((4, CHAN)), whole((1, CHAN)),
            whole((2, 8, 1)), whole((BLOCK, BLOCK)),
        ],
        [
            up((BLOCK, MODEL)), up((BLOCK, CHAN)), up((BLOCK, CHAN)), up((BLOCK, CHAN)),
            whole((8, CHAN)), up_rows(24), up(one_state), whole(state_dims),
        ],
        [
            shape((tok, MODEL), BF16), shape((tok, CHAN), BF16), shape((tok, CHAN), BF16),
            shape((tok, CHAN), BF16), shape((8, CHAN)),
            shape((24, tok)), shape(all_states), shape(state_dims),
        ],
        [pltpu.VMEM((BLOCK + 8, CHAN), F32), pltpu.VMEM((STATE, WIDE), F32), pltpu.VMEM((8, WIDE), F32)],
        2 * tok * MODEL * CHAN + 2 * tok * STATE * WIDE,
        14 * 1024 * 1024,
        marks, hidden, halo, gain, wv, ws, taps, cbias, hcols, upto,
    )
    prefix = carried(device, 1)
    z, e, yi = call(
        intra_kernel,
        blocks,
        [
            SMEM, up((BLOCK, MODEL)), up((BLOCK, MODEL)), whole((MODEL, WIDE)),
            whole((MODEL, WIDE)), up((BLOCK, CHAN)), up_rows(24), whole((1, WIDE)),
        ],
        [up((BLOCK, WIDE))] * 3,
        [shape((tok, WIDE))] * 3,
        [],
        4 * tok * MODEL * WIDE + 8 * tok * BLOCK * WIDE,
        14 * 1024 * 1024,
        marks, normed, cotangent, wg, wo_t, xbc, rows, skip,
    )
    y, mixed, part, sums = call(
        gated_kernel,
        blocks,
        [
            SMEM, up((BLOCK, WIDE)), up((BLOCK, WIDE)), up((BLOCK, WIDE)), up((BLOCK, CHAN)),
            up_rows(24), up(one_state), whole((STATE, WIDE)), whole((1, WIDE)),
            whole((MODEL, WIDE)),
        ],
        [up((BLOCK, WIDE)), up((BLOCK, WIDE)), up((BLOCK, MODEL)), up_rows(8)],
        [shape((tok, WIDE)), shape((tok, WIDE), BF16), shape((tok, MODEL), BF16), shape((8, tok))],
        [],
        2 * tok * MODEL * WIDE + 2 * tok * STATE * WIDE,
        14 * 1024 * 1024,
        marks, yi, z, e, xbc, rows, states, prefix, mgain, wo_t,
    )
    sums = jnp.sum(handed_to_all(sums[:2].reshape(32, 128), "tensor"), axis=0).reshape(2, tok)

    own = tok // lax.axis_size("tensor")
    place = rank * own
    own_hidden = lax.dynamic_slice_in_dim(hidden, place, own, 0).astype(F32)
    own_cot = lax.dynamic_slice_in_dim(cotangent, place, own, 0).astype(F32)
    own_root = lax.rsqrt(lax.dynamic_slice_in_dim(sums[0], place, own, 0) / INNER + EPSILON)
    projected = lax.psum_scatter(part, "tensor", scatter_dimension=0, tiled=True).astype(F32)
    own_out = (own_hidden + own_root[:, None] * projected).astype(BF16)

    dy, dz, reaches, back_device, gains = call(
        gate_back_kernel,
        blocks,
        [
            SMEM, down((BLOCK, WIDE)), down((BLOCK, WIDE)), down((BLOCK, WIDE)),
            down((BLOCK, CHAN)), down_rows(24), down_rows(2), whole((1, WIDE)),
        ],
        [
            down((BLOCK, WIDE)), down((BLOCK, WIDE)), down(one_state), whole(state_dims),
            whole((8, WIDE)),
        ],
        [
            shape((tok, WIDE)), shape((tok, WIDE), BF16), shape(all_states), shape(state_dims),
            shape((8, WIDE)),
        ],
        [pltpu.VMEM((STATE, WIDE), F32), pltpu.VMEM((8, WIDE), F32)],
        2 * tok * STATE * WIDE,
        14 * 1024 * 1024,
        marks, y, z, e, xbc, rows, sums, mgain,
    )
    suffix = carried(back_device, -1)
    dxi, dbc, stats, grad_out_t = call(
        intra_back_kernel,
        blocks,
        [
            SMEM, up((BLOCK, WIDE)), up((BLOCK, CHAN)), up_rows(24), up(one_state),
            whole((STATE, WIDE)), up_rows(2), up((BLOCK, WIDE)), up((BLOCK, MODEL)),
            whole((1, WIDE)),
        ],
        [up((BLOCK, WIDE)), up((BLOCK, WIDE)), up_rows(16), whole((MODEL, WIDE))],
        [shape((tok, WIDE)), shape((tok, WIDE)), shape((16, tok)), shape((MODEL, WIDE))],
        [],
        2 * tok * MODEL * WIDE + 16 * tok * BLOCK * WIDE,
        14 * 1024 * 1024,
        marks, dy, xbc, rows, states, prefix, sums, mixed, cotangent, skip,
    )
    dxi, own_out = lax.optimization_barrier((dxi, own_out))
    output = lax.all_gather(own_out, "tensor", axis=0, tiled=True)
    before = pl.BlockSpec(
        (16, CHAN), lambda s: (jnp.maximum((blocks - 1 - s) * (BLOCK // 16) - 1, 0), 0)
    )
    dn, wgrad, chan, step_rows, norm_part, spill = call(
        input_back_kernel,
        blocks,
        [
            SMEM, down((BLOCK, MODEL)), down((BLOCK, MODEL)), whole((16, MODEL)),
            down((BLOCK, WIDE)), down((BLOCK, WIDE)), down((BLOCK, WIDE)), down((BLOCK, CHAN)),
            down((BLOCK, CHAN)), down((BLOCK, CHAN)), before, whole((8, CHAN)), down_rows(24),
            down_rows(16), down(one_state), whole((STATE, WIDE)), down(one_state),
            whole((STATE, WIDE)), whole((1, MODEL)), whole((MODEL, WIDE)), whole((MODEL, WIDE)),
            whole((MODEL, WIDE)), whole((4, CHAN)), whole((2, 8, 1)), whole((BLOCK, BLOCK)),
        ],
        [
            down((BLOCK, MODEL)), whole((MODEL, 3 * WIDE)), whole((8, CHAN)), whole((16, BLOCK)),
            whole((8, MODEL)), whole((8, MODEL)),
        ],
        [
            shape((tok, MODEL), BF16), shape((MODEL, 3 * WIDE)), shape((8, CHAN)),
            shape((16, BLOCK)), shape((8, MODEL)), shape((8, MODEL)),
        ],
        [pltpu.VMEM((BLOCK + 8, CHAN), F32), pltpu.VMEM((BLOCK + 8, CHAN), F32)],
        12 * tok * MODEL * WIDE,
        24 * 1024 * 1024,
        marks, hidden, normed, halo, dz, dxi, dbc, xbc, slope, cin, cin, cin_halo,
        rows, stats, states, prefix, reaches, suffix, gain, wg, wv, ws, taps, hcols, upto.T,
    )
    arrived = passed_along(spill, "context", -1)
    end = dn[tok - 8 :].astype(F32) + arrived
    dn = lax.dynamic_update_slice(dn, end.astype(BF16), (tok - 8, 0))
    dn, output = lax.optimization_barrier((dn, output))
    own_dn = lax.psum_scatter(dn, "tensor", scatter_dimension=0, tiled=True)
    big = jnp.concatenate([wgrad, grad_out_t], axis=1).astype(BF16).reshape(-1, own_rows, 4 * WIDE)
    big = jnp.sum(lax.all_to_all(big, CELLS, 0, 0, tiled=False).astype(F32), axis=0)
    head_sums = jnp.sum(step_rows, axis=1)
    skip_sums = jnp.sum(gains[1, :INNER_DEV].reshape(HEADS_DEV, HEADDIM), axis=1)
    small = jnp.concatenate(
        [
            chan[:5].reshape(-1),
            norm_part[0],
            gains[0],
            head_sums,
            padded(skip_sums, 8),
            jnp.zeros((1000,), F32),
        ]
    ).reshape(36, 128)
    small = jnp.sum(handed_to_all(small, CELLS), axis=0).reshape(-1)
    own_dn, big, small = lax.optimization_barrier((own_dn, big, small))

    scaling = lax.rsqrt(jnp.mean(own_hidden * own_hidden, axis=1, keepdims=True) + EPSILON)
    unit = own_hidden * scaling
    own_dn = own_dn.astype(F32)
    scaled = own_dn * norm_gain[None]
    own_grad = own_cot + scaling * (
        scaled - unit * jnp.mean(scaled * unit, axis=1, keepdims=True)
    )
    grad_hidden = lax.all_gather(own_grad.astype(BF16), "tensor", axis=0, tiled=True)

    chan = small[: 5 * CHAN].reshape(5, CHAN)
    at = 5 * CHAN
    norm_cells = small[at : at + MODEL]
    at += MODEL
    grad_mixer = small[at : at + INNER_DEV]
    at += WIDE
    grad_step_bias = small[at : at + HEADS_DEV]
    grad_decay = small[at + 8 : at + 8 + HEADS_DEV]
    grad_skip = small[at + 16 : at + 16 + HEADS_DEV]
    share = 2 * STATE // lax.axis_size("tensor")
    shared = jnp.concatenate([big[:, 2 * WIDE : 3 * WIDE], chan[:, WIDE:]], axis=0)
    shared = shared.reshape(own_rows + 5, -1, share).transpose(1, 0, 2)
    shared = shared.reshape(shared.shape[0], -1)
    count = shared.shape[1]
    final = jnp.concatenate(
        [shared, jnp.broadcast_to(norm_cells[None], (shared.shape[0], MODEL))], axis=1
    )
    final = padded(final, 2560).reshape(-1, 20, 128)
    final = jnp.sum(lax.all_to_all(final, "tensor", 0, 0, tiled=False), axis=0).reshape(-1)
    state_all = final[:count].reshape(own_rows + 5, share)
    return (
        output,
        grad_hidden,
        final[count : count + MODEL],
        big[:, :INNER_DEV],
        big[:, WIDE : WIDE + INNER_DEV],
        state_all[:own_rows],
        big[:, WIDE + INNER_DEV : WIDE + INNER_DEV + HEADS_DEV],
        chan[:4, :INNER_DEV],
        state_all[own_rows : own_rows + 4],
        chan[4, :INNER_DEV],
        state_all[own_rows + 4],
        grad_step_bias,
        grad_decay,
        grad_skip,
        grad_mixer,
        big[:, 3 * WIDE : 3 * WIDE + INNER_DEV].T,
    )


def solution(mesh):
    cells = P(CELLS, None)
    split = P(CELLS, "tensor")
    return jax.shard_map(
        body,
        mesh=mesh,
        in_specs=(
            cells, cells, P("shard", None), P(), split, split, split, split, P(None, "tensor"),
            P(None, "tensor"), P("tensor"), P("tensor"), P("tensor"), P("tensor"), P("tensor"),
            P("tensor"), P("tensor", CELLS),
        ),
        out_specs=(
            cells, cells, P(), split, split, split, split, P(None, "tensor"), P(None, "tensor"),
            P("tensor"), P("tensor"), P("tensor"), P("tensor"), P("tensor"), P("tensor"),
            P("tensor", CELLS),
        ),
        check_vma=False,
    )
```

time: 1080 us -> 267 us (0.25)
  waiting for transfers between devices: 351 us -> 78.7 us
  blocking collectives: 271 us -> 0 us
  matrix products: 150 us -> 0 us
  other arithmetic: 160 us -> 15.7 us
  Pallas kernels: 0 us -> 77.7 us
  local copies, waits for them, and re-layouts: 111 us -> 34.1 us
  starting transfers between devices: 3.7 us -> 42.4 us
    reduce_scatter x4 -> x2, waiting for transfers between devices: 229 us -> 0.05 us  [the longest x1 0.03 us: body(): lax.psum_scatter(part, 'tensor', scatter_dimension=0, tiled=True)]
    dot_general x119 -> x0, matrix products: 150 us -> none  [the longest x8 18.7 us: block_backward(): jnp.einsum('hij,ihp->jhp', mixing.astype(jnp.float32), d_out, precision=H...]
    all_gather x7 -> x0, blocking collectives: 149 us -> none  [the longest x2 29.5 us: carried_in(): gathered = jax.tree.map(lambda a: lax.all_gather(a, axis), part)]
    psum x4 -> x0, blocking collectives: 113 us -> none  [the longest x1 74.5 us: body(): lax.psum((grad_norm, grad_taps[:, :inner_local], grad_taps[:, inner_local...]
    psum x2 -> x0, waiting for transfers between devices: 83.8 us -> none  [the longest x1 83.8 us: body(): normed_grad = lax.psum(normed_part, 'tensor')]
    pallas_call x0 -> x6, Pallas kernels: none -> 77.7 us  [call(): pl.pallas_call(kernel, grid=(grid,), in_specs=in_specs, out_specs=out_spe...]
    all_to_all x0 -> x6, waiting for transfers between devices: none -> 56.5 us  [the longest x4 34.6 us: handed_to_all(): lax.all_to_all(jnp.broadcast_to(values[None], (count,) + values.shape), a...]
    another operation x52 -> x4, other arithmetic: 54.7 us -> 1.05 us
  transfers between devices with their start and end apart: 10 -> 18, of which waited for: 7 -> 9; matrix products, arithmetic and copies ran while one was open for 10% -> 13% of each run, Pallas kernels for 0% -> 21%
where the time goes in v1:
time: 267 us; the launch traced here: 263 us
  waiting for transfers between devices  78.7 us (29%)
  Pallas kernels  77.7 us (29%)
  starting transfers between devices  42.4 us (16%)
  local copies, waits for them, and re-layouts  34.1 us (13%)
  other arithmetic  15.7 us (6%)
  between operations  14.3 us (5%)
    pallas_call x6, Pallas kernels, call(): pl.pallas_call(kernel, grid=(grid,), in_specs=in_specs, out_specs=out_spe...  77.7 us
    all_to_all x4, waiting for transfers between devices, handed_to_all(): lax.all_to_all(jnp.broadcast_to(values[None], (count,) + values.shape), a...  34.6 us
    all_to_all x1, waiting for transfers between devices, body(): lax.all_to_all(big, CELLS, 0, 0, tiled=False).astype(F32)  20.4 us
    all_to_all x4, starting transfers between devices, handed_to_all(): lax.all_to_all(jnp.broadcast_to(values[None], (count,) + values.shape), a...  20.2 us
    ppermute x8, starting transfers between devices, passed_along(): return lax.ppermute(values, axis, pairs)  14.9 us
    ppermute x8, waiting for transfers between devices, passed_along(): return lax.ppermute(values, axis, pairs)  12.3 us
    all_gather x1, waiting for transfers between devices, body(): lax.all_gather(own_grad.astype(BF16), 'tensor', axis=0, tiled=True)  9.79 us
    unnamed x38, local copies, waits for them, and re-layouts  8.32 us
  transfers between devices with their start and end apart: 18, of which 9 were waited for; matrix products, arithmetic and copies ran while one was open for 13% of the time, Pallas kernels for 21%

profile of v1, /device:TPU:0, one launch (start us, length us, event | category | flops | bytes accessed | tf_op | source)
XLA Modules:
  0.0 262.9 jit_solution(14270966702486152729)
XLA Ops:
  7.2 0.7 fusion.18
  8.2 0.8 concatenate.41
  9.0 0.7 reshape.174
  9.7 4.6 %all-to-all-start = ((bf16[8,2,1024]{2,1,0:T(2,128)(2,1)}), bf16[8,2,1024]{2,1,0:T(2,128)(2,1)S(1)}, u32[]{:S(2)}, u32[]{:S(2)}) async-start(bf16[8,2,1024]{2,1,0:T(2,128)(2,1)} %reshape.174), calls=%async_computation | async-start | bytes 65536 | tf_op jit(solution)/shard_map/all_to_all | solution.py:494
  14.3 0.7 slice.185
  15.0 3.8 %collective-permute-start = (bf16[16,768]{1,0:T(8,128)(2,1)S(1)}, bf16[16,768]{1,0:T(8,128)(2,1)S(1)}, u32[]{:S(2)}, u32[]{:S(2)}) collective-permute-start(bf16[16,768]{1,0:T(8,128)(2,1)S(1)} %slice.185), channel_id=1, source_target_pairs={{0,8},{8,16},{16,24},{1,9},{9,17},{17,25},{2,10},{10,18},{18,26},{... | collective-permute-start | bytes 73736 | tf_op jit(solution)/shard_map/ppermute | solution.py:489
  18.9 0.7 broadcast_in_dim.77
  19.7 1.2 pad.42.mgain
  21.5 1.3 broadcast_in_dim.69.gain
  22.8 0.8 copy.110
  23.5 0.7 pad.35
  24.3 0.7 pad.36
  25.3 0.8 concatenate.42
  26.1 1.3 broadcast_in_dim.74
  27.5 7.6 %all-to-all-start.1 = ((bf16[16,48,1024]{2,1,0:T(8,128)(2,1)}), bf16[16,48,1024]{2,1,0:T(8,128)(2,1)S(1)}, u32[]{:S(2)}, u32[]{:S(2)}) async-start(bf16[16,48,1024]{2,1,0:T(8,128)(2,1)} %broadcast_in_dim.74), calls=%async_computation.1 | async-start | bytes 3145728 | tf_op jit(solution)/shard_map/all_to_all | solution.py:494
  35.1 0.7 copy.112.hcols
  36.6 0.7 fusion.9.upto
  39.0 20.5 %all-to-all-done.1 = bf16[16,48,1024]{2,1,0:T(8,128)(2,1)S(1)} async-done(((bf16[16,48,1024]{2,1,0:T(8,128)(2,1)}), bf16[16,48,1024]{2,1,0:T(8,128)(2,1)S(1)}, u32[]{:S(2)}, u32[]{:S(2)}) %all-to-all-start.1) | async-done | bytes 1572896 | tf_op jit(solution)/shard_map/all_to_all | solution.py:494
  59.5 1.3 fusion.20
  61.4 13.4 %shard_map.288 = (bf16[2048,768]{1,0:T(8,128)(2,1)}, bf16[2048,512]{1,0:T(8,128)(2,1)}, bf16[2048,512]{1,0:T(8,128)(2,1)}, bf16[2048,512]{1,0:T(8,128)(2,1)}, f3...) custom-call(s32[8]{0:T(128)} %pad_add_fusion.marks, ...), custom_call_target="tpu_custom_call" | custom-call | flops 1744830464 | bytes 14680064 | tf_op jit(solution)/shard_map/pallas_call | solution.py:138
  74.9 1.8 collective-permute-start.3
  76.6 1.3 collective-permute-start.2
  77.9 2.8 %collective-permute-start.1 = (f32[136,256]{1,0:T(8,128)}, f32[136,256]{1,0:T(8,128)S(1)}, u32[]{:S(2)}, u32[]{:S(2)}) collective-permute-start(f32[136,256]{1,0:T(8,128)} %get-tuple-element.60), channel_id=1, source_target_pairs={{0,8},{8,16},{16,24},{1,9},{9,17},{17,25},{2,10},{10,18},{18,26},{... | collective-permute-start | bytes 417800 | tf_op jit(solution)/shard_map/ppermute | solution.py:489
  80.7 10.2 %shard_map.289 = (f32[2048,256]{1,0:T(8,128)}, f32[2048,256]{1,0:T(8,128)}, f32[2048,256]{1,0:T(8,128)}) custom-call(s32[8]{0:T(128)} %pad_add_fusion.marks, bf16[2048,768]{1,0:T(8,128)(2,1)} %get-tuple-element.53.normed, bf16[2048,768]{1,0:T(8,128)(2,1)} %cot.3, bf16[768,256]{1,0:T(8,128)(2,1)} %get-tuple-element.205.wg, ...), custom_call_target="tpu_custom_call" | custom-call | flops 2684354560 | bytes 14680064 | tf_op jit(solution)/shard_map/pallas_call | solution.py:138
  91.0 0.7 fusion.16.prefix
  91.6 10.2 %shard_map.290 = (f32[2048,256]{1,0:T(8,128)}, bf16[2048,256]{1,0:T(8,128)(2,1)}, bf16[2048,768]{1,0:T(8,128)(2,1)}, f32[8,2048]{1,0:T(8,128)}) custom-call(s32[8]{0:T(128)} %pad_add_fusion.marks, f32[2048,256]{1,0:T(8,128)} %get-tuple-element.56.yi, f32[2048,256]{1,0:T(8,128)} %get-tuple-element.57.z, f32[2048,256]{1,0:T(8,128)} %get-tuple-element.58.e, ...), custom_call_target="tpu_custom_call" | custom-call | flops 939524096 | bytes 14680064 | tf_op jit(solution)/shard_map/pallas_call | solution.py:138
  101.8 0.8 slice.205
  103.3 4.1 %all-to-all-start.2 = ((f32[8,32,128]{2,1,0:T(8,128)}), f32[8,32,128]{2,1,0:T(8,128)S(1)}, u32[]{:S(2)}, u32[]{:S(2)}) async-start(f32[8,32,128]{2,1,0:T(8,128)} %broadcast_in_dim.80), calls=%async_computation.2 | async-start | bytes 262144 | tf_op jit(solution)/shard_map/all_to_all | solution.py:494
  107.5 6.9 %all-to-all-done.2 = f32[8,32,128]{2,1,0:T(8,128)S(1)} async-done(((f32[8,32,128]{2,1,0:T(8,128)}), f32[8,32,128]{2,1,0:T(8,128)S(1)}, u32[]{:S(2)}, u32[]{:S(2)}) %all-to-all-start.2) | async-done | bytes 131104 | tf_op jit(solution)/shard_map/all_to_all | solution.py:494
  115.0 9.4 %shard_map.291 = (f32[2048,256]{1,0:T(8,128)}, bf16[2048,256]{1,0:T(8,128)(2,1)}, f32[8,136,256]{2,1,0:T(8,128)}, f32[136,256]{1,0:T(8,128)}, f32[8,256]{1,0:T(8,128)}) custom-call(s32[8]{0:T(128)} %pad_add_fusion.marks, f32[2048,256]{1,0:T(8,128)} %get-tuple-element.61.y, f32[2048,256]{1,0:T(8,128)} %get-tuple-element.57.z, ...), custom_call_target="tpu_custom_call" | custom-call | flops 134217728 | bytes 14680064 | tf_op jit(solution)/shard_map/pallas_call | solution.py:138
  124.5 12.9 %shard_map.292 = (f32[2048,256]{1,0:T(8,128)}, f32[2048,256]{1,0:T(8,128)}, f32[16,2048]{1,0:T(8,128)}, f32[768,256]{1,0:T(8,128)}) custom-call(s32[8]{0:T(128)} %pad_add_fusion.marks, f32[2048,256]{1,0:T(8,128)} %get-tuple-element.64.dy_r, bf16[2048,512]{1,0:T(8,128)(2,1)} %get-tuple-element.54.xbc, f32[24,2048]{1,0:T(8,128)} %get-tuple-element.55.rows, ...), custom_call_target="tpu_custom_call" | custom-call | flops 2952790016 | bytes 14680064 | tf_op jit(solution)/shard_map/pallas_call | solution.py:138
  137.4 2.1 fusion.8
  139.6 1.3 collective-permute-start.5
  140.9 1.3 collective-permute-start.4
  142.2 1.3 collective-permute-start.6
  143.5 0.7 fusion.10.since
  144.2 4.2 %collective-permute-done.5 = f32[136,256]{1,0:T(8,128)S(1)} collective-permute-done((f32[136,256]{1,0:T(8,128)S(1)}, f32[136,256]{1,0:T(8,128)S(1)}, u32[]{:S(2)}, u32[]{:S(2)}) %collective-permute-start.5) | collective-permute-done | bytes 139296 | tf_op jit(solution)/shard_map/ppermute | solution.py:489
  148.4 3.5 %collective-permute-done.6 = f32[136,256]{1,0:T(8,128)S(1)} collective-permute-done((f32[136,256]{1,0:T(8,128)S(1)}, f32[136,256]{1,0:T(8,128)S(1)}, u32[]{:S(2)}, u32[]{:S(2)}) %collective-permute-start.6) | collective-permute-done | bytes 139296 | tf_op jit(solution)/shard_map/ppermute | solution.py:489
  151.9 0.7 fusion.13.suffix
  152.5 21.6 %shard_map.293 = (bf16[2048,768]{1,0:T(8,128)(2,1)}, f32[768,768]{1,0:T(8,128)}, f32[8,512]{1,0:T(8,128)}, f32[16,256]{1,0:T(8,128)}, f32[8,768]{1,0:T(8,128)}, /*index=5*/f32[8,768]{1,0:T(8,128)}) custom-call(s32[8]{0:T(128)} %pad_add_fusion.marks, bf16[2048,768]{1,0:T(8,128)(2,1)} %hidden.3, bf16[2048,768]{1,0:T(8,128)(2,1)} %get-tuple-element.53.normed, ...), custom_call_target="tpu_custom_call" | custom-call | flops 4831838208 | bytes 25165824 | tf_op jit(solution)/shard_map/pallas_call | solution.py:138
  174.2 1.4 collective-permute-start.7
  175.7 4.6 %collective-permute-done.7 = f32[8,768]{1,0:T(8,128)S(1)} collective-permute-done((f32[8,768]{1,0:T(8,128)}, f32[8,768]{1,0:T(8,128)S(1)}, u32[]{:S(2)}, u32[]{:S(2)}) %collective-permute-start.7) | collective-permute-done | bytes 24608 | tf_op jit(solution)/shard_map/ppermute | solution.py:489
  180.3 1.3 fusion.17
  181.6 0.8 slice.215
  182.5 0.8 slice_reduce_fusion.2
  183.6 0.8 slice_reduce_fusion.1
  184.5 0.8 broadcast_in_dim.83
  185.2 4.0 %all-to-all-start.4 = ((f32[16,36,128]{2,1,0:T(8,128)}), f32[16,36,128]{2,1,0:T(8,128)S(1)}, u32[]{:S(2)}, u32[]{:S(2)}) async-start(f32[16,36,128]{2,1,0:T(8,128)} %broadcast_in_dim.83), calls=%async_computation.6 | async-start | bytes 655360 | tf_op jit(solution)/shard_map/all_to_all | solution.py:494
  189.4 1.4 pad_maximum_fusion
  190.7 7.3 %all-to-all-done.4 = f32[16,36,128]{2,1,0:T(8,128)S(1)} async-done(((f32[16,36,128]{2,1,0:T(8,128)}), f32[16,36,128]{2,1,0:T(8,128)S(1)}, u32[]{:S(2)}, u32[]{:S(2)}) %all-to-all-start.4) | async-done | bytes 294944 | tf_op jit(solution)/shard_map/all_to_all | solution.py:494
  198.0 3.7 %all-to-all-start.3 = ((bf16[16,48,1024]{2,1,0:T(8,128)(2,1)}), bf16[16,48,1024]{2,1,0:T(8,128)(2,1)S(1)}, u32[]{:S(2)}, u32[]{:S(2)}) async-start(bf16[16,48,1024]{2,1,0:T(8,128)(2,1)} %pad_maximum_fusion), calls=%async_computation.5 | async-start | bytes 3145728 | tf_op jit(solution)/shard_map/all_to_all | solution.py:707
  201.8 20.4 %all-to-all-done.3 = bf16[16,48,1024]{2,1,0:T(8,128)(2,1)S(1)} async-done(((bf16[16,48,1024]{2,1,0:T(8,128)(2,1)}), bf16[16,48,1024]{2,1,0:T(8,128)(2,1)S(1)}, u32[]{:S(2)}, u32[]{:S(2)}) %all-to-all-start.3) | async-done | bytes 1572896 | tf_op jit(solution)/shard_map/all_to_all | solution.py:707
  222.6 1.4 fusion.2
  224.0 2.4 fusion.6
  227.2 0.9 copy.115
  229.1 3.4 %all-to-all-start.5 = ((f32[8,20,128]{2,1,0:T(8,128)}), f32[8,20,128]{2,1,0:T(8,128)S(1)}, u32[]{:S(2)}, u32[]{:S(2)}) async-start(f32[8,20,128]{2,1,0:T(8,128)} %copy.117), calls=%async_computation.7 | async-start | bytes 196608 | tf_op jit(solution)/shard_map/all_to_all | solution.py:750
  232.5 1.5 slice_bitcast_fusion
  236.3 0.8 slice.227
  237.8 1.4 all-to-all-done.5
  241.2 0.7 copy.118
  241.8 9.8 %all-gather.5.cloned.1.call-done = bf16[2048,768]{1,0:T(8,128)(2,1)} async-done(((bf16[256,768]{1,0:T(8,128)(2,1)}), bf16[2048,768]{1,0:T(8,128)(2,1)}) %all-gather.5.cloned.1.call-update) | async-done | bytes 3145744 | tf_op jit(solution)/shard_map/all_gather | solution.py:730
  251.6 1.7 copy.126
  253.3 1.4 copy-done.1
  254.7 1.7 copy.127
  (117 shorter events, 13.5 us)
Async XLA Ops:
  9.7 15.3 %all-to-all-start = ((bf16[8,2,1024]{2,1,0:T(2,128)(2,1)}), bf16[8,2,1024]{2,1,0:T(2,128)(2,1)S(1)}, u32[]{:S(2)}, u32[]{:S(2)}) async-start(bf16[8,2,1024]{2,1,0:T(2,128)(2,1)} %reshape.174), calls=%async_computation | async-start | bytes 65536 | tf_op jit(solution)/shard_map/all_to_all | solution.py:494
  15.0 45.8 %collective-permute-start = (bf16[16,768]{1,0:T(8,128)(2,1)S(1)}, bf16[16,768]{1,0:T(8,128)(2,1)S(1)}, u32[]{:S(2)}, u32[]{:S(2)}) collective-permute-start(bf16[16,768]{1,0:T(8,128)(2,1)S(1)} %slice.185), channel_id=1, source_target_pairs={{0,8},{8,16},{16,24},{1,9},{9,17},{17,25},{2,10},{10,18},{18,26},{... | collective-permute-start | bytes 73736 | tf_op jit(solution)/shard_map/ppermute | solution.py:489
  26.1 9.0 %copy-start.13 = (f32[3]{0:T(128)S(1)}, f32[3]{0:T(128)}, u32[]{:S(2)}) copy-start(f32[3]{0:T(128)} %param.30) | copy-start | bytes 40
  26.1 9.0 %copy-start.11 = (f32[3]{0:T(128)S(1)}, f32[3]{0:T(128)}, u32[]{:S(2)}) copy-start(f32[3]{0:T(128)} %param.29) | copy-start | bytes 40
  26.1 9.7 %copy-start.14 = (s32[1,4]{1,0:T(1,128)S(1)}, s32[1,4]{1,0:T(1,128)}, u32[]{:S(2)}) copy-start(s32[1,4]{1,0:T(1,128)} %param.19) | copy-start | bytes 52
  27.5 10.4 %copy-start.10 = (f32[192]{0:T(256)S(1)}, f32[192]{0:T(256)}, u32[]{:S(2)}) copy-start(f32[192]{0:T(256)} %param.27) | copy-start | bytes 2308
  27.5 11.0 %copy-start.9 = (f32[4,192]{1,0:T(4,128)S(1)}, f32[4,192]{1,0:T(4,128)}, u32[]{:S(2)}) copy-start(f32[4,192]{1,0:T(4,128)} %param.25) | copy-start | bytes 9220
  27.5 32.1 %all-to-all-start.1 = ((bf16[16,48,1024]{2,1,0:T(8,128)(2,1)}), bf16[16,48,1024]{2,1,0:T(8,128)(2,1)S(1)}, u32[]{:S(2)}, u32[]{:S(2)}) async-start(bf16[16,48,1024]{2,1,0:T(8,128)(2,1)} %broadcast_in_dim.74), calls=%async_computation.1 | async-start | bytes 3145728 | tf_op jit(solution)/shard_map/all_to_all | solution.py:494
  35.0 102.4 %reduce-scatter.3.cloned.1.call-start = ((), (), s32[]{:S(2)}) async-start(), calls=%async_computation.8 | async-start | bytes 3538944 | tf_op jit(solution)/shard_map/reduce_scatter | solution.py:632
  60.8 0.6 copy-start.6
  74.9 16.1 %collective-permute-start.3 = (f32[136,256]{1,0:T(8,128)}, f32[136,256]{1,0:T(8,128)S(1)}, u32[]{:S(2)}, u32[]{:S(2)}) collective-permute-start(f32[136,256]{1,0:T(8,128)} %get-tuple-element.60), channel_id=1, source_target_pairs={{0,24},{1,25},{2,26},{3,27},{4,28},{5,29},{6,30},{7,31},{32,56},{3... | collective-permute-start | bytes 417800 | tf_op jit(solution)/shard_map/ppermute | solution.py:489
  76.6 14.3 %collective-permute-start.2 = (f32[136,256]{1,0:T(8,128)}, f32[136,256]{1,0:T(8,128)S(1)}, u32[]{:S(2)}, u32[]{:S(2)}) collective-permute-start(f32[136,256]{1,0:T(8,128)} %get-tuple-element.60), channel_id=1, source_target_pairs={{0,16},{8,24},{1,17},{9,25},{2,18},{10,26},{3,19},{11,27},{4,20},{... | collective-permute-start | bytes 417800 | tf_op jit(solution)/shard_map/ppermute | solution.py:489
  77.9 13.0 %collective-permute-start.1 = (f32[136,256]{1,0:T(8,128)}, f32[136,256]{1,0:T(8,128)S(1)}, u32[]{:S(2)}, u32[]{:S(2)}) collective-permute-start(f32[136,256]{1,0:T(8,128)} %get-tuple-element.60), channel_id=1, source_target_pairs={{0,8},{8,16},{16,24},{1,9},{9,17},{17,25},{2,10},{10,18},{18,26},{... | collective-permute-start | bytes 417800 | tf_op jit(solution)/shard_map/ppermute | solution.py:489
  103.3 11.0 %all-to-all-start.2 = ((f32[8,32,128]{2,1,0:T(8,128)}), f32[8,32,128]{2,1,0:T(8,128)S(1)}, u32[]{:S(2)}, u32[]{:S(2)}) async-start(f32[8,32,128]{2,1,0:T(8,128)} %broadcast_in_dim.80), calls=%async_computation.2 | async-start | bytes 262144 | tf_op jit(solution)/shard_map/all_to_all | solution.py:494
  107.5 74.1 %all-gather.3.cloned.1.call-start = ((), (), s32[]{:S(2)}) async-start(), calls=%async_computation.9 | async-start | bytes 3538944 | tf_op jit(solution)/shard_map/all_gather | solution.py:672
  124.5 15.1 %copy-start.12 = (f32[136,256]{1,0:T(8,128)S(1)}, f32[136,256]{1,0:T(8,128)}, u32[]{:S(2)}) copy-start(f32[136,256]{1,0:T(8,128)} %get-tuple-element.75) | copy-start | bytes 417796
  139.5 83.0 %reduce-scatter.5.cloned.1.call-start = ((), (), s32[]{:S(2)}) async-start(), calls=%async_computation.10 | async-start | bytes 3538944 | tf_op jit(solution)/shard_map/reduce_scatter | solution.py:705
  139.6 8.8 %collective-permute-start.5 = (f32[136,256]{1,0:T(8,128)S(1)}, f32[136,256]{1,0:T(8,128)S(1)}, u32[]{:S(2)}, u32[]{:S(2)}) collective-permute-start(f32[136,256]{1,0:T(8,128)S(1)} %copy-done.12), channel_id=1, source_target_pairs={{16,0},{24,8},{17,1},{25,9},{18,2},{26,10},{19,3},{27,11},{20,4},{... | collective-permute-start | bytes 417800 | tf_op jit(solution)/shard_map/ppermute | solution.py:489
  140.9 7.5 %collective-permute-start.4 = (f32[136,256]{1,0:T(8,128)S(1)}, f32[136,256]{1,0:T(8,128)S(1)}, u32[]{:S(2)}, u32[]{:S(2)}) collective-permute-start(f32[136,256]{1,0:T(8,128)S(1)} %copy-done.12), channel_id=1, source_target_pairs={{8,0},{16,8},{24,16},{9,1},{17,9},{25,17},{10,2},{18,10},{26,18},{... | collective-permute-start | bytes 417800 | tf_op jit(solution)/shard_map/ppermute | solution.py:489
  142.2 9.7 %collective-permute-start.6 = (f32[136,256]{1,0:T(8,128)S(1)}, f32[136,256]{1,0:T(8,128)S(1)}, u32[]{:S(2)}, u32[]{:S(2)}) collective-permute-start(f32[136,256]{1,0:T(8,128)S(1)} %copy-done.12), channel_id=1, source_target_pairs={{24,0},{25,1},{26,2},{27,3},{28,4},{29,5},{30,6},{31,7},{56,32},{5... | collective-permute-start | bytes 417800 | tf_op jit(solution)/shard_map/ppermute | solution.py:489
  174.2 9.3 %copy-start.8 = (f32[16,256]{1,0:T(8,128)S(1)}, f32[16,256]{1,0:T(8,128)}, u32[]{:S(2)}) copy-start(f32[16,256]{1,0:T(8,128)} %get-tuple-element.86) | copy-start | bytes 49156
  174.2 9.4 %copy-start.7 = (f32[8,512]{1,0:T(8,128)S(1)}, f32[8,512]{1,0:T(8,128)}, u32[]{:S(2)}) copy-start(f32[8,512]{1,0:T(8,128)} %get-tuple-element.83) | copy-start | bytes 49156
  174.2 6.1 %collective-permute-start.7 = (f32[8,768]{1,0:T(8,128)}, f32[8,768]{1,0:T(8,128)S(1)}, u32[]{:S(2)}, u32[]{:S(2)}) collective-permute-start(f32[8,768]{1,0:T(8,128)} %get-tuple-element.77), channel_id=1, source_target_pairs={{8,0},{16,8},{24,16},{9,1},{17,9},{25,17},{10,2},{18,10},{26,18},{... | collective-permute-start | bytes 73736 | tf_op jit(solution)/shard_map/ppermute | solution.py:489
  181.6 7.6 %copy-start.4 = (f32[768,256]{1,0:T(8,128)S(1)}, f32[768,256]{1,0:T(8,128)}, u32[]{:S(2)}) copy-start(f32[768,256]{1,0:T(8,128)} %get-tuple-element.82) | copy-start | bytes 2359300
  181.6 7.7 %copy-start.2 = (f32[768,768]{1,0:T(8,128)S(1)}, f32[768,768]{1,0:T(8,128)}, u32[]{:S(2)}) copy-start(f32[768,768]{1,0:T(8,128)} %get-tuple-element.81) | copy-start | bytes 7077892
  185.2 12.8 %all-to-all-start.4 = ((f32[16,36,128]{2,1,0:T(8,128)}), f32[16,36,128]{2,1,0:T(8,128)S(1)}, u32[]{:S(2)}, u32[]{:S(2)}) async-start(f32[16,36,128]{2,1,0:T(8,128)} %broadcast_in_dim.83), calls=%async_computation.6 | async-start | bytes 655360 | tf_op jit(solution)/shard_map/all_to_all | solution.py:494
  190.7 31.8 %copy-start.5 = (f32[768]{0:T(1024)S(1)}, f32[768]{0:T(1024)}, u32[]{:S(2)}) copy-start(f32[768]{0:T(1024)} %param.20) | copy-start | bytes 9220
  198.0 24.2 %all-to-all-start.3 = ((bf16[16,48,1024]{2,1,0:T(8,128)(2,1)}), bf16[16,48,1024]{2,1,0:T(8,128)(2,1)S(1)}, u32[]{:S(2)}, u32[]{:S(2)}) async-start(bf16[16,48,1024]{2,1,0:T(8,128)(2,1)} %pad_maximum_fusion), calls=%async_computation.5 | async-start | bytes 3145728 | tf_op jit(solution)/shard_map/all_to_all | solution.py:707
  201.7 49.9 %all-gather.5.cloned.1.call-start = ((), (), s32[]{:S(2)}) async-start(), calls=%async_computation.11 | async-start | bytes 3538944 | tf_op jit(solution)/shard_map/all_gather | solution.py:730
  222.5 5.5 %copy-start.3 = (f32[48,1024]{1,0:T(8,128)}, f32[48,1024]{1,0:T(8,128)S(1)}, u32[]{:S(2)}) copy-start(f32[48,1024]{1,0:T(8,128)S(1)} %convert_reduce_fusion) | copy-start | bytes 589828
  224.0 27.6 %copy-start = (bf16[2048,768]{1,0:T(8,128)(2,1)S(1)}, bf16[2048,768]{1,0:T(8,128)(2,1)}, u32[]{:S(2)}) copy-start(bf16[2048,768]{1,0:T(8,128)(2,1)} %all-gather.3.cloned.1.call-done) | copy-start | bytes 9437188
  229.1 10.1 %all-to-all-start.5 = ((f32[8,20,128]{2,1,0:T(8,128)}), f32[8,20,128]{2,1,0:T(8,128)S(1)}, u32[]{:S(2)}, u32[]{:S(2)}) async-start(f32[8,20,128]{2,1,0:T(8,128)} %copy.117), calls=%async_computation.7 | async-start | bytes 196608 | tf_op jit(solution)/shard_map/all_to_all | solution.py:750
  251.6 3.0 %copy-start.1 = (bf16[2048,768]{1,0:T(8,128)(2,1)S(1)}, bf16[2048,768]{1,0:T(8,128)(2,1)}, u32[]{:S(2)}) copy-start(bf16[2048,768]{1,0:T(8,128)(2,1)} %all-gather.5.cloned.1.call-done) | copy-start | bytes 9437188
Sparse Core Ops, SparseCore 0:
  101.9 35.4 reduce-scatter.2
  139.7 25.0 all-gather.2
  181.7 32.5 reduce-scatter.4
  226.6 24.9 all-gather.4

commit v2 on v1

v2 whole, which is shorter than its diff:
```python
import jax
import jax.numpy as jnp
from jax import lax
from jax.experimental import pallas as pl
from jax.experimental.pallas import tpu as pltpu
from jax.sharding import PartitionSpec as P

MODEL = 768
INNER = 1536
HEADDIM = 64
STATE = 128
CONV = 4
BLOCK = 256
HEADS_DEV = 3
INNER_DEV = 192
WIDE = 256
CHAN = 512
EPSILON = 1e-05
F32 = jnp.float32
BF16 = jnp.bfloat16
CELLS = ("shard", "context")
VMEM_LIMIT = 60 * 1024 * 1024
PARTS = (2, 2, 2, 2, 1, 2)


def nn(a, b):
    return lax.dot_general(a, b, (((1,), (0,)), ((), ())), preferred_element_type=F32)


def nt(a, b):
    return lax.dot_general(a, b, (((1,), (1,)), ((), ())), preferred_element_type=F32)


def tn(a, b):
    return lax.dot_general(a, b, (((0,), (0,)), ((), ())), preferred_element_type=F32)


def iota(shape, dim):
    return lax.broadcasted_iota(jnp.int32, shape, dim)


def start_of(marks, pos):
    start = jnp.zeros_like(pos)
    for k in range(3):
        start = jnp.where(pos >= marks[k], marks[k], start)
    return start


def end_of(marks, pos):
    end = jnp.full_like(pos, marks[3])
    for k in (2, 1, 0):
        end = jnp.where(pos < marks[k], marks[k], end)
    return end


def running_sum(rows, ones):
    top = rows.astype(BF16)
    rest = rows - top.astype(F32)
    mid = rest.astype(BF16)
    low = (rest - mid.astype(F32)).astype(BF16)
    pieces = [top.astype(F32), mid.astype(F32), low.astype(F32), jnp.zeros((8, BLOCK), F32)]
    sums = nn(jnp.concatenate(pieces, axis=0).astype(BF16), ones)
    return sums[0:8] + sums[8:16] + sums[16:24]


def by_head(cols, width=WIDE):
    lane = iota((1, width), 1)
    return jnp.where(
        lane < HEADDIM,
        cols[0],
        jnp.where(lane < 2 * HEADDIM, cols[1], jnp.where(lane < 3 * HEADDIM, cols[2], 0.0)),
    )


def head_masks():
    row = iota((8, WIDE), 0)
    lane = iota((8, WIDE), 1)
    low = row * HEADDIM
    return jnp.where((lane >= low) & (lane < low + HEADDIM) & (row < HEADS_DEV), 1.0, 0.0)


def of_head(values, h):
    lane = iota((1, WIDE), 1)
    return jnp.where((lane >= h * HEADDIM) & (lane < (h + 1) * HEADDIM), values, 0.0)


def to_columns(rows):
    have = 8 * len(rows)
    stacked = jnp.concatenate(list(rows) + [jnp.zeros((128 - have, BLOCK), F32)], axis=0)
    return stacked.T


def column(cols, part, h):
    at = 8 * part + h
    return cols[:, at : at + 1]


def silu_parts(values):
    sig = 1.0 / (1.0 + jnp.exp(-values))
    return values * sig, sig * (1.0 + values * (1.0 - sig))


class Block:
    def __init__(self, marks, b):
        self.marks = marks
        self.start = marks[4] + b * BLOCK
        self.pos_row = self.start + iota((1, BLOCK), 1)
        self.pos_col = self.start + iota((BLOCK, 1), 0)

    def lead(self, cum):
        carried = start_of(self.marks, self.pos_row) < self.start
        return jnp.where(carried, jnp.exp(cum), 0.0)

    def tail_base(self, cum):
        last = cum[:, BLOCK - 1 : BLOCK]
        kept = end_of(self.marks, self.pos_row) > self.start + BLOCK - 1
        return jnp.where(kept, jnp.exp(last - cum), 0.0)

    def allowed(self):
        first = start_of(self.marks, self.pos_col)
        return (self.pos_row >= first) & (self.pos_row <= self.pos_col)

    def since_start(self):
        return self.pos_col - start_of(self.marks, self.pos_col)

    def until_end(self):
        return end_of(self.marks, self.pos_col) - self.pos_col


def decay_of(allowed, cum_col, cum_row):
    return jnp.exp(jnp.where(allowed, cum_col - cum_row, -1e30))


def message(state, decay):
    return jnp.concatenate([state, decay], axis=0)


def carried(messages):
    one, two, three = (m[...] for m in messages)

    def join(near, far):
        return near[:STATE] + near[STATE : STATE + 1] * far

    return join(one, join(two, three[:STATE]))


def last_by_lane(rows):
    return by_head([rows[h : h + 1, BLOCK - 1 : BLOCK] for h in range(HEADS_DEV)])


class At:
    def __init__(self, index, blocks, part, parts):
        self.index = index
        self.count = blocks
        self.can_be_first = part == 0
        self.can_be_last = part == parts - 1

    def when_first(self, do):
        if self.can_be_first:
            pl.when(self.index == 0)(do)

    def when_last(self, do):
        if self.can_be_last:
            pl.when(self.index == self.count - 1)(do)


def rows_of(width):
    return ("rows", width)


def lanes_of(count):
    return ("lanes", count)


def whole(dims):
    return ("whole", dims)


STATE_DIMS = (STATE + 8, WIDE)
STATES = ("states",)
SMEM = ("smem",)


def call(kernel, blocks, parts, down, ins, outs, scratch, micros, *args):
    steps = blocks // parts
    tile = parts * BLOCK

    def step(s):
        return steps - 1 - s if down else s

    def spec(kind):
        what = kind[0]
        if what == "smem":
            return pl.BlockSpec(memory_space=pltpu.SMEM)
        if what == "rows":
            return pl.BlockSpec((tile, kind[1]), lambda s: (step(s), 0))
        if what == "lanes":
            return pl.BlockSpec((kind[1], tile), lambda s: (0, step(s)))
        if what == "states":
            return pl.BlockSpec((parts,) + STATE_DIMS, lambda s: (step(s), 0, 0))
        if what == "before":
            return pl.BlockSpec(
                (16, kind[1]), lambda s: (jnp.maximum(step(s) * (tile // 16) - 1, 0), 0)
            )
        return pl.BlockSpec(kind[1], lambda s: (0,) * len(kind[1]))

    def view(refs, n, kind, k):
        ref = refs[n]
        if kind[0] == "rows":
            return ref.at[pl.ds(k * BLOCK, BLOCK)]
        if kind[0] == "lanes":
            return ref.at[:, pl.ds(k * BLOCK, BLOCK)]
        if kind[0] == "states":
            return ref.at[pl.ds(k, 1)]
        if kind[0] == "before" and k > 0:
            return refs[n - 1].at[pl.ds(k * BLOCK - 16, 16)]
        return ref

    kinds = list(ins) + [kind for kind, _ in outs]

    def run(*refs):
        order = range(parts - 1, -1, -1) if down else range(parts)
        for k in order:
            at = At(step(pl.program_id(0)) * parts + k, blocks, k, parts)
            views = [view(refs, n, kind, k) for n, kind in enumerate(kinds)]
            kernel(at, *views, *refs[len(kinds) :])

    def dims(kind):
        what = kind[0]
        if what == "rows":
            return (blocks * BLOCK, kind[1])
        if what == "lanes":
            return (kind[1], blocks * BLOCK)
        if what == "states":
            return (blocks,) + STATE_DIMS
        return kind[1]

    return pl.pallas_call(
        run,
        grid=(steps,),
        in_specs=[spec(kind) for kind in ins],
        out_specs=[spec(kind) for kind, _ in outs],
        out_shape=[jax.ShapeDtypeStruct(dims(kind), dtype) for kind, dtype in outs],
        scratch_shapes=scratch,
        compiler_params=pltpu.CompilerParams(
            dimension_semantics=("arbitrary",), vmem_limit_bytes=VMEM_LIMIT
        ),
        cost_estimate=pl.CostEstimate(
            flops=int(micros * 1.15e9), bytes_accessed=int(micros * 1e6), transcendentals=0
        ),
    )(*args)


def project_kernel(
    at, marks, step_bias, decay_log, skip_gain, hidden, halo, norm_gain, weights, conv_value,
    value_bias, mixer_gain, conv_shared,
    normed_o, xbc_o, slope_o, cin_o, cin_halo_o, rows_o, state_o, device_o,
    gain, taps, lanes, hcols,
    ext, state, decay, upto,
):
    blk = Block(marks, at.index)
    wv = weights.at[:, 0:WIDE]
    ws = weights.at[:, WIDE : 2 * WIDE]

    @at.when_first
    def _():
        gain[...] = jnp.broadcast_to(norm_gain[...].reshape(1, MODEL), (8, MODEL))
        taps[...] = jnp.zeros_like(taps)
        taps[0:4, 0:INNER_DEV] = conv_value[...]
        taps[4:5, 0:INNER_DEV] = value_bias[...].reshape(1, INNER_DEV)
        taps[0:5, WIDE:] = conv_shared[...]
        lanes[...] = jnp.zeros_like(lanes)
        lanes[0:1, 0:INNER_DEV] = mixer_gain[...].reshape(1, INNER_DEV)
        lanes[1:2] = by_head([skip_gain[h] for h in range(HEADS_DEV)])
        row = iota((8, BLOCK), 0)
        bias = jnp.zeros((8, BLOCK), F32)
        rate = jnp.zeros((8, BLOCK), F32)
        for h in range(HEADS_DEV):
            bias = jnp.where(row == h, step_bias[h], bias)
            rate = jnp.where(row == h, decay_log[h], rate)
        hcols[0:8] = bias
        hcols[8:16] = jnp.where(row < HEADS_DEV, -jnp.exp(rate), 0.0)
        square = (BLOCK, BLOCK)
        upto[...] = jnp.where(iota(square, 0) <= iota(square, 1), 1.0, 0.0).astype(BF16)

    def norm(rows):
        rows = rows.astype(F32)
        scale = lax.rsqrt(jnp.mean(rows * rows, axis=1, keepdims=True) + EPSILON)
        return (rows * scale * gain[0:1]).astype(BF16)

    @at.when_first
    def _():
        ahead = norm(halo[...])
        into = jnp.concatenate([nn(ahead, wv[...]), nn(ahead, ws[...])], axis=1)
        into = into.astype(BF16).astype(F32)
        ext[0:8] = into[8:16]
        cin_halo_o[...] = into[8:16]
        state[...] = jnp.zeros_like(state)
        decay[...] = jnp.ones_like(decay)

    normed = norm(hidden[...])
    normed_o[...] = normed
    value_pre = nn(normed, wv[...])
    state_pre = nn(normed, ws[...])
    cin = jnp.concatenate([value_pre, state_pre], axis=1).astype(BF16)
    cin_o[...] = cin
    ext[8 : 8 + BLOCK] = cin.astype(F32)
    pre = taps[4:5] + taps[3:4] * ext[8 : 8 + BLOCK]
    since = blk.since_start()
    for lag in range(1, CONV):
        pre = pre + taps[3 - lag : 4 - lag] * (
            jnp.where(since >= lag, ext[8 - lag : 8 - lag + BLOCK], 0.0)
        )
    ext[0:8] = ext[BLOCK : BLOCK + 8]
    act, slope = silu_parts(pre)
    act = act.astype(BF16)
    xbc_o[...] = act
    slope_o[...] = slope.astype(BF16)

    raw = value_pre[:, 128:256].T[64:72] + hcols[0:8]
    dt = jnp.maximum(raw, 0.0) + jnp.log1p(jnp.exp(-jnp.abs(raw)))
    sig = 1.0 / (1.0 + jnp.exp(-raw))
    cum = running_sum(dt * hcols[8:16], upto[...])
    rows_o[0:8] = dt
    rows_o[8:16] = sig
    rows_o[16:24] = cum
    lead = blk.lead(cum)
    tail = blk.tail_base(cum) * dt
    cols = to_columns([tail])
    tail_lanes = by_head([column(cols, 0, h) for h in range(HEADS_DEV)])
    packed = (act[:, :WIDE].astype(F32) * tail_lanes).astype(BF16)
    fresh = tn(act[:, WIDE : WIDE + STATE], packed)
    last = last_by_lane(lead)
    state_o[0, 0:STATE] = state[...]
    state_o[0, STATE : STATE + 8] = decay[...]
    state[...] = last * state[...] + fresh
    decay[...] = last * decay[...]

    @at.when_last
    def _():
        device_o[...] = message(state[...], decay[...])


def intra_kernel(at, marks, normed, cot, weights, xbc, rows, lanes, z_o, e_o, yi_o):
    blk = Block(marks, at.index)
    z_o[...] = nn(normed[...], weights[:, 0:WIDE]).astype(BF16)
    e_o[...] = nn(cot[...], weights[:, WIDE : 2 * WIDE]).astype(BF16)
    dt = rows[0:8]
    cum = rows[16:24]
    x = xbc[:, :WIDE].astype(F32)
    scores = nt(xbc[:, WIDE + STATE :], xbc[:, WIDE : WIDE + STATE])
    allowed = blk.allowed()
    cols = to_columns([cum])
    out = lanes[1:2] * x
    for h in range(HEADS_DEV):
        decays = decay_of(allowed, column(cols, 0, h), cum[h : h + 1])
        mix = (scores * decays * dt[h : h + 1]).astype(BF16)
        out = out + nn(mix, of_head(x, h).astype(BF16))
    yi_o[...] = out.astype(BF16)


def gated_kernel(
    at, marks, yi, z, e, xbc, rows, states, one, two, three, lanes, weights,
    y_o, mixed_o, part_o, sums_o, prefix,
):
    @at.when_first
    def _():
        prefix[...] = carried((one, two, three))

    blk = Block(marks, at.index)
    lead = blk.lead(rows[16:24])
    cols = to_columns([lead])
    lead_lanes = by_head([column(cols, 0, h) for h in range(HEADS_DEV)])
    entering = states[0, 0:STATE] + states[0, STATE : STATE + 1] * prefix[...]
    y = yi[...].astype(F32) + lead_lanes * nn(xbc[:, WIDE + STATE :], entering.astype(BF16))
    y_o[...] = y.astype(BF16)
    gate, _ = silu_parts(z[...].astype(F32))
    v = y * gate
    mixed = (v * lanes[0:1]).astype(BF16)
    mixed_o[...] = mixed
    part_o[...] = nt(mixed, weights[:, WIDE : 2 * WIDE]).astype(BF16)
    row = iota((16, 2 * WIDE), 0)
    lane = iota((16, 2 * WIDE), 1)
    pick = jnp.where(((row == 0) & (lane < WIDE)) | ((row == 1) & (lane >= WIDE)), 1.0, 0.0)
    both = jnp.concatenate([v * v, e[...].astype(F32) * mixed.astype(F32)], axis=1)
    sums_o[...] = nt(pick.astype(BF16), both.astype(BF16))[0:2]


def gate_back_kernel(
    at, marks, y, z, e, xbc, rows, sums, lanes,
    dy_o, dz_o, reach_o, device_o, gains_o,
    carry, decay,
):
    blk = Block(marks, at.index)

    @at.when_last
    def _():
        carry[...] = jnp.zeros_like(carry)
        decay[...] = jnp.ones_like(decay)
        gains_o[...] = jnp.zeros_like(gains_o)

    lead = blk.lead(rows[16:24])
    root = lax.rsqrt(sums[0:1] / INNER + EPSILON)
    coef = sums[1:2] * root * root * root / INNER
    cols = to_columns([lead, jnp.broadcast_to(root, (8, BLOCK)), jnp.broadcast_to(coef, (8, BLOCK))])
    lead_lanes = by_head([column(cols, 0, h) for h in range(HEADS_DEV)])
    gate, slope = silu_parts(z[...].astype(F32))
    y_v = y[...].astype(F32)
    v = y_v * gate
    dm = column(cols, 1, 0) * e[...].astype(F32)
    dv = lanes[0:1] * dm - column(cols, 2, 0) * v
    dy = dv * gate
    dy_o[...] = dy.astype(BF16)
    dz_o[...] = (dv * y_v * slope).astype(BF16)
    x = xbc[:, :WIDE].astype(F32)
    gains_o[0:1] += jnp.sum(v * dm, axis=0, keepdims=True)
    gains_o[1:2] += jnp.sum(dy * x, axis=0, keepdims=True)
    reach = tn(xbc[:, WIDE + STATE :], (dy * lead_lanes).astype(BF16))
    last = last_by_lane(lead)
    reach_o[0, 0:STATE] = carry[...]
    reach_o[0, STATE : STATE + 8] = decay[...]
    carry[...] = last * carry[...] + reach
    decay[...] = last * decay[...]

    @at.when_first
    def _():
        device_o[...] = message(carry[...], decay[...])


def intra_back_kernel(
    at, marks, dy_r, xbc, rows, states, prefix, sums, mixed, cot, lanes,
    dxi_o, dbc_o, stats_o, grad_out_o,
):
    blk = Block(marks, at.index)

    @at.when_first
    def _():
        grad_out_o[...] = jnp.zeros_like(grad_out_o)

    dt = rows[0:8]
    cum = rows[16:24]
    lead = blk.lead(cum)
    root = lax.rsqrt(sums[0:1] / INNER + EPSILON)
    cols = to_columns([cum, lead, jnp.broadcast_to(root, (8, BLOCK))])
    lead_lanes = by_head([column(cols, 1, h) for h in range(HEADS_DEV)])
    rooted = (mixed[...].astype(F32) * column(cols, 2, 0)).astype(BF16)
    grad_out_o[...] += tn(cot[...], rooted)

    dy = dy_r[...].astype(F32)
    x_low = xbc[:, :WIDE]
    b_low = xbc[:, WIDE : WIDE + STATE]
    c_low = xbc[:, WIDE + STATE :]
    entering = states[0, 0:STATE] + states[0, STATE : STATE + 1] * prefix[...]
    held = entering.astype(BF16)
    masks = head_masks().astype(BF16)
    cross = nn(c_low, held)
    lead_grad = nt(masks, (dy * cross).astype(BF16))
    dc = nt((dy * lead_lanes).astype(BF16), held)
    scores = nt(c_low, b_low)
    allowed = blk.allowed()
    ds = jnp.zeros((BLOCK, BLOCK), F32)
    dx = lanes[1:2] * dy
    lane = iota((1, 128), 1)
    row8 = iota((8, 1), 0)
    row_sums = jnp.zeros((BLOCK, 128), F32)
    time_grad = jnp.zeros((8, BLOCK), F32)
    for h in range(HEADS_DEV):
        dt_h = dt[h : h + 1]
        dy_h = of_head(dy, h).astype(BF16)
        decays = decay_of(allowed, column(cols, 0, h), cum[h : h + 1])
        weighted = nt(dy_h, x_low) * decays
        ds = ds + weighted * dt_h
        scored = weighted * scores
        time_grad = time_grad + jnp.where(
            row8 == h, jnp.sum(scored, axis=0, keepdims=True), 0.0
        )
        row_sums = row_sums + jnp.where(
            lane == h, jnp.sum(scored * dt_h, axis=1, keepdims=True), 0.0
        )
        mix = (scores * decays * dt_h).astype(BF16)
        dx = dx + tn(mix, dy_h)
    ds_low = ds.astype(BF16)
    dxi_o[...] = dx.astype(BF16)
    dbc_o[:, 0:STATE] = tn(ds_low, c_low).astype(BF16)
    dbc_o[:, STATE : 2 * STATE] = (dc + nn(ds_low, b_low)).astype(BF16)
    stats_o[0:8] = time_grad
    stats_o[8:16] = row_sums.T[0:8] - time_grad * dt + lead_grad * lead


def input_back_kernel(
    at, marks, hidden, normed, halo, dz, dxi, dbc, xbc, slope, cin, cin_before, cin_halo,
    rows, stats, states, prefix, reaches, one, two, three, gain, later, weights, taps, hcols,
    grad_out_t, gains,
    dn_o, big_o, pack_o, spill_o,
    ext, ahead, suffix, since, wgrad_o, chan_o, step_o, norm_o,
):
    b = at.index
    blk = Block(marks, b)
    wg = later.at[:, 0:WIDE]
    wv = weights.at[:, 0:WIDE]
    ws = weights.at[:, WIDE : 2 * WIDE]

    @at.when_last
    def _():
        suffix[...] = carried((one, two, three))
        square = (BLOCK, BLOCK)
        since[...] = jnp.where(iota(square, 0) >= iota(square, 1), 1.0, 0.0).astype(BF16)
        wgrad_o[...] = jnp.zeros_like(wgrad_o)
        chan_o[...] = jnp.zeros_like(chan_o)
        step_o[...] = jnp.zeros_like(step_o)
        norm_o[...] = jnp.zeros_like(norm_o)
        ahead[BLOCK : BLOCK + 8] = jnp.zeros((8, CHAN), F32)

    dt = rows[0:8]
    sig = rows[8:16]
    cum = rows[16:24]
    rate = hcols[8:16]
    lead = blk.lead(cum)
    tail_base = blk.tail_base(cum)
    tail = tail_base * dt
    cols = to_columns([tail])
    tail_lanes = by_head([column(cols, 0, h) for h in range(HEADS_DEV)])
    entering = states[0, 0:STATE] + states[0, STATE : STATE + 1] * prefix[...]
    leaving = reaches[0, 0:STATE] + reaches[0, STATE : STATE + 1] * suffix[...]
    leaving_low = leaving.astype(BF16)
    x = xbc[:, :WIDE].astype(F32)
    dpacked = nn(xbc[:, WIDE : WIDE + STATE], leaving_low)
    packed = (x * tail_lanes).astype(BF16)
    masks = head_masks()
    tail_grad = nt(masks.astype(BF16), (dpacked * x).astype(BF16))
    dx = dxi[...].astype(F32) + dpacked * tail_lanes
    db = dbc[:, 0:STATE].astype(F32) + nt(packed, leaving_low)
    dc = dbc[:, STATE : 2 * STATE].astype(F32)

    tail_term = tail_grad * tail
    state_term = jnp.sum(leaving * entering, axis=0, keepdims=True)
    last_term = jnp.sum(tail_term, axis=1, keepdims=True) + (
        jnp.sum(masks * state_term, axis=1, keepdims=True) * lead[:, BLOCK - 1 : BLOCK]
    )
    dcum = stats[8:16] - tail_term + jnp.where(iota((8, BLOCK), 1) == BLOCK - 1, last_term, 0.0)
    dla = running_sum(dcum, since[...])
    ddt = stats[0:8] + tail_grad * tail_base + dla * rate
    dstep = jnp.where(iota((8, 1), 0) < HEADS_DEV, ddt * sig, 0.0)
    step_o[0:8] += dstep
    step_o[8:16] += dla * dt * rate
    placed = jnp.concatenate(
        [jnp.zeros((64, BLOCK), F32), dstep, jnp.zeros((56, BLOCK), F32)], axis=0
    ).T

    dpre = jnp.concatenate([dx, db, dc], axis=1) * slope[...].astype(F32)
    before = cin_before[...][8:16].astype(F32)
    ext[0:8] = jnp.where(b == 0, cin_halo[...], before) if at.can_be_first else before
    ext[8 : 8 + BLOCK] = cin[...].astype(F32)
    ahead[0:BLOCK] = dpre
    chan_o[4:5] += jnp.sum(dpre, axis=0, keepdims=True)
    chan_o[3:4] += jnp.sum(dpre * ext[8 : 8 + BLOCK], axis=0, keepdims=True)
    din = taps[3:4] * dpre
    reach_back = blk.since_start()
    reach_ahead = blk.until_end()
    for lag in range(1, CONV):
        tap = 3 - lag
        chan_o[tap : tap + 1] += jnp.sum(
            jnp.where(reach_back >= lag, dpre * ext[8 - lag : 8 - lag + BLOCK], 0.0),
            axis=0,
            keepdims=True,
        )
        din = din + taps[tap : tap + 1] * (
            jnp.where(reach_ahead > lag, ahead[lag : lag + BLOCK], 0.0)
        )
    ahead[BLOCK : BLOCK + 8] = dpre[0:8]

    dz_low = dz[...]
    dv_low = jnp.concatenate([din[:, 0:128], din[:, 128:256] + placed], axis=1).astype(BF16)
    ds_low = din[:, WIDE:].astype(BF16)
    dn = nt(dz_low, wg[...]) + nt(dv_low, wv[...]) + nt(ds_low, ws[...])
    dn_o[...] = dn.astype(BF16)
    wgrad_o[...] += tn(normed[...], jnp.concatenate([dz_low, dv_low, ds_low], axis=1))

    def unit_of(rows_in):
        rows_in = rows_in.astype(F32)
        return rows_in * lax.rsqrt(jnp.mean(rows_in * rows_in, axis=1, keepdims=True) + EPSILON)

    norm_o[0:1] += jnp.sum(dn * unit_of(hidden[...]), axis=0, keepdims=True)

    @at.when_first
    def _():
        ahead[0:8] = jnp.zeros((8, CHAN), F32)
        ahead[8:16] = dpre[0:8]
        ahead[16:24] = jnp.zeros((8, CHAN), F32)
        pos = blk.start - 8 + iota((8, 1), 0)
        left = end_of(marks, pos) - pos
        back = jnp.zeros((8, CHAN), F32)
        for lag in range(1, CONV):
            same = (left > lag) & (pos >= 0)
            back = back + taps[3 - lag : 4 - lag] * (
                ahead[lag : lag + 8] * jnp.where(same, 1.0, 0.0)
            )
        low = jnp.concatenate([jnp.zeros((8, CHAN), F32), back], axis=0).astype(BF16)
        given = nt(low[:, :WIDE], wv[...]) + nt(low[:, WIDE:], ws[...])
        spill_o[...] = given[8:16]
        unit_halo = unit_of(halo[...])
        norm_o[0:1] += jnp.sum(given[8:16] * unit_halo[8:16], axis=0, keepdims=True)
        wgrad_o[:, WIDE:] += tn((unit_halo * gain[0:1]).astype(BF16), low)
        big_o[:, 0 : 3 * WIDE] = wgrad_o[...].astype(BF16)
        big_o[:, 3 * WIDE :] = grad_out_t[...].astype(BF16)
        pack = jnp.concatenate(
            [
                jnp.concatenate([chan_o[0:5], jnp.zeros((5, CHAN), F32)], axis=1),
                jnp.concatenate([norm_o[0:1], step_o[8:9]], axis=1),
                jnp.concatenate([gains[0:1], gains[1:2], step_o[9:10], step_o[10:11]], axis=1),
                jnp.concatenate(
                    [step_o[0:1], step_o[1:2], step_o[2:3], jnp.zeros((1, WIDE), F32)], axis=1
                ),
            ],
            axis=0,
        )
        top = pack.astype(BF16).astype(F32)
        pack_o[...] = jnp.concatenate([top, pack - top], axis=0).astype(BF16)


def passed_along(values, axis, by):
    count = lax.axis_size(axis)
    pairs = [(i, i + by) for i in range(count) if 0 <= i + by < count]
    return lax.ppermute(values, axis, pairs)


def handed_to_all(values, axis):
    count = lax.axis_size(axis)
    return lax.all_to_all(
        jnp.broadcast_to(values[None], (count,) + values.shape), axis, 0, 0, tiled=False
    )


def sent_along(device, sign):
    return [passed_along(device, "context", sign * k) for k in (1, 2, 3)]


def padded(values, width):
    extra = width - values.shape[-1]
    return jnp.pad(values, [(0, 0)] * (values.ndim - 1) + [(0, extra)])


def body(
    hidden, cotangent, lengths, norm_gain, gate_proj, value_proj, state_proj, step_proj,
    conv_value, conv_state, value_bias, state_bias, step_bias, decay_log, skip_gain,
    mixer_gain, out_proj,
):
    tok = hidden.shape[0]
    blocks = tok // BLOCK
    ctx = lax.axis_index("context")
    rank = lax.axis_index("tensor")

    own_rows = state_proj.shape[0]
    first = jnp.concatenate(
        [state_proj.astype(F32), conv_state, state_bias[None], jnp.zeros((3, state_proj.shape[1]), F32)],
        axis=0,
    )
    first = handed_to_all(first, "tensor")
    first, lengths, gate_proj, out_proj, edge = lax.optimization_barrier(
        (first, lengths, gate_proj, out_proj, hidden[tok - 16 :])
    )
    first = first.transpose(1, 0, 2).reshape(own_rows + 8, 2 * STATE)
    conv_shared = first[own_rows : own_rows + 5]
    needed = jnp.concatenate(
        [
            value_proj, step_proj, jnp.zeros((own_rows, 61), BF16), first[:own_rows].astype(BF16),
        ],
        axis=1,
    )
    needed = handed_to_all(needed, CELLS).reshape(MODEL, 2 * WIDE)
    finishes = jnp.cumsum(lengths[0])
    marks = jnp.concatenate([finishes, (ctx * tok)[None], jnp.zeros((3,), jnp.int32)])
    marks = marks.astype(jnp.int32)
    later = jnp.concatenate([padded(gate_proj, WIDE), padded(out_proj.T, WIDE)], axis=1)
    later = handed_to_all(later, CELLS)
    halo = passed_along(edge, "context", 1)

    pair = whole((MODEL, 2 * WIDE))
    normed, xbc, slope, cin, cin_halo, rows, states, device, gain, taps, lanes, hcols = call(
        project_kernel, blocks, PARTS[0], False,
        [
            SMEM, SMEM, SMEM, SMEM, rows_of(MODEL), whole((16, MODEL)), whole((MODEL,)), pair,
            whole((4, INNER_DEV)), whole((INNER_DEV,)), whole((INNER_DEV,)), whole((5, 2 * STATE)),
        ],
        [
            (rows_of(MODEL), BF16), (rows_of(CHAN), BF16), (rows_of(CHAN), BF16),
            (rows_of(CHAN), BF16), (whole((8, CHAN)), F32), (lanes_of(24), F32), (STATES, F32),
            (whole(STATE_DIMS), F32), (whole((8, MODEL)), F32), (whole((8, CHAN)), F32),
            (whole((8, WIDE)), F32), (whole((16, BLOCK)), F32),
        ],
        [
            pltpu.VMEM((BLOCK + 8, CHAN), F32), pltpu.VMEM((STATE, WIDE), F32),
            pltpu.VMEM((8, WIDE), F32), pltpu.VMEM((BLOCK, BLOCK), BF16),
        ],
        14, marks, step_bias, decay_log, skip_gain, hidden, halo, norm_gain, needed, conv_value,
        value_bias, mixer_gain, conv_shared,
    )
    messages = sent_along(device, 1)
    later, xbc = lax.optimization_barrier((later, xbc))
    later = later.reshape(MODEL, 2 * WIDE)
    z, e, yi = call(
        intra_kernel, blocks, PARTS[1], False,
        [
            SMEM, rows_of(MODEL), rows_of(MODEL), pair, rows_of(CHAN), lanes_of(24),
            whole((8, WIDE)),
        ],
        [(rows_of(WIDE), BF16)] * 3,
        [], 12, marks, normed, cotangent, later, xbc, rows, lanes,
    )
    y, mixed, part, sums, prefix = call(
        gated_kernel, blocks, PARTS[2], False,
        [
            SMEM, rows_of(WIDE), rows_of(WIDE), rows_of(WIDE), rows_of(CHAN), lanes_of(24), STATES,
            whole(STATE_DIMS), whole(STATE_DIMS), whole(STATE_DIMS), whole((8, WIDE)), pair,
        ],
        [
            (rows_of(WIDE), BF16), (rows_of(WIDE), BF16), (rows_of(MODEL), BF16),
            (lanes_of(2), F32), (whole((STATE, WIDE)), F32),
        ],
        [], 10, marks, yi, z, e, xbc, rows, states, *messages, lanes, later,
    )
    sums = jnp.sum(handed_to_all(sums, "tensor"), axis=0)

    own = tok // lax.axis_size("tensor")
    place = rank * own
    own_hidden = lax.dynamic_slice_in_dim(hidden, place, own, 0).astype(F32)
    own_cot = lax.dynamic_slice_in_dim(cotangent, place, own, 0).astype(F32)
    own_root = lax.rsqrt(lax.dynamic_slice_in_dim(sums[0], place, own, 0) / INNER + EPSILON)
    projected = lax.psum_scatter(part, "tensor", scatter_dimension=0, tiled=True).astype(F32)
    own_out = (own_hidden + own_root[:, None] * projected).astype(BF16)

    dy, dz, reaches, back_device, gains = call(
        gate_back_kernel, blocks, PARTS[3], True,
        [
            SMEM, rows_of(WIDE), rows_of(WIDE), rows_of(WIDE), rows_of(CHAN), lanes_of(24),
            lanes_of(2), whole((8, WIDE)),
        ],
        [
            (rows_of(WIDE), BF16), (rows_of(WIDE), BF16), (STATES, F32), (whole(STATE_DIMS), F32),
            (whole((8, WIDE)), F32),
        ],
        [pltpu.VMEM((STATE, WIDE), F32), pltpu.VMEM((8, WIDE), F32)],
        9, marks, y, z, e, xbc, rows, sums, lanes,
    )
    messages = sent_along(back_device, -1)
    dxi, dbc, stats, grad_out_t = call(
        intra_back_kernel, blocks, PARTS[4], False,
        [
            SMEM, rows_of(WIDE), rows_of(CHAN), lanes_of(24), STATES, whole((STATE, WIDE)),
            lanes_of(2), rows_of(WIDE), rows_of(MODEL), whole((8, WIDE)),
        ],
        [
            (rows_of(WIDE), BF16), (rows_of(WIDE), BF16), (lanes_of(16), F32),
            (whole((MODEL, WIDE)), F32),
        ],
        [], 13, marks, dy, xbc, rows, states, prefix, sums, mixed, cotangent, lanes,
    )
    dxi, own_out, messages = lax.optimization_barrier((dxi, own_out, messages))
    output = lax.all_gather(own_out, "tensor", axis=0, tiled=True)
    dn, big, pack, spill = call(
        input_back_kernel, blocks, PARTS[5], True,
        [
            SMEM, rows_of(MODEL), rows_of(MODEL), whole((16, MODEL)), rows_of(WIDE), rows_of(WIDE),
            rows_of(WIDE), rows_of(CHAN), rows_of(CHAN), rows_of(CHAN), ("before", CHAN),
            whole((8, CHAN)), lanes_of(24), lanes_of(16), STATES, whole((STATE, WIDE)), STATES,
            whole(STATE_DIMS), whole(STATE_DIMS), whole(STATE_DIMS), whole((8, MODEL)), pair, pair, whole((8, CHAN)),
            whole((16, BLOCK)), whole((MODEL, WIDE)), whole((8, WIDE)),
        ],
        [
            (rows_of(MODEL), BF16), (whole((MODEL, 4 * WIDE)), BF16),
            (whole((16, 4 * WIDE)), BF16), (whole((8, MODEL)), F32),
        ],
        [
            pltpu.VMEM((BLOCK + 8, CHAN), F32), pltpu.VMEM((BLOCK + 8, CHAN), F32),
            pltpu.VMEM((STATE, WIDE), F32), pltpu.VMEM((BLOCK, BLOCK), BF16),
            pltpu.VMEM((MODEL, 3 * WIDE), F32), pltpu.VMEM((8, CHAN), F32),
            pltpu.VMEM((16, BLOCK), F32), pltpu.VMEM((8, MODEL), F32),
        ],
        22, marks, hidden, normed, halo, dz, dxi, dbc, xbc, slope, cin, cin, cin_halo,
        rows, stats, states, prefix, reaches, *messages, gain, later, needed, taps, hcols, grad_out_t, gains,
    )
    arrived = passed_along(spill, "context", -1)
    end = dn[tok - 8 :].astype(F32) + arrived
    dn = lax.dynamic_update_slice(dn, end.astype(BF16), (tok - 8, 0))
    dn, output = lax.optimization_barrier((dn, output))
    own_dn = lax.psum_scatter(dn, "tensor", scatter_dimension=0, tiled=True)

    cells = lax.axis_size("shard") * lax.axis_size("context")
    big = jnp.concatenate(
        [
            big.reshape(cells, own_rows, 4 * WIDE),
            jnp.broadcast_to(pack[None], (cells,) + pack.shape),
        ],
        axis=1,
    )
    big = jnp.sum(lax.all_to_all(big, CELLS, 0, 0, tiled=False).astype(F32), axis=0)
    own_dn, big = lax.optimization_barrier((own_dn, big))
    own_dn = own_dn.astype(F32)
    scaling = lax.rsqrt(jnp.mean(own_hidden * own_hidden, axis=1, keepdims=True) + EPSILON)
    unit = own_hidden * scaling
    scaled = own_dn * norm_gain[None]
    own_grad = own_cot + scaling * (
        scaled - unit * jnp.mean(scaled * unit, axis=1, keepdims=True)
    )
    grad_hidden = lax.all_gather(own_grad.astype(BF16), "tensor", axis=0, tiled=True)

    small = big[own_rows : own_rows + 8] + big[own_rows + 8 :]
    big = big[:own_rows]
    chan = small[:5, :CHAN]
    norm_cells = small[5, :MODEL]
    grad_mixer = small[6, :INNER_DEV]
    grad_skip = jnp.sum(small[6, WIDE : WIDE + INNER_DEV].reshape(HEADS_DEV, HEADDIM), axis=1)
    grad_step_bias = jnp.sum(small[7, : 3 * WIDE].reshape(HEADS_DEV, WIDE), axis=1)
    grad_decay = jnp.stack(
        [jnp.sum(small[5, MODEL:]), jnp.sum(small[6, 2 * WIDE : 3 * WIDE]), jnp.sum(small[6, 3 * WIDE :])]
    )
    share = 2 * STATE // lax.axis_size("tensor")
    shared = jnp.concatenate([big[:, 2 * WIDE : 3 * WIDE], chan[:, WIDE:]], axis=0)
    shared = shared.reshape(own_rows + 5, -1, share).transpose(1, 0, 2)
    shared = shared.reshape(shared.shape[0], -1)
    count = shared.shape[1]
    final = jnp.concatenate(
        [shared, jnp.broadcast_to(norm_cells[None], (shared.shape[0], MODEL))], axis=1
    )
    final = padded(final, 2560).reshape(-1, 20, 128)
    final = jnp.sum(lax.all_to_all(final, "tensor", 0, 0, tiled=False), axis=0).reshape(-1)
    state_all = final[:count].reshape(own_rows + 5, share)
    return (
        output,
        grad_hidden,
        final[count : count + MODEL],
        big[:, :INNER_DEV],
        big[:, WIDE : WIDE + INNER_DEV],
        state_all[:own_rows],
        big[:, WIDE + INNER_DEV : WIDE + INNER_DEV + HEADS_DEV],
        chan[:4, :INNER_DEV],
        state_all[own_rows : own_rows + 4],
        chan[4, :INNER_DEV],
        state_all[own_rows + 4],
        grad_step_bias,
        grad_decay,
        grad_skip,
        grad_mixer,
        big[:, 3 * WIDE : 3 * WIDE + INNER_DEV].T,
    )


def solution(mesh):
    cells = P(CELLS, None)
    split = P(CELLS, "tensor")
    return jax.shard_map(
        body,
        mesh=mesh,
        in_specs=(
            cells, cells, P("shard", None), P(), split, split, split, split, P(None, "tensor"),
            P(None, "tensor"), P("tensor"), P("tensor"), P("tensor"), P("tensor"), P("tensor"),
            P("tensor"), P("tensor", CELLS),
        ),
        out_specs=(
            cells, cells, P(), split, split, split, split, P(None, "tensor"), P(None, "tensor"),
            P("tensor"), P("tensor"), P("tensor"), P("tensor"), P("tensor"), P("tensor"),
            P("tensor", CELLS),
        ),
        check_vma=False,
    )
```

time: 267 us -> 244 us (0.914)
  waiting for transfers between devices: 78.7 us -> 62.2 us
  local copies, waits for them, and re-layouts: 34.1 us -> 25.8 us
  Pallas kernels: 77.7 us -> 70.7 us
  starting transfers between devices: 42.4 us -> 49.4 us
    all_to_all x4, waiting for transfers between devices: 34.6 us -> 19.5 us  [handed_to_all(): lax.all_to_all(jnp.broadcast_to(values[None], (count,) + values.shape), a...]
    all_to_all x1, waiting for transfers between devices: 20.4 us -> 27.9 us  [body(): lax.all_to_all(big, CELLS, 0, 0, tiled=False).astype(F32)]
    ppermute x8, waiting for transfers between devices: 12.3 us -> 5.3 us  [passed_along(): return lax.ppermute(values, axis, pairs)]
    pallas_call x6, Pallas kernels: 77.7 us -> 70.7 us  [call(): pl.pallas_call(run, grid=(steps,), in_specs=[spec(kind) for kind in ins],...]
    slice x20 -> x7, local copies, waits for them, and re-layouts: 7.42 us -> 2.13 us  [the longest x2 0.77 us: body(): conv_shared = first[own_rows:own_rows + 5]]
    all_to_all x1, starting transfers between devices: 3.71 us -> 8.12 us  [body(): lax.all_to_all(big, CELLS, 0, 0, tiled=False).astype(F32)]
    unnamed x38 -> x49, local copies, waits for them, and re-layouts: 8.32 us -> 12.5 us
    pad x5 -> x0, local copies, waits for them, and re-layouts: 3.31 us -> none  [padded(): return jnp.pad(values, [(0, 0)] * (values.ndim - 1) + [(0, extra)])]
  transfers between devices with their start and end apart: 18 -> 18, of which waited for: 9 -> 7; matrix products, arithmetic and copies ran while one was open for 13% -> 10% of each run, Pallas kernels for 21% -> 26%
where the time goes in v2:
time: 244 us; the launch traced here: 241 us
  Pallas kernels  70.7 us (29%)
  waiting for transfers between devices  62.2 us (25%)
  starting transfers between devices  49.4 us (20%)
  local copies, waits for them, and re-layouts  25.8 us (11%)
  other arithmetic  18.2 us (7%)
  between operations  14.3 us (6%)
    pallas_call x6, Pallas kernels, call(): pl.pallas_call(run, grid=(steps,), in_specs=[spec(kind) for kind in ins],...  70.7 us
    all_to_all x1, waiting for transfers between devices, body(): lax.all_to_all(big, CELLS, 0, 0, tiled=False).astype(F32)  27.9 us
    all_to_all x4, waiting for transfers between devices, handed_to_all(): lax.all_to_all(jnp.broadcast_to(values[None], (count,) + values.shape), a...  19.5 us
    all_to_all x4, starting transfers between devices, handed_to_all(): lax.all_to_all(jnp.broadcast_to(values[None], (count,) + values.shape), a...  19.4 us
    ppermute x8, starting transfers between devices, passed_along(): return lax.ppermute(values, axis, pairs)  18.1 us
    unnamed x49, local copies, waits for them, and re-layouts  12.5 us
    all_to_all x1, starting transfers between devices, body(): lax.all_to_all(big, CELLS, 0, 0, tiled=False).astype(F32)  8.12 us
    all_gather x1, waiting for transfers between devices, body(): lax.all_gather(own_grad.astype(BF16), 'tensor', axis=0, tiled=True)  6.81 us
  transfers between devices with their start and end apart: 18, of which 7 were waited for; matrix products, arithmetic and copies ran while one was open for 10% of the time, Pallas kernels for 26%

profile of v2, /device:TPU:0, one launch (start us, length us, event | category | flops | bytes accessed | tf_op | source)
XLA Modules:
  0.0 240.5 jit_solution(6544190135983050612)
XLA Ops:
  7.2 0.7 convert_element_type.39
  7.9 0.8 copy.78
  8.7 0.7 copy.79
  9.6 0.8 reshape.152
  10.4 4.6 %all-to-all-start = ((f32[8,1,1792]{2,1,0:T(1,128)}), f32[8,1,1792]{2,1,0:T(1,128)S(1)}, u32[]{:S(2)}, u32[]{:S(2)}) async-start(f32[8,1,1792]{2,1,0:T(1,128)} %reshape.152), calls=%async_computation | async-start | bytes 114688 | tf_op jit(solution)/shard_map/all_to_all | solution.py:629
  14.9 0.8 copy.81
  15.7 0.7 slice.110
  16.5 4.0 %all-to-all-done = f32[8,1,1792]{2,1,0:T(1,128)S(1)} async-done(((f32[8,1,1792]{2,1,0:T(1,128)}), f32[8,1,1792]{2,1,0:T(1,128)S(1)}, u32[]{:S(2)}, u32[]{:S(2)}) %all-to-all-start) | async-done | bytes 57376 | tf_op jit(solution)/shard_map/all_to_all | solution.py:629
  21.0 0.8 reduce.15
  22.1 0.8 pad_maximum_fusion.3
  22.9 1.0 broadcast_in_dim.27
  23.8 7.9 %all-to-all-start.1 = ((bf16[16,48,512]{2,1,0:T(8,128)(2,1)}), bf16[16,48,512]{2,1,0:T(8,128)(2,1)S(1)}, u32[]{:S(2)}, u32[]{:S(2)}) async-start(bf16[16,48,512]{2,1,0:T(8,128)(2,1)} %broadcast_in_dim.27), calls=%async_computation.1 | async-start | bytes 1572864 | tf_op jit(solution)/shard_map/all_to_all | solution.py:629
  31.7 3.8 %collective-permute-start = (bf16[16,768]{1,0:T(8,128)(2,1)S(1)}, bf16[16,768]{1,0:T(8,128)(2,1)S(1)}, u32[]{:S(2)}, u32[]{:S(2)}) collective-permute-start(bf16[16,768]{1,0:T(8,128)(2,1)S(1)} %slice.110), channel_id=1, source_target_pairs={{0,8},{8,16},{16,24},{1,9},{9,17},{17,25},{2,10},{10,18},{18,26},{... | collective-permute-start | bytes 73736 | tf_op jit(solution)/shard_map/ppermute | solution.py:624
  36.5 0.7 copy.90.refs_11_
  37.2 8.8 %all-to-all-done.1 = bf16[16,48,512]{2,1,0:T(8,128)(2,1)S(1)} async-done(((bf16[16,48,512]{2,1,0:T(8,128)(2,1)}), bf16[16,48,512]{2,1,0:T(8,128)(2,1)S(1)}, u32[]{:S(2)}, u32[]{:S(2)}) %all-to-all-start.1) | async-done | bytes 786464 | tf_op jit(solution)/shard_map/all_to_all | solution.py:629
  46.0 1.0 broadcast_in_dim.28
  47.0 3.6 %all-to-all-start.2 = ((bf16[16,48,512]{2,1,0:T(8,128)(2,1)}), bf16[16,48,512]{2,1,0:T(8,128)(2,1)S(1)}, u32[]{:S(2)}, u32[]{:S(2)}) async-start(bf16[16,48,512]{2,1,0:T(8,128)(2,1)} %broadcast_in_dim.28), calls=%async_computation.2 | async-start | bytes 1572864 | tf_op jit(solution)/shard_map/all_to_all | solution.py:629
  51.3 12.9 %shard_map.288 = (bf16[2048,768]{1,0:T(8,128)(2,1)}, bf16[2048,512]{1,0:T(8,128)(2,1)}, bf16[2048,512]{1,0:T(8,128)(2,1)}, bf16[2048,512]{1,0:T(8,128)(2,1)}, f3...) custom-call(s32[8]{0:T(128)} %pad_add_fusion.refs_0_, ...), custom_call_target="tpu_custom_call" | custom-call | flops 16099999744 | bytes 14000000 | tf_op jit(solution)/shard_map/pallas_call | solution.py:238
  64.2 4.9 %collective-permute-start.3 = (f32[136,256]{1,0:T(8,128)}, f32[136,256]{1,0:T(8,128)S(1)}, u32[]{:S(2)}, u32[]{:S(2)}) collective-permute-start(f32[136,256]{1,0:T(8,128)} %get-tuple-element.80), channel_id=1, source_target_pairs={{0,24},{1,25},{2,26},{3,27},{4,28},{5,29},{6,30},{7,31},{32,56},{3... | collective-permute-start | bytes 417800 | tf_op jit(solution)/shard_map/ppermute | solution.py:624
  69.1 1.3 collective-permute-start.2
  70.4 2.8 %collective-permute-start.1 = (f32[136,256]{1,0:T(8,128)}, f32[136,256]{1,0:T(8,128)S(1)}, u32[]{:S(2)}, u32[]{:S(2)}) collective-permute-start(f32[136,256]{1,0:T(8,128)} %get-tuple-element.80), channel_id=1, source_target_pairs={{0,8},{8,16},{16,24},{1,9},{9,17},{17,25},{2,10},{10,18},{18,26},{... | collective-permute-start | bytes 417800 | tf_op jit(solution)/shard_map/ppermute | solution.py:624
  73.2 0.9 copy-done.4
  74.1 8.1 %shard_map.289 = (bf16[2048,256]{1,0:T(8,128)(2,1)}, bf16[2048,256]{1,0:T(8,128)(2,1)}, bf16[2048,256]{1,0:T(8,128)(2,1)}) custom-call(s32[8]{0:T(128)} %pad_add_fusion.refs_0_, bf16[2048,768]{1,0:T(8,128)(2,1)} %get-tuple-element.68.refs_1_.refs_2_, bf16[2048,768]{1,0:T(8,128)(2,1)} %refs_8_.3, bf16[768,512]{1,0:T(8,128)(2,1)} %bitcast.33, ...), custom_call_target="tpu_custom_call" | custom-call | flops 13799999488 | bytes 12000000 | tf_op jit(solution)/shard_map/pallas_call | solution.py:238
  82.3 0.6 copy-done.15
  83.0 7.6 %shard_map.290 = (bf16[2048,256]{1,0:T(8,128)(2,1)}, bf16[2048,256]{1,0:T(8,128)(2,1)}, bf16[2048,768]{1,0:T(8,128)(2,1)}, f32[2,2048]{1,0:T(2,128)}, f32[128,256]{1,0:T(8,128)}) custom-call(s32[8]{0:T(128)} %pad_add_fusion.refs_0_, bf16[2048,256]{1,0:T(8,128)(2,1)} %get-tuple-element.76.refs_1_, bf16[2048,256]{1,0:T(8,128)(2,1)} %get-tuple-element.77.refs_2_, ...), custom_call_target="tpu_custom_call" | custom-call | flops 11500000256 | bytes 10000000 | tf_op jit(solution)/shard_map/pallas_call | solution.py:238
  90.7 0.7 copy-done.11
  91.4 0.7 broadcast_in_dim.29
  92.0 3.4 %all-to-all-start.3 = ((f32[8,2,2048]{2,1,0:T(2,128)}), f32[8,2,2048]{2,1,0:T(2,128)S(1)}, u32[]{:S(2)}, u32[]{:S(2)}) async-start(f32[8,2,2048]{2,1,0:T(2,128)} %broadcast_in_dim.29), calls=%async_computation.3 | async-start | bytes 262144 | tf_op jit(solution)/shard_map/all_to_all | solution.py:629
  95.5 6.8 %all-to-all-done.3 = f32[8,2,2048]{2,1,0:T(2,128)S(1)} async-done(((f32[8,2,2048]{2,1,0:T(2,128)}), f32[8,2,2048]{2,1,0:T(2,128)S(1)}, u32[]{:S(2)}, u32[]{:S(2)}) %all-to-all-start.3) | async-done | bytes 131104 | tf_op jit(solution)/shard_map/all_to_all | solution.py:629
  102.9 7.3 %shard_map.291 = (bf16[2048,256]{1,0:T(8,128)(2,1)}, bf16[2048,256]{1,0:T(8,128)(2,1)}, f32[8,136,256]{2,1,0:T(8,128)}, f32[136,256]{1,0:T(8,128)}, f32[8,256]{1,0:T(8,128)}) custom-call(s32[8]{0:T(128)} %pad_add_fusion.refs_0_, bf16[2048,256]{1,0:T(8,128)(2,1)} %get-tuple-element.81.refs_1_, bf16[2048,256]{1,0:T(8,128)(2,1)} %get-tuple-element.77.refs_2_, ...), custom_call_target="tpu_custom_call" | custom-call | flops 10350000128 | bytes 9000000 | tf_op jit(solution)/shard_map/pallas_call | solution.py:238
  110.2 1.3 collective-permute-start.6
  111.5 1.3 collective-permute-start.5
  112.8 1.3 collective-permute-start.4
  114.1 12.7 %shard_map.292 = (bf16[2048,256]{1,0:T(8,128)(2,1)}, bf16[2048,256]{1,0:T(8,128)(2,1)}, f32[16,2048]{1,0:T(8,128)}, f32[768,256]{1,0:T(8,128)}) custom-call(s32[8]{0:T(128)} %pad_add_fusion.refs_0_, bf16[2048,256]{1,0:T(8,128)(2,1)} %get-tuple-element.84.refs_1_, bf16[2048,512]{1,0:T(8,128)(2,1)} %get-tuple-element.73.refs_4_.refs_2_.refs_7_, ...), custom_call_target="tpu_custom_call" | custom-call | flops 14949999616 | bytes 13000000 | tf_op jit(solution)/shard_map/pallas_call | solution.py:238
  126.9 2.1 fusion.8
  129.7 22.1 %shard_map.293 = (bf16[2048,768]{1,0:T(8,128)(2,1)}, bf16[768,1024]{1,0:T(8,128)(2,1)}, bf16[16,1024]{1,0:T(8,128)(2,1)}, f32[8,768]{1,0:T(8,128)}) custom-call(s32[8]{0:T(128)} %pad_add_fusion.refs_0_, bf16[2048,768]{1,0:T(8,128)(2,1)} %refs_1_.3, bf16[2048,768]{1,0:T(8,128)(2,1)} %get-tuple-element.68.refs_1_.refs_2_, bf16[16,768]{1,0:T(8,128)(2,1)} %copy-done.18, ...), custom_call_target="tpu_custom_call" | custom-call | flops 25300000768 | bytes 22000000 | tf_op jit(solution)/shard_map/pallas_call | solution.py:238
  151.8 1.4 collective-permute-start.7
  153.2 5.3 %collective-permute-done.7 = f32[8,768]{1,0:T(8,128)S(1)} collective-permute-done((f32[8,768]{1,0:T(8,128)}, f32[8,768]{1,0:T(8,128)S(1)}, u32[]{:S(2)}, u32[]{:S(2)}) %collective-permute-start.7) | collective-permute-done | bytes 24608 | tf_op jit(solution)/shard_map/ppermute | solution.py:624
  158.5 1.3 fusion.12
  159.9 1.6 pad_maximum_fusion
  161.5 8.1 %all-to-all-start.4 = ((bf16[16,64,1024]{2,1,0:T(8,128)(2,1)}), bf16[16,64,1024]{2,1,0:T(8,128)(2,1)S(1)}, u32[]{:S(2)}, u32[]{:S(2)}) async-start(bf16[16,64,1024]{2,1,0:T(8,128)(2,1)} %pad_maximum_fusion), calls=%async_computation.6 | async-start | bytes 4194304 | tf_op jit(solution)/shard_map/all_to_all | solution.py:796
  169.7 27.9 %all-to-all-done.4 = bf16[16,64,1024]{2,1,0:T(8,128)(2,1)S(1)} async-done(((bf16[16,64,1024]{2,1,0:T(8,128)(2,1)}), bf16[16,64,1024]{2,1,0:T(8,128)(2,1)S(1)}, u32[]{:S(2)}, u32[]{:S(2)}) %all-to-all-start.4) | async-done | bytes 2097184 | tf_op jit(solution)/shard_map/all_to_all | solution.py:796
  198.1 1.5 fusion.2
  199.6 2.3 fusion.6
  202.6 0.7 copy.88
  203.9 0.6 reduce_sum.99
  204.6 0.6 reduce_sum.95
  205.3 0.6 pad_maximum_fusion.2
  205.9 0.9 copy.84
  206.8 0.8 copy.85
  207.7 1.0 reshape.134
  208.8 0.7 copy.86
  209.4 3.4 %all-to-all-start.5 = ((f32[8,20,128]{2,1,0:T(8,128)}), f32[8,20,128]{2,1,0:T(8,128)S(1)}, u32[]{:S(2)}, u32[]{:S(2)}) async-start(f32[8,20,128]{2,1,0:T(8,128)} %copy.86), calls=%async_computation.7 | async-start | bytes 196608 | tf_op jit(solution)/shard_map/all_to_all | solution.py:826
  212.8 1.4 slice_reduce_fusion.5
  214.2 0.7 slice_bitcast_fusion
  214.8 2.5 %pad_maximum_fusion.4 = f32[3]{0:T(128)} fusion(f32[1]{0:T(128)} %bitcast.19, f32[1]{0:T(128)} %bitcast.18, f32[1]{0:T(128)} %bitcast.17), kind=kLoop, calls=%fused_computation.40 | loop fusion | flops 6 | bytes 24 | tf_op jit(solution)/shard_map/stack | solution.py:814
  217.4 2.5 %all-to-all-done.5 = f32[8,20,128]{2,1,0:T(8,128)S(1)} async-done(((f32[8,20,128]{2,1,0:T(8,128)}), f32[8,20,128]{2,1,0:T(8,128)S(1)}, u32[]{:S(2)}, u32[]{:S(2)}) %all-to-all-start.5) | async-done | bytes 81952 | tf_op jit(solution)/shard_map/all_to_all | solution.py:826
  220.4 0.7 slice.144
  221.1 0.7 slice.129
  221.8 0.7 copy.87
  222.5 6.8 %all-gather.5.cloned.1.call-done = bf16[2048,768]{1,0:T(8,128)(2,1)} async-done(((bf16[256,768]{1,0:T(8,128)(2,1)}), bf16[2048,768]{1,0:T(8,128)(2,1)}) %all-gather.5.cloned.1.call-update) | async-done | bytes 3145744 | tf_op jit(solution)/shard_map/all_gather | solution.py:805
  229.3 1.7 copy.95
  231.0 1.4 copy-done.1
  232.3 1.7 copy.96
  (94 shorter events, 6.7 us)
Async XLA Ops:
  7.2 28.6 %copy-start.8 = (bf16[192,48]{0,1:T(8,128)(2,1)S(1)}, bf16[192,48]{0,1:T(8,128)(2,1)}, u32[]{:S(2)}) copy-start(bf16[192,48]{0,1:T(8,128)(2,1)} %param.33) | copy-start | bytes 55300
  7.2 28.6 %copy-start.9 = (bf16[48,192]{1,0:T(8,128)(2,1)S(1)}, bf16[48,192]{1,0:T(8,128)(2,1)}, u32[]{:S(2)}) copy-start(bf16[48,192]{1,0:T(8,128)(2,1)} %param.21) | copy-start | bytes 55300
  7.2 28.4 %copy-start.19 = (s32[1,4]{1,0:T(1,128)S(1)}, s32[1,4]{1,0:T(1,128)}, u32[]{:S(2)}) copy-start(s32[1,4]{1,0:T(1,128)} %param.19) | copy-start | bytes 52
  10.4 10.1 %all-to-all-start = ((f32[8,1,1792]{2,1,0:T(1,128)}), f32[8,1,1792]{2,1,0:T(1,128)S(1)}, u32[]{:S(2)}, u32[]{:S(2)}) async-start(f32[8,1,1792]{2,1,0:T(1,128)} %reshape.152), calls=%async_computation | async-start | bytes 114688 | tf_op jit(solution)/shard_map/all_to_all | solution.py:629
  23.8 22.1 %all-to-all-start.1 = ((bf16[16,48,512]{2,1,0:T(8,128)(2,1)}), bf16[16,48,512]{2,1,0:T(8,128)(2,1)S(1)}, u32[]{:S(2)}, u32[]{:S(2)}) async-start(bf16[16,48,512]{2,1,0:T(8,128)(2,1)} %broadcast_in_dim.27), calls=%async_computation.1 | async-start | bytes 1572864 | tf_op jit(solution)/shard_map/all_to_all | solution.py:629
  31.7 18.9 %collective-permute-start = (bf16[16,768]{1,0:T(8,128)(2,1)S(1)}, bf16[16,768]{1,0:T(8,128)(2,1)S(1)}, u32[]{:S(2)}, u32[]{:S(2)}) collective-permute-start(bf16[16,768]{1,0:T(8,128)(2,1)S(1)} %slice.110), channel_id=1, source_target_pairs={{0,8},{8,16},{16,24},{1,9},{9,17},{17,25},{2,10},{10,18},{18,26},{... | collective-permute-start | bytes 73736 | tf_op jit(solution)/shard_map/ppermute | solution.py:624
  45.9 4.7 %copy-start.3 = (bf16[16,48,512]{2,1,0:T(8,128)(2,1)}, bf16[16,48,512]{2,1,0:T(8,128)(2,1)S(1)}, u32[]{:S(2)}) copy-start(bf16[16,48,512]{2,1,0:T(8,128)(2,1)S(1)} %all-to-all-done.1) | copy-start | bytes 2359300
  47.0 26.2 %all-to-all-start.2 = ((bf16[16,48,512]{2,1,0:T(8,128)(2,1)}), bf16[16,48,512]{2,1,0:T(8,128)(2,1)S(1)}, u32[]{:S(2)}, u32[]{:S(2)}) async-start(bf16[16,48,512]{2,1,0:T(8,128)(2,1)} %broadcast_in_dim.28), calls=%async_computation.2 | async-start | bytes 1572864 | tf_op jit(solution)/shard_map/all_to_all | solution.py:629
  50.6 76.3 %reduce-scatter.3.cloned.1.call-start = ((), (), s32[]{:S(2)}) async-start(), calls=%async_computation.8 | async-start | bytes 3538944 | tf_op jit(solution)/shard_map/reduce_scatter | solution.py:729
  50.7 0.6 copy-start.18
  64.2 18.1 %collective-permute-start.3 = (f32[136,256]{1,0:T(8,128)}, f32[136,256]{1,0:T(8,128)S(1)}, u32[]{:S(2)}, u32[]{:S(2)}) collective-permute-start(f32[136,256]{1,0:T(8,128)} %get-tuple-element.80), channel_id=1, source_target_pairs={{0,24},{1,25},{2,26},{3,27},{4,28},{5,29},{6,30},{7,31},{32,56},{3... | collective-permute-start | bytes 417800 | tf_op jit(solution)/shard_map/ppermute | solution.py:624
  69.1 13.2 %collective-permute-start.2 = (f32[136,256]{1,0:T(8,128)}, f32[136,256]{1,0:T(8,128)S(1)}, u32[]{:S(2)}, u32[]{:S(2)}) collective-permute-start(f32[136,256]{1,0:T(8,128)} %get-tuple-element.80), channel_id=1, source_target_pairs={{0,16},{8,24},{1,17},{9,25},{2,18},{10,26},{3,19},{11,27},{4,20},{... | collective-permute-start | bytes 417800 | tf_op jit(solution)/shard_map/ppermute | solution.py:624
  70.4 11.9 %collective-permute-start.1 = (f32[136,256]{1,0:T(8,128)}, f32[136,256]{1,0:T(8,128)S(1)}, u32[]{:S(2)}, u32[]{:S(2)}) collective-permute-start(f32[136,256]{1,0:T(8,128)} %get-tuple-element.80), channel_id=1, source_target_pairs={{0,8},{8,16},{16,24},{1,9},{9,17},{17,25},{2,10},{10,18},{18,26},{... | collective-permute-start | bytes 417800 | tf_op jit(solution)/shard_map/ppermute | solution.py:624
  73.2 0.9 copy-start.4
  82.3 0.7 copy-start.15
  82.3 0.7 copy-start.16
  82.3 0.7 copy-start.17
  90.6 0.7 copy-start.11
  92.0 10.2 %all-to-all-start.3 = ((f32[8,2,2048]{2,1,0:T(2,128)}), f32[8,2,2048]{2,1,0:T(2,128)S(1)}, u32[]{:S(2)}, u32[]{:S(2)}) async-start(f32[8,2,2048]{2,1,0:T(2,128)} %broadcast_in_dim.29), calls=%async_computation.3 | async-start | bytes 262144 | tf_op jit(solution)/shard_map/all_to_all | solution.py:629
  95.4 64.4 %all-gather.3.cloned.1.call-start = ((), (), s32[]{:S(2)}) async-start(), calls=%async_computation.9 | async-start | bytes 3538944 | tf_op jit(solution)/shard_map/all_gather | solution.py:759
  102.3 0.6 copy-start.6
  110.2 18.7 %collective-permute-start.6 = (f32[136,256]{1,0:T(8,128)}, f32[136,256]{1,0:T(8,128)S(1)}, u32[]{:S(2)}, u32[]{:S(2)}) collective-permute-start(f32[136,256]{1,0:T(8,128)} %get-tuple-element.89), channel_id=1, source_target_pairs={{24,0},{25,1},{26,2},{27,3},{28,4},{29,5},{30,6},{31,7},{56,32},{5... | collective-permute-start | bytes 417800 | tf_op jit(solution)/shard_map/ppermute | solution.py:624
  111.5 17.4 %collective-permute-start.5 = (f32[136,256]{1,0:T(8,128)}, f32[136,256]{1,0:T(8,128)S(1)}, u32[]{:S(2)}, u32[]{:S(2)}) collective-permute-start(f32[136,256]{1,0:T(8,128)} %get-tuple-element.89), channel_id=1, source_target_pairs={{16,0},{24,8},{17,1},{25,9},{18,2},{26,10},{19,3},{27,11},{20,4},{... | collective-permute-start | bytes 417800 | tf_op jit(solution)/shard_map/ppermute | solution.py:624
  112.8 16.1 %collective-permute-start.4 = (f32[136,256]{1,0:T(8,128)}, f32[136,256]{1,0:T(8,128)S(1)}, u32[]{:S(2)}, u32[]{:S(2)}) collective-permute-start(f32[136,256]{1,0:T(8,128)} %get-tuple-element.89), channel_id=1, source_target_pairs={{8,0},{16,8},{24,16},{9,1},{17,9},{25,17},{10,2},{18,10},{26,18},{... | collective-permute-start | bytes 417800 | tf_op jit(solution)/shard_map/ppermute | solution.py:624
  128.9 0.7 copy-start.12
  129.0 0.7 copy-start.13
  129.0 0.7 copy-start.14
  129.0 69.1 %reduce-scatter.5.cloned.1.call-start = ((), (), s32[]{:S(2)}) async-start(), calls=%async_computation.10 | async-start | bytes 3538944 | tf_op jit(solution)/shard_map/reduce_scatter | solution.py:786
  151.8 8.1 %copy-start.7 = (bf16[16,1024]{1,0:T(8,128)(2,1)S(1)}, bf16[16,1024]{1,0:T(8,128)(2,1)}, u32[]{:S(2)}) copy-start(bf16[16,1024]{1,0:T(8,128)(2,1)} %get-tuple-element.111) | copy-start | bytes 98308
  151.8 8.1 %copy-start.2 = (bf16[768,1024]{1,0:T(8,128)(2,1)S(1)}, bf16[768,1024]{1,0:T(8,128)(2,1)}, u32[]{:S(2)}) copy-start(bf16[768,1024]{1,0:T(8,128)(2,1)} %get-tuple-element.110) | copy-start | bytes 4718596
  151.8 6.7 %collective-permute-start.7 = (f32[8,768]{1,0:T(8,128)}, f32[8,768]{1,0:T(8,128)S(1)}, u32[]{:S(2)}, u32[]{:S(2)}) collective-permute-start(f32[8,768]{1,0:T(8,128)} %get-tuple-element.106), channel_id=1, source_target_pairs={{8,0},{16,8},{24,16},{9,1},{17,9},{25,17},{10,2},{18,10},{26,18},{... | collective-permute-start | bytes 73736 | tf_op jit(solution)/shard_map/ppermute | solution.py:624
  161.5 36.5 %copy-start.10 = (f32[768]{0:T(1024)S(1)}, f32[768]{0:T(1024)}, u32[]{:S(2)}) copy-start(f32[768]{0:T(1024)} %refs_6_.1) | copy-start | bytes 9220
  161.5 36.1 %all-to-all-start.4 = ((bf16[16,64,1024]{2,1,0:T(8,128)(2,1)}), bf16[16,64,1024]{2,1,0:T(8,128)(2,1)S(1)}, u32[]{:S(2)}, u32[]{:S(2)}) async-start(bf16[16,64,1024]{2,1,0:T(8,128)(2,1)} %pad_maximum_fusion), calls=%async_computation.6 | async-start | bytes 4194304 | tf_op jit(solution)/shard_map/all_to_all | solution.py:796
  169.7 59.7 %all-gather.5.cloned.1.call-start = ((), (), s32[]{:S(2)}) async-start(), calls=%async_computation.11 | async-start | bytes 3538944 | tf_op jit(solution)/shard_map/all_gather | solution.py:805
  198.0 31.3 %copy-start = (bf16[2048,768]{1,0:T(8,128)(2,1)S(1)}, bf16[2048,768]{1,0:T(8,128)(2,1)}, u32[]{:S(2)}) copy-start(bf16[2048,768]{1,0:T(8,128)(2,1)} %all-gather.3.cloned.1.call-done) | copy-start | bytes 9437188
  202.0 3.3 %copy-start.5 = (f32[8,1024]{1,0:T(8,128)}, f32[8,1024]{1,0:T(8,128)S(1)}, u32[]{:S(2)}) copy-start(f32[8,1024]{1,0:T(8,128)S(1)} %slice_add_fusion) | copy-start | bytes 98308
  209.4 10.5 %all-to-all-start.5 = ((f32[8,20,128]{2,1,0:T(8,128)}), f32[8,20,128]{2,1,0:T(8,128)S(1)}, u32[]{:S(2)}, u32[]{:S(2)}) async-start(f32[8,20,128]{2,1,0:T(8,128)} %copy.86), calls=%async_computation.7 | async-start | bytes 196608 | tf_op jit(solution)/shard_map/all_to_all | solution.py:826
  229.3 3.0 %copy-start.1 = (bf16[2048,768]{1,0:T(8,128)(2,1)S(1)}, bf16[2048,768]{1,0:T(8,128)(2,1)}, u32[]{:S(2)}) copy-start(bf16[2048,768]{1,0:T(8,128)(2,1)} %all-gather.5.cloned.1.call-done) | copy-start | bytes 9437188
Sparse Core Ops, SparseCore 0:
  90.8 34.3 reduce-scatter.2
  129.1 29.4 all-gather.2
  161.6 36.3 reduce-scatter.4
  202.0 27.2 all-gather.4

commit v3 on v2

--- a/solution.py
+++ b/solution.py
@@ -152,6 +152,8 @@
     def __init__(self, index, blocks, part, parts):
         self.index = index
         self.count = blocks
+        self.part = part
+        self.parts = parts
         self.can_be_first = part == 0
         self.can_be_last = part == parts - 1
 
@@ -192,17 +194,13 @@
         what = kind[0]
         if what == "smem":
             return pl.BlockSpec(memory_space=pltpu.SMEM)
-        if what == "rows":
-            return pl.BlockSpec((tile, kind[1]), lambda s: (step(s), 0))
+        if what in ("rows", "tile"):
+            return pl.BlockSpec((tile, kind[1]), lambda s, marks: (step(s), 0))
         if what == "lanes":
-            return pl.BlockSpec((kind[1], tile), lambda s: (0, step(s)))
+            return pl.BlockSpec((kind[1], tile), lambda s, marks: (0, step(s)))
         if what == "states":
-            return pl.BlockSpec((parts,) + STATE_DIMS, lambda s: (step(s), 0, 0))
-        if what == "before":
-            return pl.BlockSpec(
-                (16, kind[1]), lambda s: (jnp.maximum(step(s) * (tile // 16) - 1, 0), 0)
-            )
-        return pl.BlockSpec(kind[1], lambda s: (0,) * len(kind[1]))
+            return pl.BlockSpec((parts,) + STATE_DIMS, lambda s, marks: (step(s), 0, 0))
+        return pl.BlockSpec(kind[1], lambda s, marks: (0,) * len(kind[1]))
 
     def view(refs, n, kind, k):
         ref = refs[n]
@@ -212,8 +210,6 @@
             return ref.at[:, pl.ds(k * BLOCK, BLOCK)]
         if kind[0] == "states":
             return ref.at[pl.ds(k, 1)]
-        if kind[0] == "before" and k > 0:
-            return refs[n - 1].at[pl.ds(k * BLOCK - 16, 16)]
         return ref
 
     kinds = list(ins) + [kind for kind, _ in outs]
@@ -227,7 +223,7 @@
 
     def dims(kind):
         what = kind[0]
-        if what == "rows":
+        if what in ("rows", "tile"):
             return (blocks * BLOCK, kind[1])
         if what == "lanes":
             return (kind[1], blocks * BLOCK)
@@ -237,11 +233,14 @@
 
     return pl.pallas_call(
         run,
-        grid=(steps,),
-        in_specs=[spec(kind) for kind in ins],
-        out_specs=[spec(kind) for kind, _ in outs],
+        grid_spec=pltpu.PrefetchScalarGridSpec(
+            num_scalar_prefetch=1,
+            grid=(steps,),
+            in_specs=[spec(kind) for kind in ins[1:]],
+            out_specs=[spec(kind) for kind, _ in outs],
+            scratch_shapes=scratch,
+        ),
         out_shape=[jax.ShapeDtypeStruct(dims(kind), dtype) for kind, dtype in outs],
-        scratch_shapes=scratch,
         compiler_params=pltpu.CompilerParams(
             dimension_semantics=("arbitrary",), vmem_limit_bytes=VMEM_LIMIT
         ),
@@ -488,27 +487,25 @@
 
 
 def input_back_kernel(
-    at, marks, hidden, normed, halo, dz, dxi, dbc, xbc, slope, cin, cin_before, cin_halo,
+    at, marks, normed, halo, dz, dxi, dbc, xbc, slope, cin, cin_halo,
     rows, stats, states, prefix, reaches, one, two, three, gain, later, weights, taps, hcols,
     grad_out_t, gains,
-    dn_o, big_o, pack_o, spill_o,
-    ext, ahead, suffix, since, wgrad_o, chan_o, step_o, norm_o,
+    dn_o, early_o, late_o, pack_o, spill_o,
+    ahead, suffix, since, wgrad, chan, steps, norm, low, wide,
 ):
-    b = at.index
-    blk = Block(marks, b)
-    wg = later.at[:, 0:WIDE]
-    wv = weights.at[:, 0:WIDE]
-    ws = weights.at[:, WIDE : 2 * WIDE]
+    blk = Block(marks, at.index)
 
     @at.when_last
     def _():
         suffix[...] = carried((one, two, three))
         square = (BLOCK, BLOCK)
         since[...] = jnp.where(iota(square, 0) >= iota(square, 1), 1.0, 0.0).astype(BF16)
-        wgrad_o[...] = jnp.zeros_like(wgrad_o)
-        chan_o[...] = jnp.zeros_like(chan_o)
-        step_o[...] = jnp.zeros_like(step_o)
-        norm_o[...] = jnp.zeros_like(norm_o)
+        wide[:, 0:WIDE] = later[:, 0:WIDE]
+        wide[:, WIDE : 3 * WIDE] = weights[...]
+        wgrad[...] = jnp.zeros_like(wgrad)
+        chan[...] = jnp.zeros_like(chan)
+        steps[...] = jnp.zeros_like(steps)
+        norm[...] = jnp.zeros_like(norm)
         ahead[BLOCK : BLOCK + 8] = jnp.zeros((8, CHAN), F32)
 
     dt = rows[0:8]
@@ -541,81 +538,104 @@
     dla = running_sum(dcum, since[...])
     ddt = stats[0:8] + tail_grad * tail_base + dla * rate
     dstep = jnp.where(iota((8, 1), 0) < HEADS_DEV, ddt * sig, 0.0)
-    step_o[0:8] += dstep
-    step_o[8:16] += dla * dt * rate
+    steps[0:8] += dstep
+    steps[8:16] += dla * dt * rate
     placed = jnp.concatenate(
         [jnp.zeros((64, BLOCK), F32), dstep, jnp.zeros((56, BLOCK), F32)], axis=0
     ).T
 
     dpre = jnp.concatenate([dx, db, dc], axis=1) * slope[...].astype(F32)
-    before = cin_before[...][8:16].astype(F32)
-    ext[0:8] = jnp.where(b == 0, cin_halo[...], before) if at.can_be_first else before
-    ext[8 : 8 + BLOCK] = cin[...].astype(F32)
+    inputs = cin[...].astype(F32)
     ahead[0:BLOCK] = dpre
-    chan_o[4:5] += jnp.sum(dpre, axis=0, keepdims=True)
-    chan_o[3:4] += jnp.sum(dpre * ext[8 : 8 + BLOCK], axis=0, keepdims=True)
+    chan[4:5] += jnp.sum(dpre, axis=0, keepdims=True)
+    chan[3:4] += jnp.sum(dpre * inputs, axis=0, keepdims=True)
     din = taps[3:4] * dpre
-    reach_back = blk.since_start()
-    reach_ahead = blk.until_end()
+    left = blk.until_end()
     for lag in range(1, CONV):
         tap = 3 - lag
-        chan_o[tap : tap + 1] += jnp.sum(
-            jnp.where(reach_back >= lag, dpre * ext[8 - lag : 8 - lag + BLOCK], 0.0),
-            axis=0,
-            keepdims=True,
-        )
-        din = din + taps[tap : tap + 1] * (
-            jnp.where(reach_ahead > lag, ahead[lag : lag + BLOCK], 0.0)
-        )
+        later_dpre = jnp.where(left > lag, ahead[lag : lag + BLOCK], 0.0)
+        chan[tap : tap + 1] += jnp.sum(later_dpre * inputs, axis=0, keepdims=True)
+        din = din + taps[tap : tap + 1] * later_dpre
     ahead[BLOCK : BLOCK + 8] = dpre[0:8]
-
-    dz_low = dz[...]
-    dv_low = jnp.concatenate([din[:, 0:128], din[:, 128:256] + placed], axis=1).astype(BF16)
-    ds_low = din[:, WIDE:].astype(BF16)
-    dn = nt(dz_low, wg[...]) + nt(dv_low, wv[...]) + nt(ds_low, ws[...])
+    mine = pl.ds(at.part * BLOCK, BLOCK)
+    low[mine, 0:WIDE] = dz[...]
+    low[mine, WIDE : WIDE + 128] = din[:, 0:128].astype(BF16)
+    low[mine, WIDE + 128 : 2 * WIDE] = (din[:, 128:256] + placed).astype(BF16)
+    low[mine, 2 * WIDE :] = din[:, WIDE:].astype(BF16)
+
+    if at.part > 0:
+        return
+
+    all_low = low[...]
+    normed_all = normed[...]
+    dn = nt(all_low, wide[...])
+    wgrad[...] += tn(normed_all, all_low)
+    norm[0:1] += jnp.sum(dn * normed_all.astype(F32), axis=0, keepdims=True)
     dn_o[...] = dn.astype(BF16)
-    wgrad_o[...] += tn(normed[...], jnp.concatenate([dz_low, dv_low, ds_low], axis=1))
-
-    def unit_of(rows_in):
-        rows_in = rows_in.astype(F32)
-        return rows_in * lax.rsqrt(jnp.mean(rows_in * rows_in, axis=1, keepdims=True) + EPSILON)
-
-    norm_o[0:1] += jnp.sum(dn * unit_of(hidden[...]), axis=0, keepdims=True)
 
     @at.when_first
     def _():
         ahead[0:8] = jnp.zeros((8, CHAN), F32)
-        ahead[8:16] = dpre[0:8]
+        ahead[8:16] = ahead[BLOCK : BLOCK + 8]
         ahead[16:24] = jnp.zeros((8, CHAN), F32)
         pos = blk.start - 8 + iota((8, 1), 0)
         left = end_of(marks, pos) - pos
         back = jnp.zeros((8, CHAN), F32)
         for lag in range(1, CONV):
+            tap = 3 - lag
             same = (left > lag) & (pos >= 0)
-            back = back + taps[3 - lag : 4 - lag] * (
-                ahead[lag : lag + 8] * jnp.where(same, 1.0, 0.0)
-            )
-        low = jnp.concatenate([jnp.zeros((8, CHAN), F32), back], axis=0).astype(BF16)
-        given = nt(low[:, :WIDE], wv[...]) + nt(low[:, WIDE:], ws[...])
+            later_dpre = jnp.where(same, ahead[lag : lag + 8], 0.0)
+            chan[tap : tap + 1] += jnp.sum(later_dpre * cin_halo[...], axis=0, keepdims=True)
+            back = back + taps[tap : tap + 1] * later_dpre
+        spilled = jnp.concatenate([jnp.zeros((8, CHAN), F32), back], axis=0).astype(BF16)
+        given = nt(spilled, wide[:, WIDE:])
         spill_o[...] = given[8:16]
-        unit_halo = unit_of(halo[...])
-        norm_o[0:1] += jnp.sum(given[8:16] * unit_halo[8:16], axis=0, keepdims=True)
-        wgrad_o[:, WIDE:] += tn((unit_halo * gain[0:1]).astype(BF16), low)
-        big_o[:, 0 : 3 * WIDE] = wgrad_o[...].astype(BF16)
-        big_o[:, 3 * WIDE :] = grad_out_t[...].astype(BF16)
+        rows_in = halo[...].astype(F32)
+        scale = lax.rsqrt(jnp.mean(rows_in * rows_in, axis=1, keepdims=True) + EPSILON)
+        normed_halo = (rows_in * scale * gain[0:1]).astype(BF16)
+        norm[0:1] += jnp.sum(given * normed_halo.astype(F32), axis=0, keepdims=True)
+        wgrad[:, WIDE:] += tn(normed_halo, spilled)
+        early_o[...] = wgrad[:, WIDE:].astype(BF16)
+        late_o[...] = jnp.concatenate(
+            [wgrad[:, 0:INNER_DEV], grad_out_t[:, 0:INNER_DEV]], axis=1
+        ).astype(BF16)
+        gained = norm[0:1] / gain[0:1]
+
+        def beside(left, right):
+            return jnp.concatenate([left, right], axis=1)
+
         pack = jnp.concatenate(
             [
-                jnp.concatenate([chan_o[0:5], jnp.zeros((5, CHAN), F32)], axis=1),
-                jnp.concatenate([norm_o[0:1], step_o[8:9]], axis=1),
-                jnp.concatenate([gains[0:1], gains[1:2], step_o[9:10], step_o[10:11]], axis=1),
-                jnp.concatenate(
-                    [step_o[0:1], step_o[1:2], step_o[2:3], jnp.zeros((1, WIDE), F32)], axis=1
-                ),
+                chan[0:5],
+                gained[:, 0:CHAN],
+                beside(gained[:, CHAN:], gains[0:1]),
+                beside(gains[1:2], steps[8:9]),
+                beside(steps[9:10], steps[10:11]),
+                beside(steps[0:1], steps[1:2]),
+                beside(steps[2:3], jnp.zeros((1, WIDE), F32)),
+                jnp.zeros((5, CHAN), F32),
             ],
             axis=0,
         )
-        top = pack.astype(BF16).astype(F32)
-        pack_o[...] = jnp.concatenate([top, pack - top], axis=0).astype(BF16)
+        pack_o[...] = pack.astype(BF16)
+
+
+def copied_kernel(source, out, done):
+    copy = pltpu.make_async_copy(source, out, done)
+    copy.start()
+    copy.wait()
+
+
+def copied(values):
+    return pl.pallas_call(
+        copied_kernel,
+        in_specs=[pl.BlockSpec(memory_space=pl.ANY)],
+        out_specs=pl.BlockSpec(memory_space=pl.ANY),
+        out_shape=jax.ShapeDtypeStruct(values.shape, values.dtype),
+        scratch_shapes=[pltpu.SemaphoreType.DMA],
+        compiler_params=pltpu.CompilerParams(vmem_limit_bytes=VMEM_LIMIT),
+        cost_estimate=pl.CostEstimate(flops=int(2e9), bytes_accessed=int(6e6), transcendentals=0),
+    )(values)
 
 
 def passed_along(values, axis, by):
@@ -669,7 +689,9 @@
     )
     needed = handed_to_all(needed, CELLS).reshape(MODEL, 2 * WIDE)
     finishes = jnp.cumsum(lengths[0])
-    marks = jnp.concatenate([finishes, (ctx * tok)[None], jnp.zeros((3,), jnp.int32)])
+    marks = jnp.concatenate(
+        [finishes, jnp.stack([ctx * tok, 0 * ctx, 0 * ctx, 0 * ctx])]
+    )
     marks = marks.astype(jnp.int32)
     later = jnp.concatenate([padded(gate_proj, WIDE), padded(out_proj.T, WIDE)], axis=1)
     later = handed_to_all(later, CELLS)
@@ -721,7 +743,8 @@
     )
     sums = jnp.sum(handed_to_all(sums, "tensor"), axis=0)
 
-    own = tok // lax.axis_size("tensor")
+    ranks = lax.axis_size("tensor")
+    own = tok // ranks
     place = rank * own
     own_hidden = lax.dynamic_slice_in_dim(hidden, place, own, 0).astype(F32)
     own_cot = lax.dynamic_slice_in_dim(cotangent, place, own, 0).astype(F32)
@@ -757,28 +780,31 @@
     )
     dxi, own_out, messages = lax.optimization_barrier((dxi, own_out, messages))
     output = lax.all_gather(own_out, "tensor", axis=0, tiled=True)
-    dn, big, pack, spill = call(
+    dn, early, late, pack, spill = call(
         input_back_kernel, blocks, PARTS[5], True,
         [
-            SMEM, rows_of(MODEL), rows_of(MODEL), whole((16, MODEL)), rows_of(WIDE), rows_of(WIDE),
-            rows_of(WIDE), rows_of(CHAN), rows_of(CHAN), rows_of(CHAN), ("before", CHAN),
+            SMEM, ("tile", MODEL), whole((16, MODEL)), rows_of(WIDE), rows_of(WIDE),
+            rows_of(WIDE), rows_of(CHAN), rows_of(CHAN), rows_of(CHAN),
             whole((8, CHAN)), lanes_of(24), lanes_of(16), STATES, whole((STATE, WIDE)), STATES,
-            whole(STATE_DIMS), whole(STATE_DIMS), whole(STATE_DIMS), whole((8, MODEL)), pair, pair, whole((8, CHAN)),
-            whole((16, BLOCK)), whole((MODEL, WIDE)), whole((8, WIDE)),
-        ],
-        [
-            (rows_of(MODEL), BF16), (whole((MODEL, 4 * WIDE)), BF16),
-            (whole((16, 4 * WIDE)), BF16), (whole((8, MODEL)), F32),
-        ],
-        [
-            pltpu.VMEM((BLOCK + 8, CHAN), F32), pltpu.VMEM((BLOCK + 8, CHAN), F32),
-            pltpu.VMEM((STATE, WIDE), F32), pltpu.VMEM((BLOCK, BLOCK), BF16),
-            pltpu.VMEM((MODEL, 3 * WIDE), F32), pltpu.VMEM((8, CHAN), F32),
-            pltpu.VMEM((16, BLOCK), F32), pltpu.VMEM((8, MODEL), F32),
-        ],
-        22, marks, hidden, normed, halo, dz, dxi, dbc, xbc, slope, cin, cin, cin_halo,
-        rows, stats, states, prefix, reaches, *messages, gain, later, needed, taps, hcols, grad_out_t, gains,
-    )
+            whole(STATE_DIMS), whole(STATE_DIMS), whole(STATE_DIMS), whole((8, MODEL)), pair, pair,
+            whole((8, CHAN)), whole((16, BLOCK)), whole((MODEL, WIDE)), whole((8, WIDE)),
+        ],
+        [
+            (("tile", MODEL), BF16), (whole((MODEL, CHAN)), BF16),
+            (whole((MODEL, 2 * INNER_DEV)), BF16), (whole((16, CHAN)), BF16),
+            (whole((8, MODEL)), F32),
+        ],
+        [
+            pltpu.VMEM((BLOCK + 8, CHAN), F32), pltpu.VMEM((STATE, WIDE), F32),
+            pltpu.VMEM((BLOCK, BLOCK), BF16), pltpu.VMEM((MODEL, 3 * WIDE), F32),
+            pltpu.VMEM((8, CHAN), F32), pltpu.VMEM((16, BLOCK), F32), pltpu.VMEM((8, MODEL), F32),
+            pltpu.VMEM((PARTS[5] * BLOCK, 3 * WIDE), BF16), pltpu.VMEM((MODEL, 3 * WIDE), BF16),
+        ],
+        22, marks, normed, halo, dz, dxi, dbc, xbc, slope, cin, cin_halo,
+        rows, stats, states, prefix, reaches, *messages, gain, later, needed, taps, hcols,
+        grad_out_t, gains,
+    )
+
     arrived = passed_along(spill, "context", -1)
     end = dn[tok - 8 :].astype(F32) + arrived
     dn = lax.dynamic_update_slice(dn, end.astype(BF16), (tok - 8, 0))
@@ -786,15 +812,17 @@
     own_dn = lax.psum_scatter(dn, "tensor", scatter_dimension=0, tiled=True)
 
     cells = lax.axis_size("shard") * lax.axis_size("context")
-    big = jnp.concatenate(
-        [
-            big.reshape(cells, own_rows, 4 * WIDE),
+    early = jnp.concatenate(
+        [
+            early.reshape(cells, own_rows, CHAN),
             jnp.broadcast_to(pack[None], (cells,) + pack.shape),
         ],
         axis=1,
     )
-    big = jnp.sum(lax.all_to_all(big, CELLS, 0, 0, tiled=False).astype(F32), axis=0)
-    own_dn, big = lax.optimization_barrier((own_dn, big))
+    early = lax.all_to_all(early, CELLS, 0, 0, tiled=False)
+    output = copied(output)
+    own_dn, early, output = lax.optimization_barrier((own_dn, early, output))
+    early = jnp.sum(early.astype(F32), axis=0)
     own_dn = own_dn.astype(F32)
     scaling = lax.rsqrt(jnp.mean(own_hidden * own_hidden, axis=1, keepdims=True) + EPSILON)
     unit = own_hidden * scaling
@@ -802,20 +830,21 @@
     own_grad = own_cot + scaling * (
         scaled - unit * jnp.mean(scaled * unit, axis=1, keepdims=True)
     )
-    grad_hidden = lax.all_gather(own_grad.astype(BF16), "tensor", axis=0, tiled=True)
-
-    small = big[own_rows : own_rows + 8] + big[own_rows + 8 :]
-    big = big[:own_rows]
-    chan = small[:5, :CHAN]
-    norm_cells = small[5, :MODEL]
-    grad_mixer = small[6, :INNER_DEV]
-    grad_skip = jnp.sum(small[6, WIDE : WIDE + INNER_DEV].reshape(HEADS_DEV, HEADDIM), axis=1)
-    grad_step_bias = jnp.sum(small[7, : 3 * WIDE].reshape(HEADS_DEV, WIDE), axis=1)
-    grad_decay = jnp.stack(
-        [jnp.sum(small[5, MODEL:]), jnp.sum(small[6, 2 * WIDE : 3 * WIDE]), jnp.sum(small[6, 3 * WIDE :])]
-    )
+    own_grad, late = lax.optimization_barrier((own_grad.astype(BF16), late))
+    grad_hidden = lax.all_gather(own_grad, "tensor", axis=0, tiled=True)
+    late = lax.all_to_all(late.reshape(cells, own_rows, 2 * INNER_DEV), CELLS, 0, 0, tiled=False)
+    late = jnp.sum(late.astype(F32), axis=0)
+
+    big, small = early[:own_rows], early[own_rows:]
+    chan = small[:5]
+    norm_cells = jnp.concatenate([small[5], small[6, :WIDE]])
+    grad_mixer = small[6, WIDE : WIDE + INNER_DEV]
+    grad_skip = jnp.sum(small[7, :INNER_DEV].reshape(HEADS_DEV, HEADDIM), axis=1)
+    lines = jnp.sum(small[7:11].reshape(8, WIDE), axis=1)
+    grad_decay = lines[1:4]
+    grad_step_bias = lines[4:7]
     share = 2 * STATE // lax.axis_size("tensor")
-    shared = jnp.concatenate([big[:, 2 * WIDE : 3 * WIDE], chan[:, WIDE:]], axis=0)
+    shared = jnp.concatenate([big[:, WIDE:], chan[:, WIDE:]], axis=0)
     shared = shared.reshape(own_rows + 5, -1, share).transpose(1, 0, 2)
     shared = shared.reshape(shared.shape[0], -1)
     count = shared.shape[1]
@@ -829,10 +858,10 @@
         output,
         grad_hidden,
         final[count : count + MODEL],
+        late[:, :INNER_DEV],
         big[:, :INNER_DEV],
-        big[:, WIDE : WIDE + INNER_DEV],
         state_all[:own_rows],
-        big[:, WIDE + INNER_DEV : WIDE + INNER_DEV + HEADS_DEV],
+        big[:, INNER_DEV : INNER_DEV + HEADS_DEV],
         chan[:4, :INNER_DEV],
         state_all[own_rows : own_rows + 4],
         chan[4, :INNER_DEV],
@@ -841,7 +870,7 @@
         grad_decay,
         grad_skip,
         grad_mixer,
-        big[:, 3 * WIDE : 3 * WIDE + INNER_DEV].T,
+        late[:, INNER_DEV:].T,
     )
 
 

time: 244 us -> 313 us (1.28)
  Pallas kernels: 70.7 us -> 169 us
  waiting for transfers between devices: 62.2 us -> 36.1 us
  starting transfers between devices: 49.4 us -> 56.1 us
  other arithmetic: 18.2 us -> 12.4 us
    pallas_call x6 -> x7, Pallas kernels: 70.7 us -> 169 us  [the longest x1 96.4 us: copied(): pl.pallas_call(copied_kernel, in_specs=[pl.BlockSpec(memory_space=pl.ANY)...]
    all_to_all x1 -> x2, waiting for transfers between devices: 27.9 us -> 6.46 us  [the longest x1 6.46 us: body(): lax.all_to_all(late.reshape(cells, own_rows, 2 * INNER_DEV), CELLS, 0, 0,...]
    all_gather x1, waiting for transfers between devices: 6.81 us -> 0.01 us  [body(): grad_hidden = lax.all_gather(own_grad, 'tensor', axis=0, tiled=True)]
    all_to_all x1 -> x2, starting transfers between devices: 8.12 us -> 14.9 us  [the longest x1 7.66 us: body(): early = lax.all_to_all(early, CELLS, 0, 0, tiled=False)]
    unnamed x49 -> x42, local copies, waits for them, and re-layouts: 12.5 us -> 11.6 us
  transfers between devices with their start and end apart: 18 -> 19, of which waited for: 7 -> 7; matrix products, arithmetic and copies ran while one was open for 10% -> 6% of each run, Pallas kernels for 26% -> 52%
where the time goes in v3:
time: 313 us; the launch traced here: 311 us
  Pallas kernels  169 us (54%)
  starting transfers between devices  56.1 us (18%)
  waiting for transfers between devices  36.1 us (12%)
  local copies, waits for them, and re-layouts  23.5 us (8%)
  between operations  14.3 us (5%)
  other arithmetic  12.4 us (4%)
    pallas_call x1, Pallas kernels, copied(): pl.pallas_call(copied_kernel, in_specs=[pl.BlockSpec(memory_space=pl.ANY)...  96.4 us
    pallas_call x6, Pallas kernels, call(): pl.pallas_call(run, grid_spec=pltpu.PrefetchScalarGridSpec(num_scalar_pre...  72.4 us
    all_to_all x4, waiting for transfers between devices, handed_to_all(): lax.all_to_all(jnp.broadcast_to(values[None], (count,) + values.shape), a...  19.5 us
    all_to_all x4, starting transfers between devices, handed_to_all(): lax.all_to_all(jnp.broadcast_to(values[None], (count,) + values.shape), a...  19.4 us
    ppermute x8, starting transfers between devices, passed_along(): return lax.ppermute(values, axis, pairs)  18.1 us
    unnamed x42, local copies, waits for them, and re-layouts  11.6 us
    all_to_all x1, starting transfers between devices, body(): early = lax.all_to_all(early, CELLS, 0, 0, tiled=False)  7.66 us
    all_to_all x1, starting transfers between devices, body(): lax.all_to_all(late.reshape(cells, own_rows, 2 * INNER_DEV), CELLS, 0, 0,...  7.21 us
  transfers between devices with their start and end apart: 19, of which 7 were waited for; matrix products, arithmetic and copies ran while one was open for 6% of the time, Pallas kernels for 52%

profile of v3, /device:TPU:0, one launch (start us, length us, event | category | flops | bytes accessed | tf_op | source)
XLA Modules:
  0.0 311.3 jit_solution(11032796714576032121)
XLA Ops:
  7.2 0.7 convert_element_type.42
  7.9 0.8 copy.75
  8.7 0.7 copy.76
  9.6 0.8 reshape.159
  10.4 4.6 %all-to-all-start = ((f32[8,1,1792]{2,1,0:T(1,128)}), f32[8,1,1792]{2,1,0:T(1,128)S(1)}, u32[]{:S(2)}, u32[]{:S(2)}) async-start(f32[8,1,1792]{2,1,0:T(1,128)} %reshape.159), calls=%async_computation | async-start | bytes 114688 | tf_op jit(solution)/shard_map/all_to_all | solution.py:649
  14.9 0.8 copy.78
  15.7 0.7 slice.106
  16.5 4.0 %all-to-all-done = f32[8,1,1792]{2,1,0:T(1,128)S(1)} async-done(((f32[8,1,1792]{2,1,0:T(1,128)}), f32[8,1,1792]{2,1,0:T(1,128)S(1)}, u32[]{:S(2)}, u32[]{:S(2)}) %all-to-all-start) | async-done | bytes 57376 | tf_op jit(solution)/shard_map/all_to_all | solution.py:649
  21.0 0.8 reduce.8
  22.1 0.8 pad_maximum_fusion.2
  22.9 1.0 broadcast_in_dim.22
  23.8 7.9 %all-to-all-start.1 = ((bf16[16,48,512]{2,1,0:T(8,128)(2,1)}), bf16[16,48,512]{2,1,0:T(8,128)(2,1)S(1)}, u32[]{:S(2)}, u32[]{:S(2)}) async-start(bf16[16,48,512]{2,1,0:T(8,128)(2,1)} %broadcast_in_dim.22), calls=%async_computation.1 | async-start | bytes 1572864 | tf_op jit(solution)/shard_map/all_to_all | solution.py:649
  31.7 3.8 %collective-permute-start = (bf16[16,768]{1,0:T(8,128)(2,1)S(1)}, bf16[16,768]{1,0:T(8,128)(2,1)S(1)}, u32[]{:S(2)}, u32[]{:S(2)}) collective-permute-start(bf16[16,768]{1,0:T(8,128)(2,1)S(1)} %slice.106), channel_id=1, source_target_pairs={{0,8},{8,16},{16,24},{1,9},{9,17},{17,25},{2,10},{10,18},{18,26},{... | collective-permute-start | bytes 73736 | tf_op jit(solution)/shard_map/ppermute | solution.py:644
  35.8 0.6 pad_add_fusion.refs_0_
  36.5 0.7 copy.87.refs_11_
  37.2 8.8 %all-to-all-done.1 = bf16[16,48,512]{2,1,0:T(8,128)(2,1)S(1)} async-done(((bf16[16,48,512]{2,1,0:T(8,128)(2,1)}), bf16[16,48,512]{2,1,0:T(8,128)(2,1)S(1)}, u32[]{:S(2)}, u32[]{:S(2)}) %all-to-all-start.1) | async-done | bytes 786464 | tf_op jit(solution)/shard_map/all_to_all | solution.py:649
  46.0 1.0 broadcast_in_dim.23
  47.0 3.6 %all-to-all-start.2 = ((bf16[16,48,512]{2,1,0:T(8,128)(2,1)}), bf16[16,48,512]{2,1,0:T(8,128)(2,1)S(1)}, u32[]{:S(2)}, u32[]{:S(2)}) async-start(bf16[16,48,512]{2,1,0:T(8,128)(2,1)} %broadcast_in_dim.23), calls=%async_computation.2 | async-start | bytes 1572864 | tf_op jit(solution)/shard_map/all_to_all | solution.py:649
  50.7 0.6 copy-done.15
  51.3 13.5 %shard_map.288 = (bf16[2048,768]{1,0:T(8,128)(2,1)}, bf16[2048,512]{1,0:T(8,128)(2,1)}, bf16[2048,512]{1,0:T(8,128)(2,1)}, bf16[2048,512]{1,0:T(8,128)(2,1)}, f3...) custom-call(s32[8]{0:T(128)} %pad_add_fusion.refs_0_, ...), custom_call_target="tpu_custom_call" | custom-call | flops 16099999744 | bytes 14000000 | tf_op jit(solution)/shard_map/pallas_call | solution.py:234
  64.8 4.9 %collective-permute-start.3 = (f32[136,256]{1,0:T(8,128)}, f32[136,256]{1,0:T(8,128)S(1)}, u32[]{:S(2)}, u32[]{:S(2)}) collective-permute-start(f32[136,256]{1,0:T(8,128)} %get-tuple-element.84), channel_id=1, source_target_pairs={{0,24},{1,25},{2,26},{3,27},{4,28},{5,29},{6,30},{7,31},{32,56},{3... | collective-permute-start | bytes 417800 | tf_op jit(solution)/shard_map/ppermute | solution.py:644
  69.8 1.3 collective-permute-start.2
  71.1 2.8 collective-permute-start.1
  73.9 0.9 copy-done.1
  74.7 9.0 %shard_map.289 = (bf16[2048,256]{1,0:T(8,128)(2,1)}, bf16[2048,256]{1,0:T(8,128)(2,1)}, bf16[2048,256]{1,0:T(8,128)(2,1)}) custom-call(s32[8]{0:T(128)} %pad_add_fusion.refs_0_, bf16[2048,768]{1,0:T(8,128)(2,1)} %get-tuple-element.72.refs_1_, bf16[2048,768]{1,0:T(8,128)(2,1)} %refs_8_.3, bf16[768,512]{1,0:T(8,128)(2,1)} %bitcast.32, ...), custom_call_target="tpu_custom_call" | custom-call | flops 13799999488 | bytes 12000000 | tf_op jit(solution)/shard_map/pallas_call | solution.py:234
  83.8 0.6 copy-done.12
  84.6 8.3 %shard_map.290 = (bf16[2048,256]{1,0:T(8,128)(2,1)}, bf16[2048,256]{1,0:T(8,128)(2,1)}, bf16[2048,768]{1,0:T(8,128)(2,1)}, f32[2,2048]{1,0:T(2,128)}, f32[128,256]{1,0:T(8,128)}) custom-call(s32[8]{0:T(128)} %pad_add_fusion.refs_0_, bf16[2048,256]{1,0:T(8,128)(2,1)} %get-tuple-element.80.refs_1_, bf16[2048,256]{1,0:T(8,128)(2,1)} %get-tuple-element.81.refs_2_, ...), custom_call_target="tpu_custom_call" | custom-call | flops 11500000256 | bytes 10000000 | tf_op jit(solution)/shard_map/pallas_call | solution.py:234
  92.9 0.7 copy-done.8
  93.5 0.7 broadcast_in_dim.24
  94.2 3.4 %all-to-all-start.3 = ((f32[8,2,2048]{2,1,0:T(2,128)}), f32[8,2,2048]{2,1,0:T(2,128)S(1)}, u32[]{:S(2)}, u32[]{:S(2)}) async-start(f32[8,2,2048]{2,1,0:T(2,128)} %broadcast_in_dim.24), calls=%async_computation.3 | async-start | bytes 262144 | tf_op jit(solution)/shard_map/all_to_all | solution.py:649
  97.7 6.8 %all-to-all-done.3 = f32[8,2,2048]{2,1,0:T(2,128)S(1)} async-done(((f32[8,2,2048]{2,1,0:T(2,128)}), f32[8,2,2048]{2,1,0:T(2,128)S(1)}, u32[]{:S(2)}, u32[]{:S(2)}) %all-to-all-start.3) | async-done | bytes 131104 | tf_op jit(solution)/shard_map/all_to_all | solution.py:649
  104.5 0.6 copy-done.3
  105.1 7.9 %shard_map.291 = (bf16[2048,256]{1,0:T(8,128)(2,1)}, bf16[2048,256]{1,0:T(8,128)(2,1)}, f32[8,136,256]{2,1,0:T(8,128)}, f32[136,256]{1,0:T(8,128)}, f32[8,256]{1,0:T(8,128)}) custom-call(s32[8]{0:T(128)} %pad_add_fusion.refs_0_, bf16[2048,256]{1,0:T(8,128)(2,1)} %get-tuple-element.85.refs_1_, bf16[2048,256]{1,0:T(8,128)(2,1)} %get-tuple-element.81.refs_2_, ...), custom_call_target="tpu_custom_call" | custom-call | flops 10350000128 | bytes 9000000 | tf_op jit(solution)/shard_map/pallas_call | solution.py:234
  113.0 1.3 collective-permute-start.6
  114.3 1.3 collective-permute-start.5
  115.6 1.3 collective-permute-start.4
  116.9 13.1 %shard_map.292 = (bf16[2048,256]{1,0:T(8,128)(2,1)}, bf16[2048,256]{1,0:T(8,128)(2,1)}, f32[16,2048]{1,0:T(8,128)}, f32[768,256]{1,0:T(8,128)}) custom-call(s32[8]{0:T(128)} %pad_add_fusion.refs_0_, bf16[2048,256]{1,0:T(8,128)(2,1)} %get-tuple-element.88.refs_1_, bf16[2048,512]{1,0:T(8,128)(2,1)} %get-tuple-element.77.refs_4_.refs_2_.refs_6_, ...), custom_call_target="tpu_custom_call" | custom-call | flops 14949999616 | bytes 13000000 | tf_op jit(solution)/shard_map/pallas_call | solution.py:234
  130.1 2.1 fusion.8
  132.9 20.5 %shard_map.293 = (bf16[2048,768]{1,0:T(8,128)(2,1)}, bf16[768,512]{1,0:T(8,128)(2,1)}, bf16[768,384]{1,0:T(8,128)(2,1)}, bf16[16,512]{1,0:T(8,128)(2,1)}, f32[8,768]{1,0:T(8,128)}) custom-call(s32[8]{0:T(128)} %pad_add_fusion.refs_0_, bf16[2048,768]{1,0:T(8,128)(2,1)} %get-tuple-element.72.refs_1_, bf16[16,768]{1,0:T(8,128)(2,1)} %copy-done.15, ...), custom_call_target="tpu_custom_call" | custom-call | flops 25300000768 | bytes 22000000 | tf_op jit(solution)/shard_map/pallas_call | solution.py:234
  153.5 1.4 collective-permute-start.7
  154.9 5.3 %collective-permute-done.7 = f32[8,768]{1,0:T(8,128)S(1)} collective-permute-done((f32[8,768]{1,0:T(8,128)}, f32[8,768]{1,0:T(8,128)S(1)}, u32[]{:S(2)}, u32[]{:S(2)}) %collective-permute-start.7) | collective-permute-done | bytes 24608 | tf_op jit(solution)/shard_map/ppermute | solution.py:644
  160.2 1.3 fusion.12
  161.9 1.1 pad_maximum_fusion
  162.9 7.7 %all-to-all-start.4 = ((bf16[16,64,512]{2,1,0:T(8,128)(2,1)}), bf16[16,64,512]{2,1,0:T(8,128)(2,1)S(1)}, u32[]{:S(2)}, u32[]{:S(2)}) async-start(bf16[16,64,512]{2,1,0:T(8,128)(2,1)} %pad_maximum_fusion), calls=%async_computation.6 | async-start | bytes 2097152 | tf_op jit(solution)/shard_map/all_to_all | solution.py:822
  170.7 96.4 %shard_map.294 = bf16[2048,768]{1,0:T(8,128)(2,1)} custom-call(bf16[2048,768]{1,0:T(8,128)(2,1)} %all-gather.3.cloned.1.call-done.source), custom_call_target="tpu_custom_call" | custom-call | flops 2000000000 | bytes 6000000 | tf_op jit(solution)/shard_map/pallas_call | solution.py:630
  267.1 1.4 fusion.2
  268.5 2.3 fusion.6
  271.5 0.7 copy.83
  272.2 3.4 %all-to-all-start.5 = ((f32[8,20,128]{2,1,0:T(8,128)}), f32[8,20,128]{2,1,0:T(8,128)S(1)}, u32[]{:S(2)}, u32[]{:S(2)}) async-start(f32[8,20,128]{2,1,0:T(8,128)} %copy.83), calls=%async_computation.7 | async-start | bytes 196608 | tf_op jit(solution)/shard_map/all_to_all | solution.py:855
  275.5 0.6 slice.141
  276.2 0.6 slice.138
  276.8 4.4 %all-to-all-done.5 = f32[8,20,128]{2,1,0:T(8,128)S(1)} async-done(((f32[8,20,128]{2,1,0:T(8,128)}), f32[8,20,128]{2,1,0:T(8,128)S(1)}, u32[]{:S(2)}, u32[]{:S(2)}) %all-to-all-start.5) | async-done | bytes 81952 | tf_op jit(solution)/shard_map/all_to_all | solution.py:855
  281.2 7.2 %all-to-all-start.6 = ((bf16[16,48,384]{2,1,0:T(8,128)(2,1)}), bf16[16,48,384]{2,1,0:T(8,128)(2,1)S(1)}, u32[]{:S(2)}, u32[]{:S(2)}) async-start(bf16[16,48,384]{2,1,0:T(8,128)(2,1)} %bitcast.18), calls=%async_computation.8 | async-start | bytes 1179648 | tf_op jit(solution)/shard_map/all_to_all | solution.py:835
  288.5 0.6 fusion.13
  289.1 0.6 reduce_sum.79
  289.9 0.7 copy.85
  290.5 0.6 fusion.14
  291.1 0.5 slice.144
  291.6 0.7 slice.136
  292.3 0.7 slice.122
  293.1 0.7 copy.84
  293.8 6.5 %all-to-all-done.6 = bf16[16,48,384]{2,1,0:T(8,128)(2,1)S(1)} async-done(((bf16[16,48,384]{2,1,0:T(8,128)(2,1)}), bf16[16,48,384]{2,1,0:T(8,128)(2,1)S(1)}, u32[]{:S(2)}, u32[]{:S(2)}) %all-to-all-start.6) | async-done | bytes 589856 | tf_op jit(solution)/shard_map/all_to_all | solution.py:835
  300.3 0.7 slice_bitcast_fusion
  301.0 3.8 %copy.91 = bf16[2048,768]{1,0:T(8,128)(2,1)} copy(bf16[2048,768]{1,0:T(8,128)(2,1)} %all-gather.5.cloned.1.call-done) | data formatting | bytes 6291456
  (90 shorter events, 3.9 us)
Async XLA Ops:
  7.2 28.6 %copy-start.4 = (bf16[192,48]{0,1:T(8,128)(2,1)S(1)}, bf16[192,48]{0,1:T(8,128)(2,1)}, u32[]{:S(2)}) copy-start(bf16[192,48]{0,1:T(8,128)(2,1)} %param.33) | copy-start | bytes 55300
  7.2 28.6 %copy-start.5 = (bf16[48,192]{1,0:T(8,128)(2,1)S(1)}, bf16[48,192]{1,0:T(8,128)(2,1)}, u32[]{:S(2)}) copy-start(bf16[48,192]{1,0:T(8,128)(2,1)} %param.21) | copy-start | bytes 55300
  7.2 28.4 %copy-start.16 = (s32[1,4]{1,0:T(1,128)S(1)}, s32[1,4]{1,0:T(1,128)}, u32[]{:S(2)}) copy-start(s32[1,4]{1,0:T(1,128)} %param.19) | copy-start | bytes 52
  10.4 10.1 %all-to-all-start = ((f32[8,1,1792]{2,1,0:T(1,128)}), f32[8,1,1792]{2,1,0:T(1,128)S(1)}, u32[]{:S(2)}, u32[]{:S(2)}) async-start(f32[8,1,1792]{2,1,0:T(1,128)} %reshape.159), calls=%async_computation | async-start | bytes 114688 | tf_op jit(solution)/shard_map/all_to_all | solution.py:649
  23.8 22.1 %all-to-all-start.1 = ((bf16[16,48,512]{2,1,0:T(8,128)(2,1)}), bf16[16,48,512]{2,1,0:T(8,128)(2,1)S(1)}, u32[]{:S(2)}, u32[]{:S(2)}) async-start(bf16[16,48,512]{2,1,0:T(8,128)(2,1)} %broadcast_in_dim.22), calls=%async_computation.1 | async-start | bytes 1572864 | tf_op jit(solution)/shard_map/all_to_all | solution.py:649
  31.7 18.9 %collective-permute-start = (bf16[16,768]{1,0:T(8,128)(2,1)S(1)}, bf16[16,768]{1,0:T(8,128)(2,1)S(1)}, u32[]{:S(2)}, u32[]{:S(2)}) collective-permute-start(bf16[16,768]{1,0:T(8,128)(2,1)S(1)} %slice.106), channel_id=1, source_target_pairs={{0,8},{8,16},{16,24},{1,9},{9,17},{17,25},{2,10},{10,18},{18,26},{... | collective-permute-start | bytes 73736 | tf_op jit(solution)/shard_map/ppermute | solution.py:644
  45.9 4.7 %copy-start = (bf16[16,48,512]{2,1,0:T(8,128)(2,1)}, bf16[16,48,512]{2,1,0:T(8,128)(2,1)S(1)}, u32[]{:S(2)}) copy-start(bf16[16,48,512]{2,1,0:T(8,128)(2,1)S(1)} %all-to-all-done.1) | copy-start | bytes 2359300
  47.0 26.9 %all-to-all-start.2 = ((bf16[16,48,512]{2,1,0:T(8,128)(2,1)}), bf16[16,48,512]{2,1,0:T(8,128)(2,1)S(1)}, u32[]{:S(2)}, u32[]{:S(2)}) async-start(bf16[16,48,512]{2,1,0:T(8,128)(2,1)} %broadcast_in_dim.23), calls=%async_computation.2 | async-start | bytes 1572864 | tf_op jit(solution)/shard_map/all_to_all | solution.py:649
  50.6 79.5 %reduce-scatter.3.cloned.1.call-start = ((), (), s32[]{:S(2)}) async-start(), calls=%async_computation.9 | async-start | bytes 3538944 | tf_op jit(solution)/shard_map/reduce_scatter | solution.py:752
  50.7 0.6 copy-start.15
  64.8 18.9 %collective-permute-start.3 = (f32[136,256]{1,0:T(8,128)}, f32[136,256]{1,0:T(8,128)S(1)}, u32[]{:S(2)}, u32[]{:S(2)}) collective-permute-start(f32[136,256]{1,0:T(8,128)} %get-tuple-element.84), channel_id=1, source_target_pairs={{0,24},{1,25},{2,26},{3,27},{4,28},{5,29},{6,30},{7,31},{32,56},{3... | collective-permute-start | bytes 417800 | tf_op jit(solution)/shard_map/ppermute | solution.py:644
  69.8 14.0 %collective-permute-start.2 = (f32[136,256]{1,0:T(8,128)}, f32[136,256]{1,0:T(8,128)S(1)}, u32[]{:S(2)}, u32[]{:S(2)}) collective-permute-start(f32[136,256]{1,0:T(8,128)} %get-tuple-element.84), channel_id=1, source_target_pairs={{0,16},{8,24},{1,17},{9,25},{2,18},{10,26},{3,19},{11,27},{4,20},{... | collective-permute-start | bytes 417800 | tf_op jit(solution)/shard_map/ppermute | solution.py:644
  71.1 12.7 %collective-permute-start.1 = (f32[136,256]{1,0:T(8,128)}, f32[136,256]{1,0:T(8,128)S(1)}, u32[]{:S(2)}, u32[]{:S(2)}) collective-permute-start(f32[136,256]{1,0:T(8,128)} %get-tuple-element.84), channel_id=1, source_target_pairs={{0,8},{8,16},{16,24},{1,9},{9,17},{17,25},{2,10},{10,18},{18,26},{... | collective-permute-start | bytes 417800 | tf_op jit(solution)/shard_map/ppermute | solution.py:644
  73.8 0.9 copy-start.1
  83.8 0.7 copy-start.12
  83.8 0.7 copy-start.13
  83.8 0.8 copy-start.14
  92.8 0.7 copy-start.8
  94.2 10.2 %all-to-all-start.3 = ((f32[8,2,2048]{2,1,0:T(2,128)}), f32[8,2,2048]{2,1,0:T(2,128)S(1)}, u32[]{:S(2)}, u32[]{:S(2)}) async-start(f32[8,2,2048]{2,1,0:T(2,128)} %broadcast_in_dim.24), calls=%async_computation.3 | async-start | bytes 262144 | tf_op jit(solution)/shard_map/all_to_all | solution.py:649
  97.6 64.2 %all-gather.3.cloned.1.call-start = ((), (), s32[]{:S(2)}) async-start(), calls=%async_computation.10 | async-start | bytes 3538944 | tf_op jit(solution)/shard_map/all_gather | solution.py:782
  104.5 0.6 copy-start.3
  113.0 19.1 %collective-permute-start.6 = (f32[136,256]{1,0:T(8,128)}, f32[136,256]{1,0:T(8,128)S(1)}, u32[]{:S(2)}, u32[]{:S(2)}) collective-permute-start(f32[136,256]{1,0:T(8,128)} %get-tuple-element.93), channel_id=1, source_target_pairs={{24,0},{25,1},{26,2},{27,3},{28,4},{29,5},{30,6},{31,7},{56,32},{5... | collective-permute-start | bytes 417800 | tf_op jit(solution)/shard_map/ppermute | solution.py:644
  114.3 17.8 %collective-permute-start.5 = (f32[136,256]{1,0:T(8,128)}, f32[136,256]{1,0:T(8,128)S(1)}, u32[]{:S(2)}, u32[]{:S(2)}) collective-permute-start(f32[136,256]{1,0:T(8,128)} %get-tuple-element.93), channel_id=1, source_target_pairs={{16,0},{24,8},{17,1},{25,9},{18,2},{26,10},{19,3},{27,11},{20,4},{... | collective-permute-start | bytes 417800 | tf_op jit(solution)/shard_map/ppermute | solution.py:644
  115.6 16.6 %collective-permute-start.4 = (f32[136,256]{1,0:T(8,128)}, f32[136,256]{1,0:T(8,128)S(1)}, u32[]{:S(2)}, u32[]{:S(2)}) collective-permute-start(f32[136,256]{1,0:T(8,128)} %get-tuple-element.93), channel_id=1, source_target_pairs={{8,0},{16,8},{24,16},{9,1},{17,9},{25,17},{10,2},{18,10},{26,18},{... | collective-permute-start | bytes 417800 | tf_op jit(solution)/shard_map/ppermute | solution.py:644
  132.1 0.7 copy-start.9
  132.1 0.7 copy-start.10
  132.2 0.7 copy-start.11
  132.2 134.9 %reduce-scatter.5.cloned.1.call-start = ((), (), s32[]{:S(2)}) async-start(), calls=%async_computation.11 | async-start | bytes 3538944 | tf_op jit(solution)/shard_map/reduce_scatter | solution.py:812
  153.4 8.4 %copy-start.7 = (bf16[16,512]{1,0:T(8,128)(2,1)S(1)}, bf16[16,512]{1,0:T(8,128)(2,1)}, u32[]{:S(2)}) copy-start(bf16[16,512]{1,0:T(8,128)(2,1)} %get-tuple-element.114) | copy-start | bytes 49156
  153.5 8.4 %copy-start.2 = (bf16[768,512]{1,0:T(8,128)(2,1)S(1)}, bf16[768,512]{1,0:T(8,128)(2,1)}, u32[]{:S(2)}) copy-start(bf16[768,512]{1,0:T(8,128)(2,1)} %get-tuple-element.113) | copy-start | bytes 2359300
  153.5 6.7 %collective-permute-start.7 = (f32[8,768]{1,0:T(8,128)}, f32[8,768]{1,0:T(8,128)S(1)}, u32[]{:S(2)}, u32[]{:S(2)}) collective-permute-start(f32[8,768]{1,0:T(8,128)} %get-tuple-element.110), channel_id=1, source_target_pairs={{8,0},{16,8},{24,16},{9,1},{17,9},{25,17},{10,2},{18,10},{26,18},{... | collective-permute-start | bytes 73736 | tf_op jit(solution)/shard_map/ppermute | solution.py:644
  162.9 104.2 %all-to-all-start.4 = ((bf16[16,64,512]{2,1,0:T(8,128)(2,1)}), bf16[16,64,512]{2,1,0:T(8,128)(2,1)S(1)}, u32[]{:S(2)}, u32[]{:S(2)}) async-start(bf16[16,64,512]{2,1,0:T(8,128)(2,1)} %pad_maximum_fusion), calls=%async_computation.6 | async-start | bytes 2097152 | tf_op jit(solution)/shard_map/all_to_all | solution.py:822
  170.6 130.4 %all-gather.5.cloned.1.call-start = ((), (), s32[]{:S(2)}) async-start(), calls=%async_computation.12 | async-start | bytes 3538944 | tf_op jit(solution)/shard_map/all_gather | solution.py:834
  170.7 96.5 %copy-start.6 = (f32[768]{0:T(1024)S(1)}, f32[768]{0:T(1024)}, u32[]{:S(2)}) copy-start(f32[768]{0:T(1024)} %refs_6_.1) | copy-start | bytes 9220
  272.2 9.1 %all-to-all-start.5 = ((f32[8,20,128]{2,1,0:T(8,128)}), f32[8,20,128]{2,1,0:T(8,128)S(1)}, u32[]{:S(2)}, u32[]{:S(2)}) async-start(f32[8,20,128]{2,1,0:T(8,128)} %copy.83), calls=%async_computation.7 | async-start | bytes 196608 | tf_op jit(solution)/shard_map/all_to_all | solution.py:855
  281.2 19.0 %all-to-all-start.6 = ((bf16[16,48,384]{2,1,0:T(8,128)(2,1)}), bf16[16,48,384]{2,1,0:T(8,128)(2,1)S(1)}, u32[]{:S(2)}, u32[]{:S(2)}) async-start(bf16[16,48,384]{2,1,0:T(8,128)(2,1)} %bitcast.18), calls=%async_computation.8 | async-start | bytes 1179648 | tf_op jit(solution)/shard_map/all_to_all | solution.py:835
Sparse Core Ops, SparseCore 0:
  93.0 34.3 reduce-scatter.2
  132.3 29.4 all-gather.2
  164.2 36.0 reduce-scatter.4
  270.9 27.4 all-gather.4

commit v4 on v3

--- a/solution.py
+++ b/solution.py
@@ -195,12 +195,12 @@
         if what == "smem":
             return pl.BlockSpec(memory_space=pltpu.SMEM)
         if what in ("rows", "tile"):
-            return pl.BlockSpec((tile, kind[1]), lambda s, marks: (step(s), 0))
+            return pl.BlockSpec((tile, kind[1]), lambda s: (step(s), 0))
         if what == "lanes":
-            return pl.BlockSpec((kind[1], tile), lambda s, marks: (0, step(s)))
+            return pl.BlockSpec((kind[1], tile), lambda s: (0, step(s)))
         if what == "states":
-            return pl.BlockSpec((parts,) + STATE_DIMS, lambda s, marks: (step(s), 0, 0))
-        return pl.BlockSpec(kind[1], lambda s, marks: (0,) * len(kind[1]))
+            return pl.BlockSpec((parts,) + STATE_DIMS, lambda s: (step(s), 0, 0))
+        return pl.BlockSpec(kind[1], lambda s: (0,) * len(kind[1]))
 
     def view(refs, n, kind, k):
         ref = refs[n]
@@ -233,13 +233,10 @@
 
     return pl.pallas_call(
         run,
-        grid_spec=pltpu.PrefetchScalarGridSpec(
-            num_scalar_prefetch=1,
-            grid=(steps,),
-            in_specs=[spec(kind) for kind in ins[1:]],
-            out_specs=[spec(kind) for kind, _ in outs],
-            scratch_shapes=scratch,
-        ),
+        grid=(steps,),
+        in_specs=[spec(kind) for kind in ins],
+        out_specs=[spec(kind) for kind, _ in outs],
+        scratch_shapes=scratch,
         out_shape=[jax.ShapeDtypeStruct(dims(kind), dtype) for kind, dtype in outs],
         compiler_params=pltpu.CompilerParams(
             dimension_semantics=("arbitrary",), vmem_limit_bytes=VMEM_LIMIT
@@ -620,21 +617,23 @@
         pack_o[...] = pack.astype(BF16)
 
 
-def copied_kernel(source, out, done):
-    copy = pltpu.make_async_copy(source, out, done)
-    copy.start()
-    copy.wait()
+def copied_kernel(source, out):
+    out[...] = source[...]
 
 
 def copied(values):
+    rows, width = values.shape
+    block = pl.BlockSpec((rows // 4, width), lambda s: (s, 0))
     return pl.pallas_call(
         copied_kernel,
-        in_specs=[pl.BlockSpec(memory_space=pl.ANY)],
-        out_specs=pl.BlockSpec(memory_space=pl.ANY),
+        grid=(4,),
+        in_specs=[block],
+        out_specs=block,
         out_shape=jax.ShapeDtypeStruct(values.shape, values.dtype),
-        scratch_shapes=[pltpu.SemaphoreType.DMA],
-        compiler_params=pltpu.CompilerParams(vmem_limit_bytes=VMEM_LIMIT),
-        cost_estimate=pl.CostEstimate(flops=int(2e9), bytes_accessed=int(6e6), transcendentals=0),
+        compiler_params=pltpu.CompilerParams(
+            dimension_semantics=("arbitrary",), vmem_limit_bytes=VMEM_LIMIT
+        ),
+        cost_estimate=pl.CostEstimate(flops=int(3e9), bytes_accessed=int(6e6), transcendentals=0),
     )(values)
 
 

time: 313 us -> 243 us (0.78)
  Pallas kernels: 169 us -> 72.9 us
  waiting for transfers between devices: 36.1 us -> 62.7 us
    pallas_call x7, Pallas kernels: 169 us -> 72.9 us  [the longest x6 68.6 us: call(): pl.pallas_call(run, grid=(steps,), in_specs=[spec(kind) for kind in ins],...]
    all_to_all x1, waiting for transfers between devices: 0.01 us -> 13.7 us  [body(): early = lax.all_to_all(early, CELLS, 0, 0, tiled=False)]
    reduce_scatter x1, waiting for transfers between devices: 0.02 us -> 12.2 us  [body(): own_dn = lax.psum_scatter(dn, 'tensor', scatter_dimension=0, tiled=True)]
  transfers between devices with their start and end apart: 19 -> 19, of which waited for: 7 -> 9; matrix products, arithmetic and copies ran while one was open for 6% -> 7% of each run, Pallas kernels for 52% -> 27%
where the time goes in v4:
time: 243 us; the launch traced here: 241 us
  Pallas kernels  72.9 us (30%)
  waiting for transfers between devices  62.7 us (26%)
  starting transfers between devices  55.2 us (23%)
  local copies, waits for them, and re-layouts  23.5 us (10%)
  between operations  14.3 us (6%)
  other arithmetic  12.4 us (5%)
    pallas_call x6, Pallas kernels, call(): pl.pallas_call(run, grid=(steps,), in_specs=[spec(kind) for kind in ins],...  68.6 us
    all_to_all x4, waiting for transfers between devices, handed_to_all(): lax.all_to_all(jnp.broadcast_to(values[None], (count,) + values.shape), a...  19.5 us
    all_to_all x4, starting transfers between devices, handed_to_all(): lax.all_to_all(jnp.broadcast_to(values[None], (count,) + values.shape), a...  19.4 us
    ppermute x8, starting transfers between devices, passed_along(): return lax.ppermute(values, axis, pairs)  18.1 us
    all_to_all x1, waiting for transfers between devices, body(): early = lax.all_to_all(early, CELLS, 0, 0, tiled=False)  13.7 us
    reduce_scatter x1, waiting for transfers between devices, body(): own_dn = lax.psum_scatter(dn, 'tensor', scatter_dimension=0, tiled=True)  12.2 us
    unnamed x42, local copies, waits for them, and re-layouts  11.6 us
    all_to_all x1, starting transfers between devices, body(): early = lax.all_to_all(early, CELLS, 0, 0, tiled=False)  7.01 us
  transfers between devices with their start and end apart: 19, of which 9 were waited for; matrix products, arithmetic and copies ran while one was open for 7% of the time, Pallas kernels for 27%

profile of v4, /device:TPU:0, one launch (start us, length us, event | category | flops | bytes accessed | tf_op | source)
XLA Modules:
  0.0 241.0 jit_solution(13413734284329212125)
XLA Ops:
  7.2 0.7 convert_element_type.42
  7.9 0.8 copy.75
  8.7 0.7 copy.76
  9.6 0.8 reshape.159
  10.4 4.6 %all-to-all-start = ((f32[8,1,1792]{2,1,0:T(1,128)}), f32[8,1,1792]{2,1,0:T(1,128)S(1)}, u32[]{:S(2)}, u32[]{:S(2)}) async-start(f32[8,1,1792]{2,1,0:T(1,128)} %reshape.159), calls=%async_computation | async-start | bytes 114688 | tf_op jit(solution)/shard_map/all_to_all | solution.py:648
  14.9 0.8 copy.78
  15.7 0.7 slice.106
  16.5 4.0 %all-to-all-done = f32[8,1,1792]{2,1,0:T(1,128)S(1)} async-done(((f32[8,1,1792]{2,1,0:T(1,128)}), f32[8,1,1792]{2,1,0:T(1,128)S(1)}, u32[]{:S(2)}, u32[]{:S(2)}) %all-to-all-start) | async-done | bytes 57376 | tf_op jit(solution)/shard_map/all_to_all | solution.py:648
  21.0 0.8 reduce.8
  22.1 0.8 pad_maximum_fusion.2
  22.9 1.0 broadcast_in_dim.22
  23.8 7.9 %all-to-all-start.1 = ((bf16[16,48,512]{2,1,0:T(8,128)(2,1)}), bf16[16,48,512]{2,1,0:T(8,128)(2,1)S(1)}, u32[]{:S(2)}, u32[]{:S(2)}) async-start(bf16[16,48,512]{2,1,0:T(8,128)(2,1)} %broadcast_in_dim.22), calls=%async_computation.1 | async-start | bytes 1572864 | tf_op jit(solution)/shard_map/all_to_all | solution.py:648
  31.7 3.8 %collective-permute-start = (bf16[16,768]{1,0:T(8,128)(2,1)S(1)}, bf16[16,768]{1,0:T(8,128)(2,1)S(1)}, u32[]{:S(2)}, u32[]{:S(2)}) collective-permute-start(bf16[16,768]{1,0:T(8,128)(2,1)S(1)} %slice.106), channel_id=1, source_target_pairs={{0,8},{8,16},{16,24},{1,9},{9,17},{17,25},{2,10},{10,18},{18,26},{... | collective-permute-start | bytes 73736 | tf_op jit(solution)/shard_map/ppermute | solution.py:643
  35.8 0.6 pad_add_fusion.refs_0_
  36.5 0.7 copy.87.refs_11_
  37.2 8.8 %all-to-all-done.1 = bf16[16,48,512]{2,1,0:T(8,128)(2,1)S(1)} async-done(((bf16[16,48,512]{2,1,0:T(8,128)(2,1)}), bf16[16,48,512]{2,1,0:T(8,128)(2,1)S(1)}, u32[]{:S(2)}, u32[]{:S(2)}) %all-to-all-start.1) | async-done | bytes 786464 | tf_op jit(solution)/shard_map/all_to_all | solution.py:648
  46.0 1.0 broadcast_in_dim.23
  47.0 3.6 %all-to-all-start.2 = ((bf16[16,48,512]{2,1,0:T(8,128)(2,1)}), bf16[16,48,512]{2,1,0:T(8,128)(2,1)S(1)}, u32[]{:S(2)}, u32[]{:S(2)}) async-start(bf16[16,48,512]{2,1,0:T(8,128)(2,1)} %broadcast_in_dim.23), calls=%async_computation.2 | async-start | bytes 1572864 | tf_op jit(solution)/shard_map/all_to_all | solution.py:648
  50.7 0.6 copy-done.15
  51.3 12.9 %shard_map.288 = (bf16[2048,768]{1,0:T(8,128)(2,1)}, bf16[2048,512]{1,0:T(8,128)(2,1)}, bf16[2048,512]{1,0:T(8,128)(2,1)}, bf16[2048,512]{1,0:T(8,128)(2,1)}, f3...) custom-call(s32[8]{0:T(128)} %pad_add_fusion.refs_0_, ...), custom_call_target="tpu_custom_call" | custom-call | flops 16099999744 | bytes 14000000 | tf_op jit(solution)/shard_map/pallas_call | solution.py:234
  64.1 4.9 %collective-permute-start.3 = (f32[136,256]{1,0:T(8,128)}, f32[136,256]{1,0:T(8,128)S(1)}, u32[]{:S(2)}, u32[]{:S(2)}) collective-permute-start(f32[136,256]{1,0:T(8,128)} %get-tuple-element.84), channel_id=1, source_target_pairs={{0,24},{1,25},{2,26},{3,27},{4,28},{5,29},{6,30},{7,31},{32,56},{3... | collective-permute-start | bytes 417800 | tf_op jit(solution)/shard_map/ppermute | solution.py:643
  69.1 1.3 collective-permute-start.2
  70.4 2.8 %collective-permute-start.1 = (f32[136,256]{1,0:T(8,128)}, f32[136,256]{1,0:T(8,128)S(1)}, u32[]{:S(2)}, u32[]{:S(2)}) collective-permute-start(f32[136,256]{1,0:T(8,128)} %get-tuple-element.84), channel_id=1, source_target_pairs={{0,8},{8,16},{16,24},{1,9},{9,17},{17,25},{2,10},{10,18},{18,26},{... | collective-permute-start | bytes 417800 | tf_op jit(solution)/shard_map/ppermute | solution.py:643
  73.2 0.9 copy-done.1
  74.1 8.2 %shard_map.289 = (bf16[2048,256]{1,0:T(8,128)(2,1)}, bf16[2048,256]{1,0:T(8,128)(2,1)}, bf16[2048,256]{1,0:T(8,128)(2,1)}) custom-call(s32[8]{0:T(128)} %pad_add_fusion.refs_0_, bf16[2048,768]{1,0:T(8,128)(2,1)} %get-tuple-element.72.refs_1_, bf16[2048,768]{1,0:T(8,128)(2,1)} %refs_8_.3, bf16[768,512]{1,0:T(8,128)(2,1)} %bitcast.32, ...), custom_call_target="tpu_custom_call" | custom-call | flops 13799999488 | bytes 12000000 | tf_op jit(solution)/shard_map/pallas_call | solution.py:234
  82.3 0.6 copy-done.12
  83.0 7.6 %shard_map.290 = (bf16[2048,256]{1,0:T(8,128)(2,1)}, bf16[2048,256]{1,0:T(8,128)(2,1)}, bf16[2048,768]{1,0:T(8,128)(2,1)}, f32[2,2048]{1,0:T(2,128)}, f32[128,256]{1,0:T(8,128)}) custom-call(s32[8]{0:T(128)} %pad_add_fusion.refs_0_, bf16[2048,256]{1,0:T(8,128)(2,1)} %get-tuple-element.80.refs_1_, bf16[2048,256]{1,0:T(8,128)(2,1)} %get-tuple-element.81.refs_2_, ...), custom_call_target="tpu_custom_call" | custom-call | flops 11500000256 | bytes 10000000 | tf_op jit(solution)/shard_map/pallas_call | solution.py:234
  90.7 0.7 copy-done.8
  91.4 0.7 broadcast_in_dim.24
  92.0 3.4 %all-to-all-start.3 = ((f32[8,2,2048]{2,1,0:T(2,128)}), f32[8,2,2048]{2,1,0:T(2,128)S(1)}, u32[]{:S(2)}, u32[]{:S(2)}) async-start(f32[8,2,2048]{2,1,0:T(2,128)} %broadcast_in_dim.24), calls=%async_computation.3 | async-start | bytes 262144 | tf_op jit(solution)/shard_map/all_to_all | solution.py:648
  95.5 6.8 %all-to-all-done.3 = f32[8,2,2048]{2,1,0:T(2,128)S(1)} async-done(((f32[8,2,2048]{2,1,0:T(2,128)}), f32[8,2,2048]{2,1,0:T(2,128)S(1)}, u32[]{:S(2)}, u32[]{:S(2)}) %all-to-all-start.3) | async-done | bytes 131104 | tf_op jit(solution)/shard_map/all_to_all | solution.py:648
  102.9 7.3 %shard_map.291 = (bf16[2048,256]{1,0:T(8,128)(2,1)}, bf16[2048,256]{1,0:T(8,128)(2,1)}, f32[8,136,256]{2,1,0:T(8,128)}, f32[136,256]{1,0:T(8,128)}, f32[8,256]{1,0:T(8,128)}) custom-call(s32[8]{0:T(128)} %pad_add_fusion.refs_0_, bf16[2048,256]{1,0:T(8,128)(2,1)} %get-tuple-element.85.refs_1_, bf16[2048,256]{1,0:T(8,128)(2,1)} %get-tuple-element.81.refs_2_, ...), custom_call_target="tpu_custom_call" | custom-call | flops 10350000128 | bytes 9000000 | tf_op jit(solution)/shard_map/pallas_call | solution.py:234
  110.2 1.3 collective-permute-start.6
  111.5 1.3 collective-permute-start.5
  112.8 1.3 collective-permute-start.4
  114.1 12.7 %shard_map.292 = (bf16[2048,256]{1,0:T(8,128)(2,1)}, bf16[2048,256]{1,0:T(8,128)(2,1)}, f32[16,2048]{1,0:T(8,128)}, f32[768,256]{1,0:T(8,128)}) custom-call(s32[8]{0:T(128)} %pad_add_fusion.refs_0_, bf16[2048,256]{1,0:T(8,128)(2,1)} %get-tuple-element.88.refs_1_, bf16[2048,512]{1,0:T(8,128)(2,1)} %get-tuple-element.77.refs_4_.refs_2_.refs_6_, ...), custom_call_target="tpu_custom_call" | custom-call | flops 14949999616 | bytes 13000000 | tf_op jit(solution)/shard_map/pallas_call | solution.py:234
  126.9 2.1 fusion.8
  129.7 19.9 %shard_map.293 = (bf16[2048,768]{1,0:T(8,128)(2,1)}, bf16[768,512]{1,0:T(8,128)(2,1)}, bf16[768,384]{1,0:T(8,128)(2,1)}, bf16[16,512]{1,0:T(8,128)(2,1)}, f32[8,768]{1,0:T(8,128)}) custom-call(s32[8]{0:T(128)} %pad_add_fusion.refs_0_, bf16[2048,768]{1,0:T(8,128)(2,1)} %get-tuple-element.72.refs_1_, bf16[16,768]{1,0:T(8,128)(2,1)} %copy-done.15, ...), custom_call_target="tpu_custom_call" | custom-call | flops 25300000768 | bytes 22000000 | tf_op jit(solution)/shard_map/pallas_call | solution.py:234
  149.6 1.4 collective-permute-start.7
  151.1 5.3 %collective-permute-done.7 = f32[8,768]{1,0:T(8,128)S(1)} collective-permute-done((f32[8,768]{1,0:T(8,128)}, f32[8,768]{1,0:T(8,128)S(1)}, u32[]{:S(2)}, u32[]{:S(2)}) %collective-permute-start.7) | collective-permute-done | bytes 24608 | tf_op jit(solution)/shard_map/ppermute | solution.py:643
  156.3 1.3 fusion.12
  157.6 1.0 all-gather.3.cloned.1.call-done.source
  158.7 1.1 pad_maximum_fusion
  159.7 7.0 %all-to-all-start.4 = ((bf16[16,64,512]{2,1,0:T(8,128)(2,1)}), bf16[16,64,512]{2,1,0:T(8,128)(2,1)S(1)}, u32[]{:S(2)}, u32[]{:S(2)}) async-start(bf16[16,64,512]{2,1,0:T(8,128)(2,1)} %pad_maximum_fusion), calls=%async_computation.6 | async-start | bytes 2097152 | tf_op jit(solution)/shard_map/all_to_all | solution.py:821
  166.8 4.3 %shard_map.294 = bf16[2048,768]{1,0:T(8,128)(2,1)} custom-call(bf16[2048,768]{1,0:T(8,128)(2,1)} %all-gather.3.cloned.1.call-done.source), custom_call_target="tpu_custom_call" | custom-call | flops 3000000000 | bytes 6000000 | tf_op jit(solution)/shard_map/pallas_call | solution.py:627
  171.2 13.7 %all-to-all-done.4 = bf16[16,64,512]{2,1,0:T(8,128)(2,1)S(1)} async-done(((bf16[16,64,512]{2,1,0:T(8,128)(2,1)}), bf16[16,64,512]{2,1,0:T(8,128)(2,1)S(1)}, u32[]{:S(2)}, u32[]{:S(2)}) %all-to-all-start.4) | async-done | bytes 1048608 | tf_op jit(solution)/shard_map/all_to_all | solution.py:821
  184.9 12.2 %reduce-scatter.5.cloned.1.call-done = bf16[256,768]{1,0:T(8,128)(2,1)} async-done(((bf16[2048,768]{1,0:T(8,128)(2,1)}), bf16[256,768]{1,0:T(8,128)(2,1)}) %reduce-scatter.5.cloned.1.call-update) | async-done | bytes 393232 | tf_op jit(solution)/shard_map/reduce_scatter | solution.py:811
  197.1 1.4 fusion.2
  198.5 2.3 fusion.6
  201.5 0.7 copy.83
  202.1 3.4 %all-to-all-start.5 = ((f32[8,20,128]{2,1,0:T(8,128)}), f32[8,20,128]{2,1,0:T(8,128)S(1)}, u32[]{:S(2)}, u32[]{:S(2)}) async-start(f32[8,20,128]{2,1,0:T(8,128)} %copy.83), calls=%async_computation.7 | async-start | bytes 196608 | tf_op jit(solution)/shard_map/all_to_all | solution.py:854
  205.5 0.6 slice.141
  206.2 0.6 slice.138
  206.8 4.4 %all-to-all-done.5 = f32[8,20,128]{2,1,0:T(8,128)S(1)} async-done(((f32[8,20,128]{2,1,0:T(8,128)}), f32[8,20,128]{2,1,0:T(8,128)S(1)}, u32[]{:S(2)}, u32[]{:S(2)}) %all-to-all-start.5) | async-done | bytes 81952 | tf_op jit(solution)/shard_map/all_to_all | solution.py:854
  211.2 6.9 %all-to-all-start.6 = ((bf16[16,48,384]{2,1,0:T(8,128)(2,1)}), bf16[16,48,384]{2,1,0:T(8,128)(2,1)S(1)}, u32[]{:S(2)}, u32[]{:S(2)}) async-start(bf16[16,48,384]{2,1,0:T(8,128)(2,1)} %bitcast.18), calls=%async_computation.8 | async-start | bytes 1179648 | tf_op jit(solution)/shard_map/all_to_all | solution.py:834
  218.8 0.6 reduce_sum.79
  219.6 0.7 copy.85
  220.2 0.6 fusion.14
  221.3 0.7 slice.136
  222.0 0.7 slice.122
  222.7 0.7 copy.84
  223.4 6.5 %all-to-all-done.6 = bf16[16,48,384]{2,1,0:T(8,128)(2,1)S(1)} async-done(((bf16[16,48,384]{2,1,0:T(8,128)(2,1)}), bf16[16,48,384]{2,1,0:T(8,128)(2,1)S(1)}, u32[]{:S(2)}, u32[]{:S(2)}) %all-to-all-start.6) | async-done | bytes 589856 | tf_op jit(solution)/shard_map/all_to_all | solution.py:834
  230.0 0.7 slice_bitcast_fusion
  230.7 3.8 %copy.91 = bf16[2048,768]{1,0:T(8,128)(2,1)} copy(bf16[2048,768]{1,0:T(8,128)(2,1)} %all-gather.5.cloned.1.call-done) | data formatting | bytes 6291456
  (90 shorter events, 5.3 us)
Async XLA Ops:
  7.2 28.6 %copy-start.4 = (bf16[192,48]{0,1:T(8,128)(2,1)S(1)}, bf16[192,48]{0,1:T(8,128)(2,1)}, u32[]{:S(2)}) copy-start(bf16[192,48]{0,1:T(8,128)(2,1)} %param.33) | copy-start | bytes 55300
  7.2 28.6 %copy-start.5 = (bf16[48,192]{1,0:T(8,128)(2,1)S(1)}, bf16[48,192]{1,0:T(8,128)(2,1)}, u32[]{:S(2)}) copy-start(bf16[48,192]{1,0:T(8,128)(2,1)} %param.21) | copy-start | bytes 55300
  7.2 28.4 %copy-start.16 = (s32[1,4]{1,0:T(1,128)S(1)}, s32[1,4]{1,0:T(1,128)}, u32[]{:S(2)}) copy-start(s32[1,4]{1,0:T(1,128)} %param.19) | copy-start | bytes 52
  10.4 10.1 %all-to-all-start = ((f32[8,1,1792]{2,1,0:T(1,128)}), f32[8,1,1792]{2,1,0:T(1,128)S(1)}, u32[]{:S(2)}, u32[]{:S(2)}) async-start(f32[8,1,1792]{2,1,0:T(1,128)} %reshape.159), calls=%async_computation | async-start | bytes 114688 | tf_op jit(solution)/shard_map/all_to_all | solution.py:648
  23.8 22.1 %all-to-all-start.1 = ((bf16[16,48,512]{2,1,0:T(8,128)(2,1)}), bf16[16,48,512]{2,1,0:T(8,128)(2,1)S(1)}, u32[]{:S(2)}, u32[]{:S(2)}) async-start(bf16[16,48,512]{2,1,0:T(8,128)(2,1)} %broadcast_in_dim.22), calls=%async_computation.1 | async-start | bytes 1572864 | tf_op jit(solution)/shard_map/all_to_all | solution.py:648
  31.7 18.9 %collective-permute-start = (bf16[16,768]{1,0:T(8,128)(2,1)S(1)}, bf16[16,768]{1,0:T(8,128)(2,1)S(1)}, u32[]{:S(2)}, u32[]{:S(2)}) collective-permute-start(bf16[16,768]{1,0:T(8,128)(2,1)S(1)} %slice.106), channel_id=1, source_target_pairs={{0,8},{8,16},{16,24},{1,9},{9,17},{17,25},{2,10},{10,18},{18,26},{... | collective-permute-start | bytes 73736 | tf_op jit(solution)/shard_map/ppermute | solution.py:643
  45.9 4.7 %copy-start = (bf16[16,48,512]{2,1,0:T(8,128)(2,1)}, bf16[16,48,512]{2,1,0:T(8,128)(2,1)S(1)}, u32[]{:S(2)}) copy-start(bf16[16,48,512]{2,1,0:T(8,128)(2,1)S(1)} %all-to-all-done.1) | copy-start | bytes 2359300
  47.0 26.2 %all-to-all-start.2 = ((bf16[16,48,512]{2,1,0:T(8,128)(2,1)}), bf16[16,48,512]{2,1,0:T(8,128)(2,1)S(1)}, u32[]{:S(2)}, u32[]{:S(2)}) async-start(bf16[16,48,512]{2,1,0:T(8,128)(2,1)} %broadcast_in_dim.23), calls=%async_computation.2 | async-start | bytes 1572864 | tf_op jit(solution)/shard_map/all_to_all | solution.py:648
  50.6 76.3 %reduce-scatter.3.cloned.1.call-start = ((), (), s32[]{:S(2)}) async-start(), calls=%async_computation.9 | async-start | bytes 3538944 | tf_op jit(solution)/shard_map/reduce_scatter | solution.py:751
  50.7 0.6 copy-start.15
  64.1 18.1 %collective-permute-start.3 = (f32[136,256]{1,0:T(8,128)}, f32[136,256]{1,0:T(8,128)S(1)}, u32[]{:S(2)}, u32[]{:S(2)}) collective-permute-start(f32[136,256]{1,0:T(8,128)} %get-tuple-element.84), channel_id=1, source_target_pairs={{0,24},{1,25},{2,26},{3,27},{4,28},{5,29},{6,30},{7,31},{32,56},{3... | collective-permute-start | bytes 417800 | tf_op jit(solution)/shard_map/ppermute | solution.py:643
  69.1 13.2 %collective-permute-start.2 = (f32[136,256]{1,0:T(8,128)}, f32[136,256]{1,0:T(8,128)S(1)}, u32[]{:S(2)}, u32[]{:S(2)}) collective-permute-start(f32[136,256]{1,0:T(8,128)} %get-tuple-element.84), channel_id=1, source_target_pairs={{0,16},{8,24},{1,17},{9,25},{2,18},{10,26},{3,19},{11,27},{4,20},{... | collective-permute-start | bytes 417800 | tf_op jit(solution)/shard_map/ppermute | solution.py:643
  70.4 11.9 %collective-permute-start.1 = (f32[136,256]{1,0:T(8,128)}, f32[136,256]{1,0:T(8,128)S(1)}, u32[]{:S(2)}, u32[]{:S(2)}) collective-permute-start(f32[136,256]{1,0:T(8,128)} %get-tuple-element.84), channel_id=1, source_target_pairs={{0,8},{8,16},{16,24},{1,9},{9,17},{17,25},{2,10},{10,18},{18,26},{... | collective-permute-start | bytes 417800 | tf_op jit(solution)/shard_map/ppermute | solution.py:643
  73.2 0.9 copy-start.1
  82.2 0.7 copy-start.12
  82.2 0.7 copy-start.13
  82.3 0.8 copy-start.14
  90.6 0.7 copy-start.8
  92.0 10.2 %all-to-all-start.3 = ((f32[8,2,2048]{2,1,0:T(2,128)}), f32[8,2,2048]{2,1,0:T(2,128)S(1)}, u32[]{:S(2)}, u32[]{:S(2)}) async-start(f32[8,2,2048]{2,1,0:T(2,128)} %broadcast_in_dim.24), calls=%async_computation.3 | async-start | bytes 262144 | tf_op jit(solution)/shard_map/all_to_all | solution.py:648
  95.4 63.2 %all-gather.3.cloned.1.call-start = ((), (), s32[]{:S(2)}) async-start(), calls=%async_computation.10 | async-start | bytes 3538944 | tf_op jit(solution)/shard_map/all_gather | solution.py:781
  102.3 0.6 copy-start.3
  110.2 18.8 %collective-permute-start.6 = (f32[136,256]{1,0:T(8,128)}, f32[136,256]{1,0:T(8,128)S(1)}, u32[]{:S(2)}, u32[]{:S(2)}) collective-permute-start(f32[136,256]{1,0:T(8,128)} %get-tuple-element.93), channel_id=1, source_target_pairs={{24,0},{25,1},{26,2},{27,3},{28,4},{29,5},{30,6},{31,7},{56,32},{5... | collective-permute-start | bytes 417800 | tf_op jit(solution)/shard_map/ppermute | solution.py:643
  111.5 17.5 %collective-permute-start.5 = (f32[136,256]{1,0:T(8,128)}, f32[136,256]{1,0:T(8,128)S(1)}, u32[]{:S(2)}, u32[]{:S(2)}) collective-permute-start(f32[136,256]{1,0:T(8,128)} %get-tuple-element.93), channel_id=1, source_target_pairs={{16,0},{24,8},{17,1},{25,9},{18,2},{26,10},{19,3},{27,11},{20,4},{... | collective-permute-start | bytes 417800 | tf_op jit(solution)/shard_map/ppermute | solution.py:643
  112.8 16.2 %collective-permute-start.4 = (f32[136,256]{1,0:T(8,128)}, f32[136,256]{1,0:T(8,128)S(1)}, u32[]{:S(2)}, u32[]{:S(2)}) collective-permute-start(f32[136,256]{1,0:T(8,128)} %get-tuple-element.93), channel_id=1, source_target_pairs={{8,0},{16,8},{24,16},{9,1},{17,9},{25,17},{10,2},{18,10},{26,18},{... | collective-permute-start | bytes 417800 | tf_op jit(solution)/shard_map/ppermute | solution.py:643
  128.9 0.7 copy-start.9
  129.0 0.7 copy-start.10
  129.0 0.7 copy-start.11
  129.0 68.1 %reduce-scatter.5.cloned.1.call-start = ((), (), s32[]{:S(2)}) async-start(), calls=%async_computation.11 | async-start | bytes 3538944 | tf_op jit(solution)/shard_map/reduce_scatter | solution.py:811
  149.6 9.0 %copy-start.7 = (bf16[16,512]{1,0:T(8,128)(2,1)S(1)}, bf16[16,512]{1,0:T(8,128)(2,1)}, u32[]{:S(2)}) copy-start(bf16[16,512]{1,0:T(8,128)(2,1)} %get-tuple-element.114) | copy-start | bytes 49156
  149.6 9.1 %copy-start.2 = (bf16[768,512]{1,0:T(8,128)(2,1)S(1)}, bf16[768,512]{1,0:T(8,128)(2,1)}, u32[]{:S(2)}) copy-start(bf16[768,512]{1,0:T(8,128)(2,1)} %get-tuple-element.113) | copy-start | bytes 2359300
  149.6 6.7 %collective-permute-start.7 = (f32[8,768]{1,0:T(8,128)}, f32[8,768]{1,0:T(8,128)S(1)}, u32[]{:S(2)}, u32[]{:S(2)}) collective-permute-start(f32[8,768]{1,0:T(8,128)} %get-tuple-element.110), channel_id=1, source_target_pairs={{8,0},{16,8},{24,16},{9,1},{17,9},{25,17},{10,2},{18,10},{26,18},{... | collective-permute-start | bytes 73736 | tf_op jit(solution)/shard_map/ppermute | solution.py:643
  159.7 25.2 %all-to-all-start.4 = ((bf16[16,64,512]{2,1,0:T(8,128)(2,1)}), bf16[16,64,512]{2,1,0:T(8,128)(2,1)S(1)}, u32[]{:S(2)}, u32[]{:S(2)}) async-start(bf16[16,64,512]{2,1,0:T(8,128)(2,1)} %pad_maximum_fusion), calls=%async_computation.6 | async-start | bytes 2097152 | tf_op jit(solution)/shard_map/all_to_all | solution.py:821
  166.8 63.9 %all-gather.5.cloned.1.call-start = ((), (), s32[]{:S(2)}) async-start(), calls=%async_computation.12 | async-start | bytes 3538944 | tf_op jit(solution)/shard_map/all_gather | solution.py:833
  166.8 30.3 %copy-start.6 = (f32[768]{0:T(1024)S(1)}, f32[768]{0:T(1024)}, u32[]{:S(2)}) copy-start(f32[768]{0:T(1024)} %refs_6_.1) | copy-start | bytes 9220
  202.1 9.1 %all-to-all-start.5 = ((f32[8,20,128]{2,1,0:T(8,128)}), f32[8,20,128]{2,1,0:T(8,128)S(1)}, u32[]{:S(2)}, u32[]{:S(2)}) async-start(f32[8,20,128]{2,1,0:T(8,128)} %copy.83), calls=%async_computation.7 | async-start | bytes 196608 | tf_op jit(solution)/shard_map/all_to_all | solution.py:854
  211.2 18.7 %all-to-all-start.6 = ((bf16[16,48,384]{2,1,0:T(8,128)(2,1)}), bf16[16,48,384]{2,1,0:T(8,128)(2,1)S(1)}, u32[]{:S(2)}, u32[]{:S(2)}) async-start(bf16[16,48,384]{2,1,0:T(8,128)(2,1)} %bitcast.18), calls=%async_computation.8 | async-start | bytes 1179648 | tf_op jit(solution)/shard_map/all_to_all | solution.py:834
Sparse Core Ops, SparseCore 0:
  90.8 34.2 reduce-scatter.2
  129.1 29.4 all-gather.2
  161.0 36.0 reduce-scatter.4
  200.9 26.5 all-gather.4

commit v5 on v4

--- a/solution.py
+++ b/solution.py
@@ -20,7 +20,7 @@
 BF16 = jnp.bfloat16
 CELLS = ("shard", "context")
 VMEM_LIMIT = 60 * 1024 * 1024
-PARTS = (2, 2, 2, 2, 1, 2)
+PARTS = (2, 2, 4, 2, 1, 2)
 
 
 def nn(a, b):
@@ -829,7 +829,7 @@
     own_grad = own_cot + scaling * (
         scaled - unit * jnp.mean(scaled * unit, axis=1, keepdims=True)
     )
-    own_grad, late = lax.optimization_barrier((own_grad.astype(BF16), late))
+    own_grad = own_grad.astype(BF16)
     grad_hidden = lax.all_gather(own_grad, "tensor", axis=0, tiled=True)
     late = lax.all_to_all(late.reshape(cells, own_rows, 2 * INNER_DEV), CELLS, 0, 0, tiled=False)
     late = jnp.sum(late.astype(F32), axis=0)

time: 243 us -> 245 us (level)
  blocking collectives: 0 us -> 17.3 us
  waiting for transfers between devices: 62.7 us -> 53.8 us
  starting transfers between devices: 55.2 us -> 48.2 us
    all_to_all x0 -> x1, blocking collectives: none -> 17.3 us  [body(): lax.all_to_all(late.reshape(cells, own_rows, 2 * INNER_DEV), CELLS, 0, 0,...]
    all_to_all x1 -> x0, starting transfers between devices: 6.93 us -> none  [body(): lax.all_to_all(late.reshape(cells, own_rows, 2 * INNER_DEV), CELLS, 0, 0,...]
    all_to_all x1 -> x0, waiting for transfers between devices: 6.46 us -> none  [body(): lax.all_to_all(late.reshape(cells, own_rows, 2 * INNER_DEV), CELLS, 0, 0,...]
    all_to_all x1, waiting for transfers between devices: 4.41 us -> 1.93 us  [body(): lax.all_to_all(final, 'tensor', 0, 0, tiled=False)]
    unnamed x42 -> x44, local copies, waits for them, and re-layouts: 11.6 us -> 11.6 us
  transfers between devices with their start and end apart: 19 -> 18, of which waited for: 9 -> 8; matrix products, arithmetic and copies ran while one was open for 7% -> 7% of each run, Pallas kernels for 27% -> 27%
where the time goes in v5:
time: 245 us; the launch traced here: 242 us
  Pallas kernels  72.7 us (30%)
  waiting for transfers between devices  53.8 us (22%)
  starting transfers between devices  48.2 us (20%)
  local copies, waits for them, and re-layouts  23.5 us (10%)
  blocking collectives  17.3 us (7%)
  between operations  14.3 us (6%)
  other arithmetic  12.4 us (5%)
    pallas_call x6, Pallas kernels, call(): pl.pallas_call(run, grid=(steps,), in_specs=[spec(kind) for kind in ins],...  68.4 us
    all_to_all x4, waiting for transfers between devices, handed_to_all(): lax.all_to_all(jnp.broadcast_to(values[None], (count,) + values.shape), a...  19.5 us
    all_to_all x4, starting transfers between devices, handed_to_all(): lax.all_to_all(jnp.broadcast_to(values[None], (count,) + values.shape), a...  19.4 us
    ppermute x8, starting transfers between devices, passed_along(): return lax.ppermute(values, axis, pairs)  18.1 us
    all_to_all x1, blocking collectives, body(): lax.all_to_all(late.reshape(cells, own_rows, 2 * INNER_DEV), CELLS, 0, 0,...  17.3 us
    all_to_all x1, waiting for transfers between devices, body(): early = lax.all_to_all(early, CELLS, 0, 0, tiled=False)  13.8 us
    reduce_scatter x1, waiting for transfers between devices, body(): own_dn = lax.psum_scatter(dn, 'tensor', scatter_dimension=0, tiled=True)  12.1 us
    unnamed x44, local copies, waits for them, and re-layouts  11.6 us
  transfers between devices with their start and end apart: 18, of which 8 were waited for; matrix products, arithmetic and copies ran while one was open for 7% of the time, Pallas kernels for 27%

profile of v5, /device:TPU:0, one launch (start us, length us, event | category | flops | bytes accessed | tf_op | source)
XLA Modules:
  0.0 242.2 jit_solution(12338540421171579163)
XLA Ops:
  7.2 0.7 convert_element_type.42
  7.9 0.8 copy.75
  8.7 0.7 copy.76
  9.6 0.8 reshape.159
  10.4 4.6 %all-to-all-start = ((f32[8,1,1792]{2,1,0:T(1,128)}), f32[8,1,1792]{2,1,0:T(1,128)S(1)}, u32[]{:S(2)}, u32[]{:S(2)}) async-start(f32[8,1,1792]{2,1,0:T(1,128)} %reshape.159), calls=%async_computation | async-start | bytes 114688 | tf_op jit(solution)/shard_map/all_to_all | solution.py:648
  14.9 0.8 copy.78
  15.7 0.7 slice.106
  16.5 4.0 %all-to-all-done = f32[8,1,1792]{2,1,0:T(1,128)S(1)} async-done(((f32[8,1,1792]{2,1,0:T(1,128)}), f32[8,1,1792]{2,1,0:T(1,128)S(1)}, u32[]{:S(2)}, u32[]{:S(2)}) %all-to-all-start) | async-done | bytes 57376 | tf_op jit(solution)/shard_map/all_to_all | solution.py:648
  21.0 0.8 reduce.8
  22.1 0.8 pad_maximum_fusion.2
  22.9 1.0 broadcast_in_dim.22
  23.8 7.9 %all-to-all-start.1 = ((bf16[16,48,512]{2,1,0:T(8,128)(2,1)}), bf16[16,48,512]{2,1,0:T(8,128)(2,1)S(1)}, u32[]{:S(2)}, u32[]{:S(2)}) async-start(bf16[16,48,512]{2,1,0:T(8,128)(2,1)} %broadcast_in_dim.22), calls=%async_computation.1 | async-start | bytes 1572864 | tf_op jit(solution)/shard_map/all_to_all | solution.py:648
  31.7 3.8 %collective-permute-start = (bf16[16,768]{1,0:T(8,128)(2,1)S(1)}, bf16[16,768]{1,0:T(8,128)(2,1)S(1)}, u32[]{:S(2)}, u32[]{:S(2)}) collective-permute-start(bf16[16,768]{1,0:T(8,128)(2,1)S(1)} %slice.106), channel_id=1, source_target_pairs={{0,8},{8,16},{16,24},{1,9},{9,17},{17,25},{2,10},{10,18},{18,26},{... | collective-permute-start | bytes 73736 | tf_op jit(solution)/shard_map/ppermute | solution.py:643
  35.8 0.6 pad_add_fusion.refs_0_
  36.5 0.7 copy.87.refs_11_
  37.2 8.8 %all-to-all-done.1 = bf16[16,48,512]{2,1,0:T(8,128)(2,1)S(1)} async-done(((bf16[16,48,512]{2,1,0:T(8,128)(2,1)}), bf16[16,48,512]{2,1,0:T(8,128)(2,1)S(1)}, u32[]{:S(2)}, u32[]{:S(2)}) %all-to-all-start.1) | async-done | bytes 786464 | tf_op jit(solution)/shard_map/all_to_all | solution.py:648
  46.0 1.0 broadcast_in_dim.23
  47.0 3.6 %all-to-all-start.2 = ((bf16[16,48,512]{2,1,0:T(8,128)(2,1)}), bf16[16,48,512]{2,1,0:T(8,128)(2,1)S(1)}, u32[]{:S(2)}, u32[]{:S(2)}) async-start(bf16[16,48,512]{2,1,0:T(8,128)(2,1)} %broadcast_in_dim.23), calls=%async_computation.2 | async-start | bytes 1572864 | tf_op jit(solution)/shard_map/all_to_all | solution.py:648
  50.7 0.6 copy-done.16
  51.3 12.9 %shard_map.288 = (bf16[2048,768]{1,0:T(8,128)(2,1)}, bf16[2048,512]{1,0:T(8,128)(2,1)}, bf16[2048,512]{1,0:T(8,128)(2,1)}, bf16[2048,512]{1,0:T(8,128)(2,1)}, f3...) custom-call(s32[8]{0:T(128)} %pad_add_fusion.refs_0_, ...), custom_call_target="tpu_custom_call" | custom-call | flops 16099999744 | bytes 14000000 | tf_op jit(solution)/shard_map/pallas_call | solution.py:234
  64.1 4.9 %collective-permute-start.3 = (f32[136,256]{1,0:T(8,128)}, f32[136,256]{1,0:T(8,128)S(1)}, u32[]{:S(2)}, u32[]{:S(2)}) collective-permute-start(f32[136,256]{1,0:T(8,128)} %get-tuple-element.82), channel_id=1, source_target_pairs={{0,24},{1,25},{2,26},{3,27},{4,28},{5,29},{6,30},{7,31},{32,56},{3... | collective-permute-start | bytes 417800 | tf_op jit(solution)/shard_map/ppermute | solution.py:643
  69.1 1.3 collective-permute-start.2
  70.4 2.8 %collective-permute-start.1 = (f32[136,256]{1,0:T(8,128)}, f32[136,256]{1,0:T(8,128)S(1)}, u32[]{:S(2)}, u32[]{:S(2)}) collective-permute-start(f32[136,256]{1,0:T(8,128)} %get-tuple-element.82), channel_id=1, source_target_pairs={{0,8},{8,16},{16,24},{1,9},{9,17},{17,25},{2,10},{10,18},{18,26},{... | collective-permute-start | bytes 417800 | tf_op jit(solution)/shard_map/ppermute | solution.py:643
  73.2 0.9 copy-done.1
  74.1 8.2 %shard_map.289 = (bf16[2048,256]{1,0:T(8,128)(2,1)}, bf16[2048,256]{1,0:T(8,128)(2,1)}, bf16[2048,256]{1,0:T(8,128)(2,1)}) custom-call(s32[8]{0:T(128)} %pad_add_fusion.refs_0_, bf16[2048,768]{1,0:T(8,128)(2,1)} %get-tuple-element.70.refs_1_, bf16[2048,768]{1,0:T(8,128)(2,1)} %refs_8_.3, bf16[768,512]{1,0:T(8,128)(2,1)} %bitcast.32, ...), custom_call_target="tpu_custom_call" | custom-call | flops 13799999488 | bytes 12000000 | tf_op jit(solution)/shard_map/pallas_call | solution.py:234
  82.3 0.6 copy-done.13
  83.1 7.4 %shard_map.290 = (bf16[2048,256]{1,0:T(8,128)(2,1)}, bf16[2048,256]{1,0:T(8,128)(2,1)}, bf16[2048,768]{1,0:T(8,128)(2,1)}, f32[2,2048]{1,0:T(2,128)}, f32[128,256]{1,0:T(8,128)}) custom-call(s32[8]{0:T(128)} %pad_add_fusion.refs_0_, bf16[2048,256]{1,0:T(8,128)(2,1)} %get-tuple-element.78.refs_1_, bf16[2048,256]{1,0:T(8,128)(2,1)} %get-tuple-element.79.refs_2_, ...), custom_call_target="tpu_custom_call" | custom-call | flops 11500000256 | bytes 10000000 | tf_op jit(solution)/shard_map/pallas_call | solution.py:234
  90.5 0.7 copy-done.9
  91.2 0.7 broadcast_in_dim.24
  91.9 3.4 %all-to-all-start.3 = ((f32[8,2,2048]{2,1,0:T(2,128)}), f32[8,2,2048]{2,1,0:T(2,128)S(1)}, u32[]{:S(2)}, u32[]{:S(2)}) async-start(f32[8,2,2048]{2,1,0:T(2,128)} %broadcast_in_dim.24), calls=%async_computation.3 | async-start | bytes 262144 | tf_op jit(solution)/shard_map/all_to_all | solution.py:648
  95.3 6.8 %all-to-all-done.3 = f32[8,2,2048]{2,1,0:T(2,128)S(1)} async-done(((f32[8,2,2048]{2,1,0:T(2,128)}), f32[8,2,2048]{2,1,0:T(2,128)S(1)}, u32[]{:S(2)}, u32[]{:S(2)}) %all-to-all-start.3) | async-done | bytes 131104 | tf_op jit(solution)/shard_map/all_to_all | solution.py:648
  102.2 0.6 copy-done.4
  102.8 7.3 %shard_map.291 = (bf16[2048,256]{1,0:T(8,128)(2,1)}, bf16[2048,256]{1,0:T(8,128)(2,1)}, f32[8,136,256]{2,1,0:T(8,128)}, f32[136,256]{1,0:T(8,128)}, f32[8,256]{1,0:T(8,128)}) custom-call(s32[8]{0:T(128)} %pad_add_fusion.refs_0_, bf16[2048,256]{1,0:T(8,128)(2,1)} %get-tuple-element.83.refs_1_, bf16[2048,256]{1,0:T(8,128)(2,1)} %get-tuple-element.79.refs_2_, ...), custom_call_target="tpu_custom_call" | custom-call | flops 10350000128 | bytes 9000000 | tf_op jit(solution)/shard_map/pallas_call | solution.py:234
  110.1 1.3 collective-permute-start.6
  111.4 1.3 collective-permute-start.5
  112.7 1.3 collective-permute-start.4
  114.0 12.7 %shard_map.292 = (bf16[2048,256]{1,0:T(8,128)(2,1)}, bf16[2048,256]{1,0:T(8,128)(2,1)}, f32[16,2048]{1,0:T(8,128)}, f32[768,256]{1,0:T(8,128)}) custom-call(s32[8]{0:T(128)} %pad_add_fusion.refs_0_, bf16[2048,256]{1,0:T(8,128)(2,1)} %get-tuple-element.86.refs_1_, bf16[2048,512]{1,0:T(8,128)(2,1)} %get-tuple-element.75.refs_4_.refs_2_.refs_6_, ...), custom_call_target="tpu_custom_call" | custom-call | flops 14949999616 | bytes 13000000 | tf_op jit(solution)/shard_map/pallas_call | solution.py:234
  126.8 2.1 fusion.8
  129.6 19.9 %shard_map.293 = (bf16[2048,768]{1,0:T(8,128)(2,1)}, bf16[768,512]{1,0:T(8,128)(2,1)}, bf16[768,384]{1,0:T(8,128)(2,1)}, bf16[16,512]{1,0:T(8,128)(2,1)}, f32[8,768]{1,0:T(8,128)}) custom-call(s32[8]{0:T(128)} %pad_add_fusion.refs_0_, bf16[2048,768]{1,0:T(8,128)(2,1)} %get-tuple-element.70.refs_1_, bf16[16,768]{1,0:T(8,128)(2,1)} %copy-done.16, ...), custom_call_target="tpu_custom_call" | custom-call | flops 25300000768 | bytes 22000000 | tf_op jit(solution)/shard_map/pallas_call | solution.py:234
  149.5 1.4 collective-permute-start.7
  150.9 5.2 %collective-permute-done.7 = f32[8,768]{1,0:T(8,128)S(1)} collective-permute-done((f32[8,768]{1,0:T(8,128)}, f32[8,768]{1,0:T(8,128)S(1)}, u32[]{:S(2)}, u32[]{:S(2)}) %collective-permute-start.7) | collective-permute-done | bytes 24608 | tf_op jit(solution)/shard_map/ppermute | solution.py:643
  156.2 1.3 fusion.12
  157.5 1.0 all-gather.3.cloned.1.call-done.source
  158.6 1.1 pad_maximum_fusion
  159.6 7.0 %all-to-all-start.4 = ((bf16[16,64,512]{2,1,0:T(8,128)(2,1)}), bf16[16,64,512]{2,1,0:T(8,128)(2,1)S(1)}, u32[]{:S(2)}, u32[]{:S(2)}) async-start(bf16[16,64,512]{2,1,0:T(8,128)(2,1)} %pad_maximum_fusion), calls=%async_computation.6 | async-start | bytes 2097152 | tf_op jit(solution)/shard_map/all_to_all | solution.py:821
  166.7 4.3 %shard_map.294 = bf16[2048,768]{1,0:T(8,128)(2,1)} custom-call(bf16[2048,768]{1,0:T(8,128)(2,1)} %all-gather.3.cloned.1.call-done.source), custom_call_target="tpu_custom_call" | custom-call | flops 3000000000 | bytes 6000000 | tf_op jit(solution)/shard_map/pallas_call | solution.py:627
  171.0 13.8 %all-to-all-done.4 = bf16[16,64,512]{2,1,0:T(8,128)(2,1)S(1)} async-done(((bf16[16,64,512]{2,1,0:T(8,128)(2,1)}), bf16[16,64,512]{2,1,0:T(8,128)(2,1)S(1)}, u32[]{:S(2)}, u32[]{:S(2)}) %all-to-all-start.4) | async-done | bytes 1048608 | tf_op jit(solution)/shard_map/all_to_all | solution.py:821
  184.8 12.1 %reduce-scatter.5.cloned.1.call-done = bf16[256,768]{1,0:T(8,128)(2,1)} async-done(((bf16[2048,768]{1,0:T(8,128)(2,1)}), bf16[256,768]{1,0:T(8,128)(2,1)}) %reduce-scatter.5.cloned.1.call-update) | async-done | bytes 393232 | tf_op jit(solution)/shard_map/reduce_scatter | solution.py:811
  196.9 1.4 fusion.2
  198.3 2.3 fusion.6
  200.6 17.3 %all_to_all.35 = bf16[16,48,384]{2,1,0:T(8,128)(2,1)S(1)} all-to-all(bf16[16,48,384]{2,1,0:T(8,128)(2,1)S(1)} %bitcast.36), channel_id=1, replica_groups=mesh['shard'=4,'context'=4,'tensor'=8] {'shard','context'}, dimensions={0} | all-to-all | bytes 1179648 | tf_op jit(solution)/shard_map/all_to_all | solution.py:834
  218.0 0.7 slice_bitcast_fusion
  219.5 0.7 copy.83
  220.2 3.4 %all-to-all-start.5 = ((f32[8,20,128]{2,1,0:T(8,128)}), f32[8,20,128]{2,1,0:T(8,128)S(1)}, u32[]{:S(2)}, u32[]{:S(2)}) async-start(f32[8,20,128]{2,1,0:T(8,128)} %copy.83), calls=%async_computation.7 | async-start | bytes 196608 | tf_op jit(solution)/shard_map/all_to_all | solution.py:854
  224.1 0.6 fusion.14
  224.7 0.6 slice.141
  225.4 0.6 slice.138
  226.1 0.6 reduce_sum.79
  226.7 0.7 copy.85
  227.4 1.9 all-to-all-done.5
  229.8 0.7 slice.136
  230.5 0.7 slice.122
  231.3 0.7 copy.84
  231.9 3.8 %copy.91 = bf16[2048,768]{1,0:T(8,128)(2,1)} copy(bf16[2048,768]{1,0:T(8,128)(2,1)} %all-gather.5.cloned.1.call-done) | data formatting | bytes 6291456
  (91 shorter events, 4.7 us)
Async XLA Ops:
  7.2 28.6 %copy-start.5 = (bf16[192,48]{0,1:T(8,128)(2,1)S(1)}, bf16[192,48]{0,1:T(8,128)(2,1)}, u32[]{:S(2)}) copy-start(bf16[192,48]{0,1:T(8,128)(2,1)} %param.33) | copy-start | bytes 55300
  7.2 28.6 %copy-start.6 = (bf16[48,192]{1,0:T(8,128)(2,1)S(1)}, bf16[48,192]{1,0:T(8,128)(2,1)}, u32[]{:S(2)}) copy-start(bf16[48,192]{1,0:T(8,128)(2,1)} %param.21) | copy-start | bytes 55300
  7.2 28.4 %copy-start.17 = (s32[1,4]{1,0:T(1,128)S(1)}, s32[1,4]{1,0:T(1,128)}, u32[]{:S(2)}) copy-start(s32[1,4]{1,0:T(1,128)} %param.19) | copy-start | bytes 52
  10.4 10.1 %all-to-all-start = ((f32[8,1,1792]{2,1,0:T(1,128)}), f32[8,1,1792]{2,1,0:T(1,128)S(1)}, u32[]{:S(2)}, u32[]{:S(2)}) async-start(f32[8,1,1792]{2,1,0:T(1,128)} %reshape.159), calls=%async_computation | async-start | bytes 114688 | tf_op jit(solution)/shard_map/all_to_all | solution.py:648
  23.8 22.1 %all-to-all-start.1 = ((bf16[16,48,512]{2,1,0:T(8,128)(2,1)}), bf16[16,48,512]{2,1,0:T(8,128)(2,1)S(1)}, u32[]{:S(2)}, u32[]{:S(2)}) async-start(bf16[16,48,512]{2,1,0:T(8,128)(2,1)} %broadcast_in_dim.22), calls=%async_computation.1 | async-start | bytes 1572864 | tf_op jit(solution)/shard_map/all_to_all | solution.py:648
  31.7 18.9 %collective-permute-start = (bf16[16,768]{1,0:T(8,128)(2,1)S(1)}, bf16[16,768]{1,0:T(8,128)(2,1)S(1)}, u32[]{:S(2)}, u32[]{:S(2)}) collective-permute-start(bf16[16,768]{1,0:T(8,128)(2,1)S(1)} %slice.106), channel_id=1, source_target_pairs={{0,8},{8,16},{16,24},{1,9},{9,17},{17,25},{2,10},{10,18},{18,26},{... | collective-permute-start | bytes 73736 | tf_op jit(solution)/shard_map/ppermute | solution.py:643
  45.9 4.7 %copy-start = (bf16[16,48,512]{2,1,0:T(8,128)(2,1)}, bf16[16,48,512]{2,1,0:T(8,128)(2,1)S(1)}, u32[]{:S(2)}) copy-start(bf16[16,48,512]{2,1,0:T(8,128)(2,1)S(1)} %all-to-all-done.1) | copy-start | bytes 2359300
  47.0 26.2 %all-to-all-start.2 = ((bf16[16,48,512]{2,1,0:T(8,128)(2,1)}), bf16[16,48,512]{2,1,0:T(8,128)(2,1)S(1)}, u32[]{:S(2)}, u32[]{:S(2)}) async-start(bf16[16,48,512]{2,1,0:T(8,128)(2,1)} %broadcast_in_dim.23), calls=%async_computation.2 | async-start | bytes 1572864 | tf_op jit(solution)/shard_map/all_to_all | solution.py:648
  50.6 76.2 %reduce-scatter.3.cloned.1.call-start = ((), (), s32[]{:S(2)}) async-start(), calls=%async_computation.9 | async-start | bytes 3538944 | tf_op jit(solution)/shard_map/reduce_scatter | solution.py:751
  50.7 0.6 copy-start.16
  64.1 18.1 %collective-permute-start.3 = (f32[136,256]{1,0:T(8,128)}, f32[136,256]{1,0:T(8,128)S(1)}, u32[]{:S(2)}, u32[]{:S(2)}) collective-permute-start(f32[136,256]{1,0:T(8,128)} %get-tuple-element.82), channel_id=1, source_target_pairs={{0,24},{1,25},{2,26},{3,27},{4,28},{5,29},{6,30},{7,31},{32,56},{3... | collective-permute-start | bytes 417800 | tf_op jit(solution)/shard_map/ppermute | solution.py:643
  69.1 13.2 %collective-permute-start.2 = (f32[136,256]{1,0:T(8,128)}, f32[136,256]{1,0:T(8,128)S(1)}, u32[]{:S(2)}, u32[]{:S(2)}) collective-permute-start(f32[136,256]{1,0:T(8,128)} %get-tuple-element.82), channel_id=1, source_target_pairs={{0,16},{8,24},{1,17},{9,25},{2,18},{10,26},{3,19},{11,27},{4,20},{... | collective-permute-start | bytes 417800 | tf_op jit(solution)/shard_map/ppermute | solution.py:643
  70.4 11.9 %collective-permute-start.1 = (f32[136,256]{1,0:T(8,128)}, f32[136,256]{1,0:T(8,128)S(1)}, u32[]{:S(2)}, u32[]{:S(2)}) collective-permute-start(f32[136,256]{1,0:T(8,128)} %get-tuple-element.82), channel_id=1, source_target_pairs={{0,8},{8,16},{16,24},{1,9},{9,17},{17,25},{2,10},{10,18},{18,26},{... | collective-permute-start | bytes 417800 | tf_op jit(solution)/shard_map/ppermute | solution.py:643
  73.2 0.9 copy-start.1
  82.2 0.7 copy-start.13
  82.3 0.7 copy-start.14
  82.3 0.8 copy-start.15
  90.5 0.7 copy-start.9
  91.9 10.2 %all-to-all-start.3 = ((f32[8,2,2048]{2,1,0:T(2,128)}), f32[8,2,2048]{2,1,0:T(2,128)S(1)}, u32[]{:S(2)}, u32[]{:S(2)}) async-start(f32[8,2,2048]{2,1,0:T(2,128)} %broadcast_in_dim.24), calls=%async_computation.3 | async-start | bytes 262144 | tf_op jit(solution)/shard_map/all_to_all | solution.py:648
  95.3 63.2 %all-gather.3.cloned.1.call-start = ((), (), s32[]{:S(2)}) async-start(), calls=%async_computation.10 | async-start | bytes 3538944 | tf_op jit(solution)/shard_map/all_gather | solution.py:781
  102.1 0.6 copy-start.4
  110.1 18.8 %collective-permute-start.6 = (f32[136,256]{1,0:T(8,128)}, f32[136,256]{1,0:T(8,128)S(1)}, u32[]{:S(2)}, u32[]{:S(2)}) collective-permute-start(f32[136,256]{1,0:T(8,128)} %get-tuple-element.91), channel_id=1, source_target_pairs={{24,0},{25,1},{26,2},{27,3},{28,4},{29,5},{30,6},{31,7},{56,32},{5... | collective-permute-start | bytes 417800 | tf_op jit(solution)/shard_map/ppermute | solution.py:643
  111.4 17.5 %collective-permute-start.5 = (f32[136,256]{1,0:T(8,128)}, f32[136,256]{1,0:T(8,128)S(1)}, u32[]{:S(2)}, u32[]{:S(2)}) collective-permute-start(f32[136,256]{1,0:T(8,128)} %get-tuple-element.91), channel_id=1, source_target_pairs={{16,0},{24,8},{17,1},{25,9},{18,2},{26,10},{19,3},{27,11},{20,4},{... | collective-permute-start | bytes 417800 | tf_op jit(solution)/shard_map/ppermute | solution.py:643
  112.7 16.2 %collective-permute-start.4 = (f32[136,256]{1,0:T(8,128)}, f32[136,256]{1,0:T(8,128)S(1)}, u32[]{:S(2)}, u32[]{:S(2)}) collective-permute-start(f32[136,256]{1,0:T(8,128)} %get-tuple-element.91), channel_id=1, source_target_pairs={{8,0},{16,8},{24,16},{9,1},{17,9},{25,17},{10,2},{18,10},{26,18},{... | collective-permute-start | bytes 417800 | tf_op jit(solution)/shard_map/ppermute | solution.py:643
  128.8 0.7 copy-start.10
  128.8 0.7 copy-start.11
  128.9 0.7 copy-start.12
  128.9 68.0 %reduce-scatter.5.cloned.1.call-start = ((), (), s32[]{:S(2)}) async-start(), calls=%async_computation.11 | async-start | bytes 3538944 | tf_op jit(solution)/shard_map/reduce_scatter | solution.py:811
  149.5 9.1 %copy-start.8 = (bf16[16,512]{1,0:T(8,128)(2,1)S(1)}, bf16[16,512]{1,0:T(8,128)(2,1)}, u32[]{:S(2)}) copy-start(bf16[16,512]{1,0:T(8,128)(2,1)} %get-tuple-element.112) | copy-start | bytes 49156
  149.5 9.1 %copy-start.2 = (bf16[768,512]{1,0:T(8,128)(2,1)S(1)}, bf16[768,512]{1,0:T(8,128)(2,1)}, u32[]{:S(2)}) copy-start(bf16[768,512]{1,0:T(8,128)(2,1)} %get-tuple-element.111) | copy-start | bytes 2359300
  149.5 6.7 %collective-permute-start.7 = (f32[8,768]{1,0:T(8,128)}, f32[8,768]{1,0:T(8,128)S(1)}, u32[]{:S(2)}, u32[]{:S(2)}) collective-permute-start(f32[8,768]{1,0:T(8,128)} %get-tuple-element.108), channel_id=1, source_target_pairs={{8,0},{16,8},{24,16},{9,1},{17,9},{25,17},{10,2},{18,10},{26,18},{... | collective-permute-start | bytes 73736 | tf_op jit(solution)/shard_map/ppermute | solution.py:643
  159.6 25.2 %all-to-all-start.4 = ((bf16[16,64,512]{2,1,0:T(8,128)(2,1)}), bf16[16,64,512]{2,1,0:T(8,128)(2,1)S(1)}, u32[]{:S(2)}, u32[]{:S(2)}) async-start(bf16[16,64,512]{2,1,0:T(8,128)(2,1)} %pad_maximum_fusion), calls=%async_computation.6 | async-start | bytes 2097152 | tf_op jit(solution)/shard_map/all_to_all | solution.py:821
  166.6 65.3 %all-gather.5.cloned.1.call-start = ((), (), s32[]{:S(2)}) async-start(), calls=%async_computation.12 | async-start | bytes 3538944 | tf_op jit(solution)/shard_map/all_gather | solution.py:833
  166.7 30.3 %copy-start.7 = (f32[768]{0:T(1024)S(1)}, f32[768]{0:T(1024)}, u32[]{:S(2)}) copy-start(f32[768]{0:T(1024)} %refs_6_.1) | copy-start | bytes 9220
  171.0 29.6 %copy-start.3 = (bf16[768,384]{1,0:T(8,128)(2,1)S(1)}, bf16[768,384]{1,0:T(8,128)(2,1)}, u32[]{:S(2)}) copy-start(bf16[768,384]{1,0:T(8,128)(2,1)} %get-tuple-element.117) | copy-start | bytes 1769476
  220.2 9.1 %all-to-all-start.5 = ((f32[8,20,128]{2,1,0:T(8,128)}), f32[8,20,128]{2,1,0:T(8,128)S(1)}, u32[]{:S(2)}, u32[]{:S(2)}) async-start(f32[8,20,128]{2,1,0:T(8,128)} %copy.83), calls=%async_computation.7 | async-start | bytes 196608 | tf_op jit(solution)/shard_map/all_to_all | solution.py:854
Sparse Core Ops, SparseCore 0:
  90.7 34.2 reduce-scatter.2
  129.0 29.4 all-gather.2
  160.9 35.9 reduce-scatter.4
  200.7 26.6 all-gather.4

commit v6 on v4

--- a/solution.py
+++ b/solution.py
@@ -637,6 +637,31 @@
     )(values)
 
 
+def finish_kernel(dn, hidden, cot, gain, out):
+    rows = hidden[...].astype(F32)
+    scale = lax.rsqrt(jnp.mean(rows * rows, axis=1, keepdims=True) + EPSILON)
+    unit = rows * scale
+    scaled = dn[...].astype(F32) * gain[0:1]
+    across = jnp.mean(scaled * unit, axis=1, keepdims=True)
+    out[...] = (cot[...].astype(F32) + scale * (scaled - unit * across)).astype(BF16)
+
+
+def finished(dn, hidden, cot, gain):
+    rows, width = dn.shape
+    block = pl.BlockSpec((rows // 2, width), lambda s: (s, 0))
+    return pl.pallas_call(
+        finish_kernel,
+        grid=(2,),
+        in_specs=[block, block, block, pl.BlockSpec((8, width), lambda s: (0, 0))],
+        out_specs=block,
+        out_shape=jax.ShapeDtypeStruct(dn.shape, BF16),
+        compiler_params=pltpu.CompilerParams(
+            dimension_semantics=("arbitrary",), vmem_limit_bytes=VMEM_LIMIT
+        ),
+        cost_estimate=pl.CostEstimate(flops=int(2e9), bytes_accessed=int(2e6), transcendentals=0),
+    )(dn, hidden, cot, gain)
+
+
 def passed_along(values, axis, by):
     count = lax.axis_size(axis)
     pairs = [(i, i + by) for i in range(count) if 0 <= i + by < count]
@@ -746,7 +771,6 @@
     own = tok // ranks
     place = rank * own
     own_hidden = lax.dynamic_slice_in_dim(hidden, place, own, 0).astype(F32)
-    own_cot = lax.dynamic_slice_in_dim(cotangent, place, own, 0).astype(F32)
     own_root = lax.rsqrt(lax.dynamic_slice_in_dim(sums[0], place, own, 0) / INNER + EPSILON)
     projected = lax.psum_scatter(part, "tensor", scatter_dimension=0, tiled=True).astype(F32)
     own_out = (own_hidden + own_root[:, None] * projected).astype(BF16)
@@ -807,7 +831,7 @@
     arrived = passed_along(spill, "context", -1)
     end = dn[tok - 8 :].astype(F32) + arrived
     dn = lax.dynamic_update_slice(dn, end.astype(BF16), (tok - 8, 0))
-    dn, output = lax.optimization_barrier((dn, output))
+    dn, output, hidden_late, cot_late = lax.optimization_barrier((dn, output, hidden, cotangent))
     own_dn = lax.psum_scatter(dn, "tensor", scatter_dimension=0, tiled=True)
 
     cells = lax.axis_size("shard") * lax.axis_size("context")
@@ -820,16 +844,14 @@
     )
     early = lax.all_to_all(early, CELLS, 0, 0, tiled=False)
     output = copied(output)
-    own_dn, early, output = lax.optimization_barrier((own_dn, early, output))
+    own_rows_in = lax.dynamic_slice_in_dim(hidden_late, place, own, 0)
+    own_cot = lax.dynamic_slice_in_dim(cot_late, place, own, 0)
+    own_dn, early, output, own_rows_in, own_cot = lax.optimization_barrier(
+        (own_dn, early, output, own_rows_in, own_cot)
+    )
     early = jnp.sum(early.astype(F32), axis=0)
-    own_dn = own_dn.astype(F32)
-    scaling = lax.rsqrt(jnp.mean(own_hidden * own_hidden, axis=1, keepdims=True) + EPSILON)
-    unit = own_hidden * scaling
-    scaled = own_dn * norm_gain[None]
-    own_grad = own_cot + scaling * (
-        scaled - unit * jnp.mean(scaled * unit, axis=1, keepdims=True)
-    )
-    own_grad, late = lax.optimization_barrier((own_grad.astype(BF16), late))
+    own_grad = finished(own_dn, own_rows_in, own_cot, gain)
+    own_grad, late = lax.optimization_barrier((own_grad, late))
     grad_hidden = lax.all_gather(own_grad, "tensor", axis=0, tiled=True)
     late = lax.all_to_all(late.reshape(cells, own_rows, 2 * INNER_DEV), CELLS, 0, 0, tiled=False)
     late = jnp.sum(late.astype(F32), axis=0)

time: 243 us -> 242 us (level)
  other arithmetic: 12.4 us -> 8.74 us
    reduce_sum x2 -> x0, other arithmetic: 3.45 us -> none  [the longest x1 2.07 us: body(): jnp.mean(own_hidden * own_hidden, axis=1, keepdims=True) + EPSILON]
    unnamed x42 -> x40, local copies, waits for them, and re-layouts: 11.6 us -> 11.5 us
  transfers between devices with their start and end apart: 19 -> 19, of which waited for: 9 -> 9; matrix products, arithmetic and copies ran while one was open for 7% -> 8% of each run, Pallas kernels for 27% -> 27%
where the time goes in v6:
time: 242 us; the launch traced here: 240 us
  Pallas kernels  75.2 us (31%)
  waiting for transfers between devices  60.6 us (25%)
  starting transfers between devices  55.2 us (23%)
  local copies, waits for them, and re-layouts  25.5 us (11%)
  between operations  14.3 us (6%)
  other arithmetic  8.74 us (4%)
    pallas_call x6, Pallas kernels, call(): pl.pallas_call(run, grid=(steps,), in_specs=[spec(kind) for kind in ins],...  68.6 us
    all_to_all x4, waiting for transfers between devices, handed_to_all(): lax.all_to_all(jnp.broadcast_to(values[None], (count,) + values.shape), a...  19.5 us
    all_to_all x4, starting transfers between devices, handed_to_all(): lax.all_to_all(jnp.broadcast_to(values[None], (count,) + values.shape), a...  19.4 us
    ppermute x8, starting transfers between devices, passed_along(): return lax.ppermute(values, axis, pairs)  18.1 us
    reduce_scatter x1, waiting for transfers between devices, body(): own_dn = lax.psum_scatter(dn, 'tensor', scatter_dimension=0, tiled=True)  12.1 us
    all_to_all x1, waiting for transfers between devices, body(): early = lax.all_to_all(early, CELLS, 0, 0, tiled=False)  11.7 us
    unnamed x40, local copies, waits for them, and re-layouts  11.5 us
    all_to_all x1, starting transfers between devices, body(): early = lax.all_to_all(early, CELLS, 0, 0, tiled=False)  7.02 us
  transfers between devices with their start and end apart: 19, of which 9 were waited for; matrix products, arithmetic and copies ran while one was open for 8% of the time, Pallas kernels for 27%

profile of v6, /device:TPU:0, one launch (start us, length us, event | category | flops | bytes accessed | tf_op | source)
XLA Modules:
  0.0 239.7 jit_solution(9773130955839861803)
XLA Ops:
  7.2 0.7 convert_element_type.33
  7.9 0.8 copy.75
  8.7 0.7 copy.76
  9.6 0.8 reshape.146
  10.4 4.6 %all-to-all-start = ((f32[8,1,1792]{2,1,0:T(1,128)}), f32[8,1,1792]{2,1,0:T(1,128)S(1)}, u32[]{:S(2)}, u32[]{:S(2)}) async-start(f32[8,1,1792]{2,1,0:T(1,128)} %reshape.146), calls=%async_computation | async-start | bytes 114688 | tf_op jit(solution)/shard_map/all_to_all | solution.py:673
  14.9 0.8 copy.78
  15.7 0.7 slice.106
  16.5 4.0 %all-to-all-done = f32[8,1,1792]{2,1,0:T(1,128)S(1)} async-done(((f32[8,1,1792]{2,1,0:T(1,128)}), f32[8,1,1792]{2,1,0:T(1,128)S(1)}, u32[]{:S(2)}, u32[]{:S(2)}) %all-to-all-start) | async-done | bytes 57376 | tf_op jit(solution)/shard_map/all_to_all | solution.py:673
  21.0 0.8 reduce.8
  22.1 0.8 pad_maximum_fusion.2
  22.9 1.0 broadcast_in_dim.22
  23.8 7.9 %all-to-all-start.1 = ((bf16[16,48,512]{2,1,0:T(8,128)(2,1)}), bf16[16,48,512]{2,1,0:T(8,128)(2,1)S(1)}, u32[]{:S(2)}, u32[]{:S(2)}) async-start(bf16[16,48,512]{2,1,0:T(8,128)(2,1)} %broadcast_in_dim.22), calls=%async_computation.1 | async-start | bytes 1572864 | tf_op jit(solution)/shard_map/all_to_all | solution.py:673
  31.7 3.8 %collective-permute-start = (bf16[16,768]{1,0:T(8,128)(2,1)S(1)}, bf16[16,768]{1,0:T(8,128)(2,1)S(1)}, u32[]{:S(2)}, u32[]{:S(2)}) collective-permute-start(bf16[16,768]{1,0:T(8,128)(2,1)S(1)} %slice.106), channel_id=1, source_target_pairs={{0,8},{8,16},{16,24},{1,9},{9,17},{17,25},{2,10},{10,18},{18,26},{... | collective-permute-start | bytes 73736 | tf_op jit(solution)/shard_map/ppermute | solution.py:668
  35.8 0.6 pad_add_fusion.refs_0_
  36.5 0.7 copy.87.refs_11_
  37.2 8.8 %all-to-all-done.1 = bf16[16,48,512]{2,1,0:T(8,128)(2,1)S(1)} async-done(((bf16[16,48,512]{2,1,0:T(8,128)(2,1)}), bf16[16,48,512]{2,1,0:T(8,128)(2,1)S(1)}, u32[]{:S(2)}, u32[]{:S(2)}) %all-to-all-start.1) | async-done | bytes 786464 | tf_op jit(solution)/shard_map/all_to_all | solution.py:673
  46.0 1.0 broadcast_in_dim.23
  47.0 3.6 %all-to-all-start.2 = ((bf16[16,48,512]{2,1,0:T(8,128)(2,1)}), bf16[16,48,512]{2,1,0:T(8,128)(2,1)S(1)}, u32[]{:S(2)}, u32[]{:S(2)}) async-start(bf16[16,48,512]{2,1,0:T(8,128)(2,1)} %broadcast_in_dim.23), calls=%async_computation.2 | async-start | bytes 1572864 | tf_op jit(solution)/shard_map/all_to_all | solution.py:673
  50.7 0.6 copy-done.14
  51.3 12.9 %shard_map.288 = (bf16[2048,768]{1,0:T(8,128)(2,1)}, bf16[2048,512]{1,0:T(8,128)(2,1)}, bf16[2048,512]{1,0:T(8,128)(2,1)}, bf16[2048,512]{1,0:T(8,128)(2,1)}, f3...) custom-call(s32[8]{0:T(128)} %pad_add_fusion.refs_0_, ...), custom_call_target="tpu_custom_call" | custom-call | flops 16099999744 | bytes 14000000 | tf_op jit(solution)/shard_map/pallas_call | solution.py:234
  64.1 4.9 %collective-permute-start.3 = (f32[136,256]{1,0:T(8,128)}, f32[136,256]{1,0:T(8,128)S(1)}, u32[]{:S(2)}, u32[]{:S(2)}) collective-permute-start(f32[136,256]{1,0:T(8,128)} %get-tuple-element.88), channel_id=1, source_target_pairs={{0,24},{1,25},{2,26},{3,27},{4,28},{5,29},{6,30},{7,31},{32,56},{3... | collective-permute-start | bytes 417800 | tf_op jit(solution)/shard_map/ppermute | solution.py:668
  69.1 1.3 collective-permute-start.2
  70.4 2.8 %collective-permute-start.1 = (f32[136,256]{1,0:T(8,128)}, f32[136,256]{1,0:T(8,128)S(1)}, u32[]{:S(2)}, u32[]{:S(2)}) collective-permute-start(f32[136,256]{1,0:T(8,128)} %get-tuple-element.88), channel_id=1, source_target_pairs={{0,8},{8,16},{16,24},{1,9},{9,17},{17,25},{2,10},{10,18},{18,26},{... | collective-permute-start | bytes 417800 | tf_op jit(solution)/shard_map/ppermute | solution.py:668
  73.2 0.9 copy-done.1
  74.1 8.2 %shard_map.289 = (bf16[2048,256]{1,0:T(8,128)(2,1)}, bf16[2048,256]{1,0:T(8,128)(2,1)}, bf16[2048,256]{1,0:T(8,128)(2,1)}) custom-call(s32[8]{0:T(128)} %pad_add_fusion.refs_0_, bf16[2048,768]{1,0:T(8,128)(2,1)} %get-tuple-element.76.refs_1_, bf16[2048,768]{1,0:T(8,128)(2,1)} %refs_8_.3, bf16[768,512]{1,0:T(8,128)(2,1)} %bitcast.32, ...), custom_call_target="tpu_custom_call" | custom-call | flops 13799999488 | bytes 12000000 | tf_op jit(solution)/shard_map/pallas_call | solution.py:234
  82.3 0.6 copy-done.11
  83.0 7.6 %shard_map.290 = (bf16[2048,256]{1,0:T(8,128)(2,1)}, bf16[2048,256]{1,0:T(8,128)(2,1)}, bf16[2048,768]{1,0:T(8,128)(2,1)}, f32[2,2048]{1,0:T(2,128)}, f32[128,256]{1,0:T(8,128)}) custom-call(s32[8]{0:T(128)} %pad_add_fusion.refs_0_, bf16[2048,256]{1,0:T(8,128)(2,1)} %get-tuple-element.84.refs_1_, bf16[2048,256]{1,0:T(8,128)(2,1)} %get-tuple-element.85.refs_2_, ...), custom_call_target="tpu_custom_call" | custom-call | flops 11500000256 | bytes 10000000 | tf_op jit(solution)/shard_map/pallas_call | solution.py:234
  90.6 0.7 copy-done.7
  91.3 0.7 broadcast_in_dim.24
  92.0 3.4 %all-to-all-start.3 = ((f32[8,2,2048]{2,1,0:T(2,128)}), f32[8,2,2048]{2,1,0:T(2,128)S(1)}, u32[]{:S(2)}, u32[]{:S(2)}) async-start(f32[8,2,2048]{2,1,0:T(2,128)} %broadcast_in_dim.24), calls=%async_computation.3 | async-start | bytes 262144 | tf_op jit(solution)/shard_map/all_to_all | solution.py:673
  95.5 6.8 %all-to-all-done.3 = f32[8,2,2048]{2,1,0:T(2,128)S(1)} async-done(((f32[8,2,2048]{2,1,0:T(2,128)}), f32[8,2,2048]{2,1,0:T(2,128)S(1)}, u32[]{:S(2)}, u32[]{:S(2)}) %all-to-all-start.3) | async-done | bytes 131104 | tf_op jit(solution)/shard_map/all_to_all | solution.py:673
  102.9 7.3 %shard_map.291 = (bf16[2048,256]{1,0:T(8,128)(2,1)}, bf16[2048,256]{1,0:T(8,128)(2,1)}, f32[8,136,256]{2,1,0:T(8,128)}, f32[136,256]{1,0:T(8,128)}, f32[8,256]{1,0:T(8,128)}) custom-call(s32[8]{0:T(128)} %pad_add_fusion.refs_0_, bf16[2048,256]{1,0:T(8,128)(2,1)} %get-tuple-element.89.refs_1_, bf16[2048,256]{1,0:T(8,128)(2,1)} %get-tuple-element.85.refs_2_, ...), custom_call_target="tpu_custom_call" | custom-call | flops 10350000128 | bytes 9000000 | tf_op jit(solution)/shard_map/pallas_call | solution.py:234
  110.2 1.3 collective-permute-start.6
  111.5 1.3 collective-permute-start.5
  112.8 1.3 collective-permute-start.4
  114.1 12.7 %shard_map.292 = (bf16[2048,256]{1,0:T(8,128)(2,1)}, bf16[2048,256]{1,0:T(8,128)(2,1)}, f32[16,2048]{1,0:T(8,128)}, f32[768,256]{1,0:T(8,128)}) custom-call(s32[8]{0:T(128)} %pad_add_fusion.refs_0_, bf16[2048,256]{1,0:T(8,128)(2,1)} %get-tuple-element.92.refs_1_, bf16[2048,512]{1,0:T(8,128)(2,1)} %get-tuple-element.81.refs_4_.refs_2_.refs_6_, ...), custom_call_target="tpu_custom_call" | custom-call | flops 14949999616 | bytes 13000000 | tf_op jit(solution)/shard_map/pallas_call | solution.py:234
  126.9 2.1 add_convert_fusion
  129.7 19.9 %shard_map.293 = (bf16[2048,768]{1,0:T(8,128)(2,1)}, bf16[768,512]{1,0:T(8,128)(2,1)}, bf16[768,384]{1,0:T(8,128)(2,1)}, bf16[16,512]{1,0:T(8,128)(2,1)}, f32[8,768]{1,0:T(8,128)}) custom-call(s32[8]{0:T(128)} %pad_add_fusion.refs_0_, bf16[2048,768]{1,0:T(8,128)(2,1)} %get-tuple-element.76.refs_1_, bf16[16,768]{1,0:T(8,128)(2,1)} %copy-done.14, ...), custom_call_target="tpu_custom_call" | custom-call | flops 25300000768 | bytes 22000000 | tf_op jit(solution)/shard_map/pallas_call | solution.py:234
  149.6 1.4 collective-permute-start.7
  151.0 5.3 %collective-permute-done.7 = f32[8,768]{1,0:T(8,128)S(1)} collective-permute-done((f32[8,768]{1,0:T(8,128)}, f32[8,768]{1,0:T(8,128)S(1)}, u32[]{:S(2)}, u32[]{:S(2)}) %collective-permute-start.7) | collective-permute-done | bytes 24608 | tf_op jit(solution)/shard_map/ppermute | solution.py:668
  156.3 1.3 fusion.3
  157.6 1.0 all-gather.3.cloned.1.call-done.source
  158.7 1.1 pad_maximum_fusion
  159.7 7.0 %all-to-all-start.4 = ((bf16[16,64,512]{2,1,0:T(8,128)(2,1)}), bf16[16,64,512]{2,1,0:T(8,128)(2,1)S(1)}, u32[]{:S(2)}, u32[]{:S(2)}) async-start(bf16[16,64,512]{2,1,0:T(8,128)(2,1)} %pad_maximum_fusion), calls=%async_computation.6 | async-start | bytes 2097152 | tf_op jit(solution)/shard_map/all_to_all | solution.py:845
  166.8 2.1 constant_dynamic-slice_fusion
  168.9 4.3 %shard_map.294 = bf16[2048,768]{1,0:T(8,128)(2,1)} custom-call(bf16[2048,768]{1,0:T(8,128)(2,1)} %all-gather.3.cloned.1.call-done.source), custom_call_target="tpu_custom_call" | custom-call | flops 3000000000 | bytes 6000000 | tf_op jit(solution)/shard_map/pallas_call | solution.py:627
  173.2 11.7 %all-to-all-done.4 = bf16[16,64,512]{2,1,0:T(8,128)(2,1)S(1)} async-done(((bf16[16,64,512]{2,1,0:T(8,128)(2,1)}), bf16[16,64,512]{2,1,0:T(8,128)(2,1)S(1)}, u32[]{:S(2)}, u32[]{:S(2)}) %all-to-all-start.4) | async-done | bytes 1048608 | tf_op jit(solution)/shard_map/all_to_all | solution.py:845
  184.9 12.1 %reduce-scatter.5.cloned.1.call-done.dn = bf16[256,768]{1,0:T(8,128)(2,1)} async-done(((bf16[2048,768]{1,0:T(8,128)(2,1)}), bf16[256,768]{1,0:T(8,128)(2,1)}) %reduce-scatter.5.cloned.1.call-update) | async-done | bytes 393232 | tf_op jit(solution)/shard_map/reduce_scatter | solution.py:835
  197.0 2.3 shard_map.295
  200.1 0.7 copy.83
  200.8 3.4 %all-to-all-start.5 = ((f32[8,20,128]{2,1,0:T(8,128)}), f32[8,20,128]{2,1,0:T(8,128)S(1)}, u32[]{:S(2)}, u32[]{:S(2)}) async-start(f32[8,20,128]{2,1,0:T(8,128)} %copy.83), calls=%async_computation.7 | async-start | bytes 196608 | tf_op jit(solution)/shard_map/all_to_all | solution.py:876
  204.1 0.6 slice.141
  204.8 0.6 slice.138
  205.4 4.4 %all-to-all-done.5 = f32[8,20,128]{2,1,0:T(8,128)S(1)} async-done(((f32[8,20,128]{2,1,0:T(8,128)}), f32[8,20,128]{2,1,0:T(8,128)S(1)}, u32[]{:S(2)}, u32[]{:S(2)}) %all-to-all-start.5) | async-done | bytes 81952 | tf_op jit(solution)/shard_map/all_to_all | solution.py:876
  209.8 7.0 %all-to-all-start.6 = ((bf16[16,48,384]{2,1,0:T(8,128)(2,1)}), bf16[16,48,384]{2,1,0:T(8,128)(2,1)S(1)}, u32[]{:S(2)}, u32[]{:S(2)}) async-start(bf16[16,48,384]{2,1,0:T(8,128)(2,1)} %bitcast.18), calls=%async_computation.8 | async-start | bytes 1179648 | tf_op jit(solution)/shard_map/all_to_all | solution.py:856
  217.5 0.6 reduce_sum.59
  218.3 0.7 copy.85
  218.9 0.6 fusion.8
  220.0 0.7 slice.136
  220.7 0.7 slice.122
  221.5 0.7 copy.84
  222.1 6.5 %all-to-all-done.6 = bf16[16,48,384]{2,1,0:T(8,128)(2,1)S(1)} async-done(((bf16[16,48,384]{2,1,0:T(8,128)(2,1)}), bf16[16,48,384]{2,1,0:T(8,128)(2,1)S(1)}, u32[]{:S(2)}, u32[]{:S(2)}) %all-to-all-start.6) | async-done | bytes 589856 | tf_op jit(solution)/shard_map/all_to_all | solution.py:856
  228.7 0.7 slice_bitcast_fusion
  229.4 3.8 %copy.91 = bf16[2048,768]{1,0:T(8,128)(2,1)} copy(bf16[2048,768]{1,0:T(8,128)(2,1)} %all-gather.5.cloned.1.call-done) | data formatting | bytes 6291456
  (86 shorter events, 5.2 us)
Async XLA Ops:
  7.2 28.6 %copy-start.4 = (bf16[192,48]{0,1:T(8,128)(2,1)S(1)}, bf16[192,48]{0,1:T(8,128)(2,1)}, u32[]{:S(2)}) copy-start(bf16[192,48]{0,1:T(8,128)(2,1)} %param.33) | copy-start | bytes 55300
  7.2 28.6 %copy-start.5 = (bf16[48,192]{1,0:T(8,128)(2,1)S(1)}, bf16[48,192]{1,0:T(8,128)(2,1)}, u32[]{:S(2)}) copy-start(bf16[48,192]{1,0:T(8,128)(2,1)} %param.21) | copy-start | bytes 55300
  7.2 28.4 %copy-start.15 = (s32[1,4]{1,0:T(1,128)S(1)}, s32[1,4]{1,0:T(1,128)}, u32[]{:S(2)}) copy-start(s32[1,4]{1,0:T(1,128)} %param.19) | copy-start | bytes 52
  10.4 10.1 %all-to-all-start = ((f32[8,1,1792]{2,1,0:T(1,128)}), f32[8,1,1792]{2,1,0:T(1,128)S(1)}, u32[]{:S(2)}, u32[]{:S(2)}) async-start(f32[8,1,1792]{2,1,0:T(1,128)} %reshape.146), calls=%async_computation | async-start | bytes 114688 | tf_op jit(solution)/shard_map/all_to_all | solution.py:673
  23.8 22.1 %all-to-all-start.1 = ((bf16[16,48,512]{2,1,0:T(8,128)(2,1)}), bf16[16,48,512]{2,1,0:T(8,128)(2,1)S(1)}, u32[]{:S(2)}, u32[]{:S(2)}) async-start(bf16[16,48,512]{2,1,0:T(8,128)(2,1)} %broadcast_in_dim.22), calls=%async_computation.1 | async-start | bytes 1572864 | tf_op jit(solution)/shard_map/all_to_all | solution.py:673
  31.7 18.9 %collective-permute-start = (bf16[16,768]{1,0:T(8,128)(2,1)S(1)}, bf16[16,768]{1,0:T(8,128)(2,1)S(1)}, u32[]{:S(2)}, u32[]{:S(2)}) collective-permute-start(bf16[16,768]{1,0:T(8,128)(2,1)S(1)} %slice.106), channel_id=1, source_target_pairs={{0,8},{8,16},{16,24},{1,9},{9,17},{17,25},{2,10},{10,18},{18,26},{... | collective-permute-start | bytes 73736 | tf_op jit(solution)/shard_map/ppermute | solution.py:668
  45.9 4.7 %copy-start = (bf16[16,48,512]{2,1,0:T(8,128)(2,1)}, bf16[16,48,512]{2,1,0:T(8,128)(2,1)S(1)}, u32[]{:S(2)}) copy-start(bf16[16,48,512]{2,1,0:T(8,128)(2,1)S(1)} %all-to-all-done.1) | copy-start | bytes 2359300
  47.0 26.2 %all-to-all-start.2 = ((bf16[16,48,512]{2,1,0:T(8,128)(2,1)}), bf16[16,48,512]{2,1,0:T(8,128)(2,1)S(1)}, u32[]{:S(2)}, u32[]{:S(2)}) async-start(bf16[16,48,512]{2,1,0:T(8,128)(2,1)} %broadcast_in_dim.23), calls=%async_computation.2 | async-start | bytes 1572864 | tf_op jit(solution)/shard_map/all_to_all | solution.py:673
  50.6 76.3 %reduce-scatter.3.cloned.1.call-start = ((), (), s32[]{:S(2)}) async-start(), calls=%async_computation.9 | async-start | bytes 3538944 | tf_op jit(solution)/shard_map/reduce_scatter | solution.py:775
  50.6 0.6 copy-start.14
  64.1 18.1 %collective-permute-start.3 = (f32[136,256]{1,0:T(8,128)}, f32[136,256]{1,0:T(8,128)S(1)}, u32[]{:S(2)}, u32[]{:S(2)}) collective-permute-start(f32[136,256]{1,0:T(8,128)} %get-tuple-element.88), channel_id=1, source_target_pairs={{0,24},{1,25},{2,26},{3,27},{4,28},{5,29},{6,30},{7,31},{32,56},{3... | collective-permute-start | bytes 417800 | tf_op jit(solution)/shard_map/ppermute | solution.py:668
  69.1 13.2 %collective-permute-start.2 = (f32[136,256]{1,0:T(8,128)}, f32[136,256]{1,0:T(8,128)S(1)}, u32[]{:S(2)}, u32[]{:S(2)}) collective-permute-start(f32[136,256]{1,0:T(8,128)} %get-tuple-element.88), channel_id=1, source_target_pairs={{0,16},{8,24},{1,17},{9,25},{2,18},{10,26},{3,19},{11,27},{4,20},{... | collective-permute-start | bytes 417800 | tf_op jit(solution)/shard_map/ppermute | solution.py:668
  70.4 11.9 %collective-permute-start.1 = (f32[136,256]{1,0:T(8,128)}, f32[136,256]{1,0:T(8,128)S(1)}, u32[]{:S(2)}, u32[]{:S(2)}) collective-permute-start(f32[136,256]{1,0:T(8,128)} %get-tuple-element.88), channel_id=1, source_target_pairs={{0,8},{8,16},{16,24},{1,9},{9,17},{17,25},{2,10},{10,18},{18,26},{... | collective-permute-start | bytes 417800 | tf_op jit(solution)/shard_map/ppermute | solution.py:668
  73.2 0.9 copy-start.1
  82.2 0.7 copy-start.11
  82.2 0.7 copy-start.12
  82.3 0.7 copy-start.13
  90.6 0.7 copy-start.7
  92.0 10.2 %all-to-all-start.3 = ((f32[8,2,2048]{2,1,0:T(2,128)}), f32[8,2,2048]{2,1,0:T(2,128)S(1)}, u32[]{:S(2)}, u32[]{:S(2)}) async-start(f32[8,2,2048]{2,1,0:T(2,128)} %broadcast_in_dim.24), calls=%async_computation.3 | async-start | bytes 262144 | tf_op jit(solution)/shard_map/all_to_all | solution.py:673
  95.4 63.2 %all-gather.3.cloned.1.call-start = ((), (), s32[]{:S(2)}) async-start(), calls=%async_computation.10 | async-start | bytes 3538944 | tf_op jit(solution)/shard_map/all_gather | solution.py:805
  102.3 0.6 copy-start.3
  110.2 18.7 %collective-permute-start.6 = (f32[136,256]{1,0:T(8,128)}, f32[136,256]{1,0:T(8,128)S(1)}, u32[]{:S(2)}, u32[]{:S(2)}) collective-permute-start(f32[136,256]{1,0:T(8,128)} %get-tuple-element.97), channel_id=1, source_target_pairs={{24,0},{25,1},{26,2},{27,3},{28,4},{29,5},{30,6},{31,7},{56,32},{5... | collective-permute-start | bytes 417800 | tf_op jit(solution)/shard_map/ppermute | solution.py:668
  111.5 17.4 %collective-permute-start.5 = (f32[136,256]{1,0:T(8,128)}, f32[136,256]{1,0:T(8,128)S(1)}, u32[]{:S(2)}, u32[]{:S(2)}) collective-permute-start(f32[136,256]{1,0:T(8,128)} %get-tuple-element.97), channel_id=1, source_target_pairs={{16,0},{24,8},{17,1},{25,9},{18,2},{26,10},{19,3},{27,11},{20,4},{... | collective-permute-start | bytes 417800 | tf_op jit(solution)/shard_map/ppermute | solution.py:668
  112.8 16.1 %collective-permute-start.4 = (f32[136,256]{1,0:T(8,128)}, f32[136,256]{1,0:T(8,128)S(1)}, u32[]{:S(2)}, u32[]{:S(2)}) collective-permute-start(f32[136,256]{1,0:T(8,128)} %get-tuple-element.97), channel_id=1, source_target_pairs={{8,0},{16,8},{24,16},{9,1},{17,9},{25,17},{10,2},{18,10},{26,18},{... | collective-permute-start | bytes 417800 | tf_op jit(solution)/shard_map/ppermute | solution.py:668
  128.9 0.6 copy-start.8
  128.9 0.7 copy-start.9
  128.9 0.7 copy-start.10
  129.0 68.1 %reduce-scatter.5.cloned.1.call-start = ((), (), s32[]{:S(2)}) async-start(), calls=%async_computation.11 | async-start | bytes 3538944 | tf_op jit(solution)/shard_map/reduce_scatter | solution.py:835
  149.6 9.1 %copy-start.6 = (bf16[16,512]{1,0:T(8,128)(2,1)S(1)}, bf16[16,512]{1,0:T(8,128)(2,1)}, u32[]{:S(2)}) copy-start(bf16[16,512]{1,0:T(8,128)(2,1)} %get-tuple-element.118) | copy-start | bytes 49156
  149.6 9.1 %copy-start.2 = (bf16[768,512]{1,0:T(8,128)(2,1)S(1)}, bf16[768,512]{1,0:T(8,128)(2,1)}, u32[]{:S(2)}) copy-start(bf16[768,512]{1,0:T(8,128)(2,1)} %get-tuple-element.117) | copy-start | bytes 2359300
  149.6 6.7 %collective-permute-start.7 = (f32[8,768]{1,0:T(8,128)}, f32[8,768]{1,0:T(8,128)S(1)}, u32[]{:S(2)}, u32[]{:S(2)}) collective-permute-start(f32[8,768]{1,0:T(8,128)} %get-tuple-element.114), channel_id=1, source_target_pairs={{8,0},{16,8},{24,16},{9,1},{17,9},{25,17},{10,2},{18,10},{26,18},{... | collective-permute-start | bytes 73736 | tf_op jit(solution)/shard_map/ppermute | solution.py:668
  159.7 25.2 %all-to-all-start.4 = ((bf16[16,64,512]{2,1,0:T(8,128)(2,1)}), bf16[16,64,512]{2,1,0:T(8,128)(2,1)S(1)}, u32[]{:S(2)}, u32[]{:S(2)}) async-start(bf16[16,64,512]{2,1,0:T(8,128)(2,1)} %pad_maximum_fusion), calls=%async_computation.6 | async-start | bytes 2097152 | tf_op jit(solution)/shard_map/all_to_all | solution.py:845
  166.8 62.6 %all-gather.5.cloned.1.call-start = ((), (), s32[]{:S(2)}) async-start(), calls=%async_computation.12 | async-start | bytes 3538944 | tf_op jit(solution)/shard_map/all_gather | solution.py:855
  200.8 9.1 %all-to-all-start.5 = ((f32[8,20,128]{2,1,0:T(8,128)}), f32[8,20,128]{2,1,0:T(8,128)S(1)}, u32[]{:S(2)}, u32[]{:S(2)}) async-start(f32[8,20,128]{2,1,0:T(8,128)} %copy.83), calls=%async_computation.7 | async-start | bytes 196608 | tf_op jit(solution)/shard_map/all_to_all | solution.py:876
  209.8 18.8 %all-to-all-start.6 = ((bf16[16,48,384]{2,1,0:T(8,128)(2,1)}), bf16[16,48,384]{2,1,0:T(8,128)(2,1)S(1)}, u32[]{:S(2)}, u32[]{:S(2)}) async-start(bf16[16,48,384]{2,1,0:T(8,128)(2,1)} %bitcast.18), calls=%async_computation.8 | async-start | bytes 1179648 | tf_op jit(solution)/shard_map/all_to_all | solution.py:856
Sparse Core Ops, SparseCore 0:
  90.8 34.2 reduce-scatter.2
  129.1 29.4 all-gather.2
  161.0 35.9 reduce-scatter.4
  199.5 26.6 all-gather.4
